TPU v7x, 32 devices: a whole 2x2x4 slice. The times are simulated.
32 devices in a mesh: row: 8 (over y, x, core), col: 4 (over z).
Axes of the slice: x: 2, y: 2, z: 4, core: 2. Of those that a mesh axis runs over, the one named last changes fastest.
Arguments:
- blocks: bfloat16 [8, 4, 64, 128, 128], P('row', 'col'), may hold values from -0.046875 to 0.046875
- block_rows: int32 [8, 4, 64], P('row', 'col'), may hold values from 0 to 7, as said below
- block_cols: int32 [8, 4, 64], P('row', 'col'), may hold values from 0 to 15, as said below
- block_count: int32 [8, 4], P('row', 'col'), may hold values from 16 to 64, as said below
- probes: float32 [64, 8192], P(None, ('row', 'col')), may hold values from -6 to 6
- t_prev: float32 [64, 8192], P(None, ('row', 'col')), may hold values from -6 to 6
- t_cur: float32 [64, 8192], P(None, ('row', 'col')), may hold values from -6 to 6
- accum: float32 [64, 8192], P(None, ('row', 'col')), may hold values from -6 to 6
- coeffs: float32 [2], replicated, may hold values from 0.5 to 1.5
Outputs:
- t_next: float32 [64, 8192], P(None, ('row', 'col'))
- t_after: float32 [64, 8192], P(None, ('row', 'col'))
- accum_out: float32 [64, 8192], P(None, ('row', 'col'))
- moments: float32 [2, 64], replicated
Inputs may be any that keep to these rules, and one draw needn't show every extreme that they name: `block_rows`: within one device the live slots name distinct blocks; block rows lie in [0, 8) and block columns in [0, 16). `block_cols`: pairs with block_rows: within one device the live slots name distinct blocks. `block_count`: some device has all 64 slots live in every draw.
All inputs are finite; a program needn't handle non-finite values.
Results may differ from a plain program's by a relative error of at most 0.0025.
Values may be sent and summed in bfloat16 or wider, within the bound.
No kernel may reach another device: no remote copies, remote signals or barrier semaphores. Data moves between devices by JAX's collectives and lax.ppermute only.
A program may use at most 64 MiB of HBM per device.

v0:
```python
import jax
import jax.numpy as jnp
from jax import lax
from jax.sharding import PartitionSpec as P


def local(blocks, block_rows, block_cols, block_count, probes, t_prev, t_cur, accum, coeffs):
    tiles_all = blocks[0, 0]
    row_ids = block_rows[0, 0]
    col_ids = block_cols[0, 0]
    live_total = block_count[0, 0]
    slot_total = tiles_all.shape[0]
    tile_size = tiles_all.shape[-1]
    probe_count = t_cur.shape[0]
    width = t_cur.shape[1]
    local_rows = width // tile_size * lax.axis_size("col")
    group_size = min(32, slot_total)
    turns = (live_total + group_size - 1) // group_size
    total_rows = width * lax.axis_size("row") * lax.axis_size("col")

    def product(vectors):
        gathered = lax.all_gather(vectors.astype(jnp.bfloat16), "row", axis=1, tiled=True)
        column_set = gathered.reshape(probe_count, -1, tile_size)

        def add_group(step_idx, total):
            first_slot = jnp.minimum(step_idx * group_size, slot_total - group_size)
            tile_group = lax.dynamic_slice_in_dim(tiles_all, first_slot, group_size, 0)
            group_rows = lax.dynamic_slice_in_dim(row_ids, first_slot, group_size, 0)
            group_cols = lax.dynamic_slice_in_dim(col_ids, first_slot, group_size, 0)
            slot_ids = first_slot + jnp.arange(group_size, dtype=jnp.int32)
            alive = (slot_ids >= step_idx * group_size) & (slot_ids < live_total)
            picked = jnp.take(column_set, group_cols, axis=1)
            contrib = jnp.einsum(
                "pgj,gij->pgi", picked, tile_group, preferred_element_type=jnp.float32
            )
            contrib = jnp.where(alive[None, :, None], contrib, 0.0)
            return total.at[:, group_rows, :].add(contrib)

        start = jnp.zeros((probe_count, local_rows, tile_size), jnp.float32)
        partial_value = lax.fori_loop(0, turns, add_group, start).reshape(
            probe_count, local_rows * tile_size
        )
        summed = lax.psum(partial_value, "col")
        return lax.dynamic_slice_in_dim(summed, lax.axis_index("col") * width, width, 1)

    def moment_one(local_sum):
        return lax.psum(local_sum, ("row", "col"))

    scale = float(total_rows) ** (-0.5)
    t_next = 2.0 * product(t_cur) - t_prev
    local_first = jnp.sum(probes * t_next, axis=1)
    first = moment_one(local_first)
    t_after = 2.0 * product(t_next) - t_cur
    second = moment_one(jnp.sum(probes * t_after, axis=1))
    moments = jnp.stack([first, second]) * scale
    accum_out = accum + coeffs[0] * t_next + coeffs[1] * t_after
    return (t_next, t_after, accum_out, moments)


def solution(mesh):
    return jax.shard_map(
        local,
        mesh=mesh,
        in_specs=(
            P("row", "col", None, None, None),
            P("row", "col", None),
            P("row", "col", None),
            P("row", "col"),
            P(None, ("row", "col")),
            P(None, ("row", "col")),
            P(None, ("row", "col")),
            P(None, ("row", "col")),
            P(),
        ),
        out_specs=(P(None, ("row", "col")), P(None, ("row", "col")), P(None, ("row", "col")), P()),
        check_vma=False,
    )
```

profile of v0, /device:TPU:0, one launch (start us, length us, event | category | flops | bytes accessed | tf_op | source)
XLA Modules:
  0.0 181.8 jit_solution(8852229048387807847)
XLA Ops:
  7.2 0.0 all-reduce.4.cloned.1.call-start
  7.9 0.8 convert_element_type.6
  8.7 11.3 %all_gather.6 = bf16[64,2048]{1,0:T(8,128)(2,1)S(1)} all-gather(bf16[64,256]{1,0:T(8,128)(2,1)S(1)} %convert_element_type.6), channel_id=1, replica_groups=mesh['row'=8,'col'=4] {'row'}, dimensions={1}, use_global_device_ids=true | all-gather | bytes 294912 | tf_op jit(solution)/shard_map/all_gather | solution.py:22
  20.0 0.1 copy_bitcast_fusion.3
  20.1 0.0 copy-start.4
  20.1 12.8 %while.20 = (s32[]{:T(128)}, f32[64,8,128]{2,0,1:T(8,128)S(1)}, s32[]{:T(128)}, s32[64]{0:T(128)}, s32[]{:T(128)}, /*index=5*/bf16[64,128,128]{2,1,0:T(8,128)(2,...) while((s32[]{:T(128)}, f32[64,8,128]{2,0,1:T(8,128)S(1)}, ...), condition=%wide.region_2.4_spmd, body=%wide.region_0.3_spmd.sunk | while | flops 67896744 | bytes 6822115 | solution.py:40
  20.1 0.0 copy-start.7
  20.2 1.4 compare_and_fusion.6
  21.6 0.6 gather_fusion
  22.2 2.1 %fusion.30 = f32[32,64,128]{2,1,0:T(8,128)S(1)} fusion(bf16[64,128,128]{2,1,0:T(8,128)(2,1)} %get-tuple-element.305, s32[]{:T(128)S(6)} %select_n.86, bf16[32,64,128]{2,1,0:T(8,128)(2,1)S(1)} %gather_fusion, pred[32]{0:T(512)(128)(4,1)S(1)} %get-tuple-element.263, pred[32]{0:T(512)(128)(4,1)S(1)} %get-tuple-element.264), kind=kOutput, calls=%fused_computation.5.clone.1 | convolution fusion | flops 67633152 | bytes 2621508 | tf_op jit(solution)/shard_map/while/body/pgj,gij->pgi/dot_general | solution.py:33
  24.3 0.0 copy-done.7
  24.3 0.1 compare_select_fusion.8
  24.4 2.1 %scatter_fusion = f32[64,8,128]{2,0,1:T(8,128)S(1)} fusion(f32[64,8,128]{2,0,1:T(8,128)S(1)} %get-tuple-element.289, s32[32]{0:T(128)S(1)} %compare_select_fusion.8, f32[32,64,128]{2,1,0:T(8,128)S(1)} %fusion.30), kind=kCustom, calls=%fused_computation.2.clone.1 | custom fusion | flops 262144 | bytes 3145856 | tf_op jit(solution)/shard_map/while/body/scatter-add | solution.py:37
  26.5 0.0 copy-start.7
  26.6 1.4 compare_and_fusion.6
  28.0 0.6 gather_fusion
  28.6 2.1 %fusion.30 = f32[32,64,128]{2,1,0:T(8,128)S(1)} fusion(bf16[64,128,128]{2,1,0:T(8,128)(2,1)} %get-tuple-element.305, s32[]{:T(128)S(6)} %select_n.86, bf16[32,64,128]{2,1,0:T(8,128)(2,1)S(1)} %gather_fusion, pred[32]{0:T(512)(128)(4,1)S(1)} %get-tuple-element.263, pred[32]{0:T(512)(128)(4,1)S(1)} %get-tuple-element.264), kind=kOutput, calls=%fused_computation.5.clone.1 | convolution fusion | flops 67633152 | bytes 2621508 | tf_op jit(solution)/shard_map/while/body/pgj,gij->pgi/dot_general | solution.py:33
  30.7 0.0 copy-done.7
  30.7 0.1 compare_select_fusion.8
  30.8 2.1 %scatter_fusion = f32[64,8,128]{2,0,1:T(8,128)S(1)} fusion(f32[64,8,128]{2,0,1:T(8,128)S(1)} %get-tuple-element.289, s32[32]{0:T(128)S(1)} %compare_select_fusion.8, f32[32,64,128]{2,1,0:T(8,128)S(1)} %fusion.30), kind=kCustom, calls=%fused_computation.2.clone.1 | custom fusion | flops 262144 | bytes 3145856 | tf_op jit(solution)/shard_map/while/body/scatter-add | solution.py:37
  32.9 0.0 copy-start
  33.0 0.0 copy-start.5
  33.0 0.7 copy_bitcast_fusion.1
  33.7 0.0 all-reduce.4.cloned.1.call-update
  33.7 0.0 all-reduce.6.cloned.1.call-start
  33.8 35.8 %all-reduce.4.cloned.1.call-done = f32[64,1024]{1,0:T(8,128)} async-done(((f32[64,1024]{1,0:T(8,128)}), f32[64,1024]{1,0:T(8,128)}) %all-reduce.4.cloned.1.call-update) | async-done | bytes 262160 | tf_op jit(solution)/shard_map/psum | solution.py:43
  69.5 0.0 copy-done.4
  69.5 0.9 fusion.16
  70.4 0.0 copy-start.1
  70.4 9.8 %all_gather.7 = bf16[64,2048]{1,0:T(8,128)(2,1)S(1)} all-gather(bf16[64,256]{1,0:T(8,128)(2,1)S(1)} %get-tuple-element.158), channel_id=1, replica_groups=mesh['row'=8,'col'=4] {'row'}, dimensions={1}, use_global_device_ids=true | all-gather | bytes 294912 | tf_op jit(solution)/shard_map/all_gather | solution.py:22
  80.2 0.8 copy_bitcast_fusion.2
  81.0 0.0 copy-done
  81.0 0.0 copy-done.5
  81.0 0.0 copy-start.6
  81.0 0.0 copy-start.2
  81.0 14.5 %while.21 = (s32[]{:T(128)}, f32[64,8,128]{2,0,1:T(8,128)S(1)}, s32[]{:T(128)}, s32[64]{0:T(128)}, s32[]{:T(128)}, /*index=5*/bf16[64,128,128]{2,1,0:T(8,128)(2,...) while((s32[]{:T(128)}, f32[64,8,128]{2,0,1:T(8,128)S(1)}, ...), condition=%wide.region_6.8_spmd, body=%wide.region_4.7_spmd.sunk | while | flops 67896744 | bytes 6823075 | solution.py:40
  81.1 0.7 compare_and_fusion.7
  81.8 2.4 %gather_fusion.1 = bf16[32,64,128]{2,1,0:T(8,128)(2,1)} fusion(bf16[64,16,128]{2,0,1:T(8,128)(2,1)} %get-tuple-element.343, s32[1024]{0:T(1024)S(1)} %pad_clamp_fusion.5), kind=kCustom, calls=%fused_computation.1.clone.clone.1 | custom fusion | bytes 1048704 | tf_op jit(solution)/shard_map/while/body/jit(_take)/gather | solution.py:32
  84.2 0.0 copy-start.8
  84.2 1.9 %fusion.33 = f32[32,64,128]{2,1,0:T(8,128)S(1)} fusion(bf16[64,128,128]{2,1,0:T(8,128)(2,1)S(1)} %get-tuple-element.341, s32[]{:T(128)S(6)} %select_n.90, bf16[32,64,128]{2,1,0:T(8,128)(2,1)} %gather_fusion.1, pred[32]{0:T(512)(128)(4,1)S(1)} %get-tuple-element.274, pred[32]{0:T(512)(128)(4,1)S(1)} %get-tuple-element.275), kind=kOutput, calls=%fused_computation.19.clone.1 | convolution fusion | flops 67633152 | bytes 2622468 | tf_op jit(solution)/shard_map/while/body/pgj,gij->pgi/dot_general | solution.py:33
  86.0 0.0 copy-done.8
  86.1 0.1 compare_select_fusion.9
  86.1 2.1 %scatter_fusion.1 = f32[64,8,128]{2,0,1:T(8,128)S(1)} fusion(f32[64,8,128]{2,0,1:T(8,128)S(1)} %get-tuple-element.325, s32[32]{0:T(128)S(1)} %compare_select_fusion.9, f32[32,64,128]{2,1,0:T(8,128)S(1)} %fusion.33), kind=kCustom, calls=%fused_computation.3.clone.1 | custom fusion | flops 262144 | bytes 3145856 | tf_op jit(solution)/shard_map/while/body/scatter-add | solution.py:37
  88.3 0.7 compare_and_fusion.7
  89.0 2.4 %gather_fusion.1 = bf16[32,64,128]{2,1,0:T(8,128)(2,1)} fusion(bf16[64,16,128]{2,0,1:T(8,128)(2,1)} %get-tuple-element.343, s32[1024]{0:T(1024)S(1)} %pad_clamp_fusion.5), kind=kCustom, calls=%fused_computation.1.clone.clone.1 | custom fusion | bytes 1048704 | tf_op jit(solution)/shard_map/while/body/jit(_take)/gather | solution.py:32
  91.4 0.0 copy-start.8
  91.4 1.9 %fusion.33 = f32[32,64,128]{2,1,0:T(8,128)S(1)} fusion(bf16[64,128,128]{2,1,0:T(8,128)(2,1)S(1)} %get-tuple-element.341, s32[]{:T(128)S(6)} %select_n.90, bf16[32,64,128]{2,1,0:T(8,128)(2,1)} %gather_fusion.1, pred[32]{0:T(512)(128)(4,1)S(1)} %get-tuple-element.274, pred[32]{0:T(512)(128)(4,1)S(1)} %get-tuple-element.275), kind=kOutput, calls=%fused_computation.19.clone.1 | convolution fusion | flops 67633152 | bytes 2622468 | tf_op jit(solution)/shard_map/while/body/pgj,gij->pgi/dot_general | solution.py:33
  93.3 0.0 copy-done.8
  93.3 0.1 compare_select_fusion.9
  93.4 2.1 %scatter_fusion.1 = f32[64,8,128]{2,0,1:T(8,128)S(1)} fusion(f32[64,8,128]{2,0,1:T(8,128)S(1)} %get-tuple-element.325, s32[32]{0:T(128)S(1)} %compare_select_fusion.9, f32[32,64,128]{2,1,0:T(8,128)S(1)} %fusion.33), kind=kCustom, calls=%fused_computation.3.clone.1 | custom fusion | flops 262144 | bytes 3145856 | tf_op jit(solution)/shard_map/while/body/scatter-add | solution.py:37
  95.5 0.7 copy_bitcast_fusion
  96.3 0.0 all-reduce.6.cloned.1.call-update
  96.3 0.0 copy-done.6
  96.3 0.6 fusion.17
  96.9 33.7 %all-reduce.6.cloned.1.call-done = f32[64,1024]{1,0:T(8,128)} async-done(((f32[64,1024]{1,0:T(8,128)}), f32[64,1024]{1,0:T(8,128)}) %all-reduce.6.cloned.1.call-update) | async-done | bytes 262160 | tf_op jit(solution)/shard_map/psum | solution.py:43
  130.6 0.0 copy-done.2
  130.6 1.0 multiply_reduce_fusion.1
  131.6 0.0 copy-start.3
  131.6 40.2 %all-reduce = (f32[1,64]{1,0:T(1,128)S(1)}, f32[1,64]{1,0:T(1,128)S(1)}) all-reduce(f32[1,64]{1,0:T(1,128)S(1)} %bitcast.50, f32[1,64]{1,0:T(1,128)S(1)} %bitcast.49), channel_id=1, replica_groups=mesh['row'=8,'col'=4] {'row','col'}, use_global_device_ids=true, to_apply=%region_11.13 | all-reduce | flops 128 | bytes 1024 | tf_op jit(solution)/shard_map/psum | solution.py:47
  171.8 0.6 maximum_multiply_fusion
  172.3 0.0 copy-done.1
  172.3 2.6 %multiply_add_fusion = f32[64,256]{1,0:T(8,128)} fusion(f32[64,256]{1,0:T(8,128)S(1)} %get-tuple-element.157, f32[64,256]{1,0:T(8,128)} %param.22, f32[64,256]{1,0:T(8,128)S(1)} %get-tuple-element.159, f32[]{:T(128)} %bitcast.9, f32[]{:T(128)} %bitcast.8), kind=kLoop, calls=%fused_computation.38 | loop fusion | flops 65536 | bytes 262152 | tf_op jit(solution)/shard_map/add | solution.py:56
  175.0 0.0 copy-done.3
  (6 shorter events, 0.1 us)
Async XLA Ops:
  7.2 62.4 %all-reduce.4.cloned.1.call-start = ((), (), s32[]{:S(2)}) async-start(), calls=%async_computation | async-start | bytes 524288 | tf_op jit(solution)/shard_map/psum | solution.py:43
  20.1 49.4 %copy-start.4 = (f32[64,256]{1,0:T(8,128)S(1)}, f32[64,256]{1,0:T(8,128)}, u32[]{:S(2)}) copy-start(f32[64,256]{1,0:T(8,128)} %param.20) | copy-start | bytes 196612
  20.1 4.2 %copy-start.7 = (s32[64]{0:T(128)S(1)}, s32[64]{0:T(128)}, u32[]{:S(2)}) copy-start(s32[64]{0:T(128)} %get-tuple-element.303) | copy-start | bytes 772 | tf_op jit(solution)/shard_map/while
  26.5 4.2 %copy-start.7 = (s32[64]{0:T(128)S(1)}, s32[64]{0:T(128)}, u32[]{:S(2)}) copy-start(s32[64]{0:T(128)} %get-tuple-element.303) | copy-start | bytes 772 | tf_op jit(solution)/shard_map/while
  32.9 48.0 %copy-start = (bf16[64,128,128]{2,1,0:T(8,128)(2,1)S(1)}, bf16[64,128,128]{2,1,0:T(8,128)(2,1)}, u32[]{:S(2)}) copy-start(bf16[64,128,128]{2,1,0:T(8,128)(2,1)} %get-tuple-element.350) | copy-start | bytes 6291460
  33.0 48.0 %copy-start.5 = (s32[64]{0:T(128)S(1)}, s32[64]{0:T(128)}, u32[]{:S(2)}) copy-start(s32[64]{0:T(128)} %get-tuple-element.355) | copy-start | bytes 772
  33.7 96.9 %all-reduce.6.cloned.1.call-start = ((), (), s32[]{:S(2)}) async-start(), calls=%async_computation.1 | async-start | bytes 524288 | tf_op jit(solution)/shard_map/psum | solution.py:43
  70.4 102.0 %copy-start.1 = (f32[64,256]{1,0:T(8,128)}, f32[64,256]{1,0:T(8,128)S(1)}, u32[]{:S(2)}) copy-start(f32[64,256]{1,0:T(8,128)S(1)} %get-tuple-element.159) | copy-start | bytes 196612
  81.0 15.3 %copy-start.6 = (f32[2]{0:T(128)S(1)}, f32[2]{0:T(128)}, u32[]{:S(2)}) copy-start(f32[2]{0:T(128)} %param.23) | copy-start | bytes 28
  81.0 49.6 %copy-start.2 = (f32[64,256]{1,0:T(8,128)S(1)}, f32[64,256]{1,0:T(8,128)}, u32[]{:S(2)}) copy-start(f32[64,256]{1,0:T(8,128)} %param.21) | copy-start | bytes 196612
  84.2 1.9 %copy-start.8 = (s32[64]{0:T(128)S(1)}, s32[64]{0:T(128)}, u32[]{:S(2)}) copy-start(s32[64]{0:T(128)} %get-tuple-element.339) | copy-start | bytes 772 | tf_op jit(solution)/shard_map/while
  91.4 1.9 %copy-start.8 = (s32[64]{0:T(128)S(1)}, s32[64]{0:T(128)}, u32[]{:S(2)}) copy-start(s32[64]{0:T(128)} %get-tuple-element.339) | copy-start | bytes 772 | tf_op jit(solution)/shard_map/while
  131.6 43.4 %copy-start.3 = (f32[64,256]{1,0:T(8,128)}, f32[64,256]{1,0:T(8,128)S(1)}, u32[]{:S(2)}) copy-start(f32[64,256]{1,0:T(8,128)S(1)} %get-tuple-element.157) | copy-start | bytes 196612
Sparse Core Ops, SparseCore 0:
  33.8 35.6 all-reduce.3
  96.4 34.1 all-reduce.5
where the time goes:
time: 183 us; the launch traced here: 182 us
  waiting for transfers between devices  69.5 us (38%)
  blocking collectives  61.2 us (33%)
  other arithmetic  19 us (10%)
  between operations  14.8 us (8%)
  local copies, waits for them, and re-layouts  8.95 us (5%)
  matrix products  7.92 us (4%)
    psum x2, waiting for transfers between devices, product(): summed = lax.psum(partial_value, 'col')  69.5 us
    psum x1, blocking collectives, moment_one(): return lax.psum(local_sum, ('row', 'col'))  40.2 us
    all_gather x2, blocking collectives, product(): lax.all_gather(vectors.astype(jnp.bfloat16), 'row', axis=1, tiled=True)  21.1 us
    scatter-add x4, other arithmetic, add_group(): return total.at[:, group_rows, :].add(contrib)  8.56 us
    dot_general x4, matrix products, add_group(): jnp.einsum('pgj,gij->pgi', picked, tile_group, preferred_element_type=jnp...  7.92 us
    gather x4, local copies, waits for them, and re-layouts, add_group(): picked = jnp.take(column_set, group_cols, axis=1)  6.01 us
    and x4, other arithmetic, add_group(): picked = jnp.take(column_set, group_cols, axis=1)  4.22 us
  transfers between devices with their start and end apart: 2, of which 2 were waited for; matrix products, arithmetic and copies ran while one was open for 0% of the time, Pallas kernels for 0%

commit v1 on v0

v1 whole, which is shorter than its diff:
```python
import functools

import jax
import jax.numpy as jnp
from jax import lax
from jax.experimental import pallas as pl
from jax.experimental.pallas import tpu as pltpu
from jax.sharding import PartitionSpec as P

VMEM = pl.BlockSpec(memory_space=pltpu.VMEM)
SMEM = pl.BlockSpec(memory_space=pltpu.SMEM)
HBM = pl.BlockSpec(memory_space=pltpu.HBM)
CONTRACT_LAST = (((1,), (1,)), ((), ()))
F32, BF16 = jnp.float32, jnp.bfloat16
LANES = 128


def place_kernel(pb, group, count, rows_in, cols_in, blocks, dense, held, rows, cols, sems, own_sems):
    r, c = lax.axis_index("row"), lax.axis_index("col")
    bs = blocks.shape[-1]
    groups = held.shape[0] // group

    def fetch(g):
        span = pl.ds(g * group, group)
        return pltpu.make_async_copy(blocks.at[0, 0, span], held.at[span], sems.at[g])

    names = (
        pltpu.make_async_copy(rows_in, rows, own_sems.at[0]),
        pltpu.make_async_copy(cols_in, cols, own_sems.at[1]),
    )
    for copy in names:
        copy.start()
    for g in range(groups):
        fetch(g).start()
    dense[...] = jnp.zeros_like(dense)
    for copy in names:
        copy.wait()
    live = count[0, 0]

    def put(slot):
        @pl.when(slot < live)
        def _():
            i, j = rows[0, 0, slot], cols[0, 0, slot]
            line = ((i // pb) ^ c) * pb + i % pb
            dense[(j // pb) ^ r, j % pb, pl.ds(pl.multiple_of(line * bs, bs), bs), :] = held[slot]

    for g in range(groups):
        fetch(g).wait()
        for n in range(group):
            put(g * group + n)


def dots(pb, order, vectors, dense, m, width):
    total = None
    for h, k in enumerate(order):
        w = jnp.concatenate([dense[k, s, pl.ds(m * width, width), :] for s in range(pb)], axis=1)
        part = lax.dot_general(vectors[h], w, CONTRACT_LAST, preferred_element_type=F32)
        total = part if total is None else total + part
    return total


def first_half_kernel(pb, order, vectors, dense, out):
    width = vectors.shape[2]
    for m in range(out.shape[0]):
        out[m] = dots(pb, order, vectors, dense, m, width)


def as_row(column):
    n = column.shape[0]
    shape = (n, LANES)
    here = lax.broadcasted_iota(jnp.int32, shape, 0) == lax.broadcasted_iota(jnp.int32, shape, 1)
    return jnp.sum(jnp.where(here, column, 0.0), axis=0, keepdims=True)


def two_parts(x):
    high = x.astype(BF16).astype(F32)
    return high, x - high


def second_half_kernel(pb, order, n_probes, vectors, dense, half, *refs):
    width = vectors.shape[2]
    chunks = half.shape[0]
    tile = None
    if n_probes:
        before, probes, refs = refs[0], refs[1 : 1 + n_probes], refs[1 + n_probes :]
    own, sends = refs[0], refs[1 : chunks]
    sums = None
    for m in range(chunks):
        total = half[m] + dots(pb, order, vectors, dense, m, width)
        if n_probes:
            part = jnp.sum(probes[m][...] * total, axis=1, keepdims=True)
            sums = part if sums is None else sums + part
        if m == 0:
            own[...] = total
        else:
            sends[m - 1][pl.ds(0, total.shape[0]), :] = total.astype(BF16)[:, :LANES]
            for s in range(1, width // LANES):
                sends[m - 1][pl.ds(s * total.shape[0], total.shape[0]), :] = total.astype(BF16)[
                    :, s * LANES : (s + 1) * LANES
                ]
    if n_probes:
        tile_out = refs[chunks]
        both = before[...][:2] + jnp.concatenate([jnp.zeros((1, LANES), F32), 2.0 * as_row(sums)], axis=0)
        tile_out[...] = jnp.concatenate([both, jnp.zeros((6, LANES), F32)], axis=0)
        high, low = two_parts(both)
        tile = jnp.concatenate([high, low, jnp.zeros((12, LANES), F32)], axis=0).astype(BF16)
        for m in range(1, chunks):
            sends[m - 1][pl.ds(width // LANES * own.shape[0], 16), :] = tile


def gathered(own, received):
    count, width = own.shape
    total = own[...]
    for r in received:
        piece = jnp.concatenate(
            [r[pl.ds(s * count, count), :] for s in range(width // LANES)], axis=1
        )
        total = total + piece.astype(F32)
    return total


def next_kernel(n_col, own, *refs):
    received, (prev, cur, probes, rounded, tile) = refs[: n_col - 1], refs[n_col - 1 :]
    value = 2.0 * gathered(own, received) - prev[...]
    rounded[...] = value.astype(BF16)
    ahead = as_row(jnp.sum(probes[...] * value, axis=1, keepdims=True))
    back = as_row(jnp.sum(probes[...] * cur[...], axis=1, keepdims=True))
    tile[...] = jnp.concatenate([ahead, -back, jnp.zeros((6, LANES), F32)], axis=0)


def value_kernel(n_col, own, *refs):
    received, (prev, out) = refs[: n_col - 1], refs[n_col - 1 :]
    out[...] = 2.0 * gathered(own, received) - prev[...]


def tile_kernel(start, mine, *refs):
    received, tile = refs[:-1], refs[-1]
    total = mine[...]
    for r in received:
        t = r[pl.ds(start, 16), :].astype(F32)
        total = total + jnp.concatenate([t[0:2] + t[2:4], jnp.zeros((6, LANES), F32)], axis=0)
    tile[...] = total


def last_kernel(n_col, coeffs, own, *refs):
    received = refs[: n_col - 1]
    prev, t_next, accum, t_after, accum_out = refs[n_col - 1 :]
    value = 2.0 * gathered(own, received) - prev[...]
    t_after[...] = value
    accum_out[...] = accum[...] + coeffs[0] * t_next[...] + coeffs[1] * value


def local(n_row, n_col, blocks, block_rows, block_cols, block_count, probes, t_prev, t_cur, accum, coeffs):
    n_slots, bs = blocks.shape[2], blocks.shape[-1]
    count, width = t_cur.shape
    pb = width // bs
    total_rows = width * n_row * n_col
    dense_bytes = n_row * n_col * width * width * 2
    params = pltpu.CompilerParams(vmem_limit_bytes=min(60 * 1024 * 1024, 3 * dense_bytes))
    barrier = lax.optimization_barrier

    def swap(x, axis, k):
        n = n_row if axis == "row" else n_col
        return lax.ppermute(x, axis, [(i, i ^ k) for i in range(n)])

    def call(kernel, out_shape, in_specs, name, **more):
        one = not isinstance(out_shape, list)
        return pl.pallas_call(
            kernel,
            out_shape=out_shape,
            in_specs=in_specs,
            out_specs=VMEM if one else [VMEM] * len(out_shape),
            compiler_params=params,
            name=name,
            **more,
        )

    def in_hbm(x):
        return pltpu.with_memory_space_constraint(x, pltpu.HBM)

    def shape(*dims, dtype=F32):
        return jax.ShapeDtypeStruct(dims, dtype)

    group = 8
    dense = call(
        functools.partial(place_kernel, pb, group),
        shape(n_row, pb, n_col * width, bs, dtype=BF16),
        [SMEM] + [HBM] * 3,
        "place",
        scratch_shapes=[
            pltpu.VMEM((n_slots, bs, bs), BF16),
            pltpu.SMEM(block_rows.shape, jnp.int32),
            pltpu.SMEM(block_cols.shape, jnp.int32),
            pltpu.SemaphoreType.DMA((n_slots // group,)),
            pltpu.SemaphoreType.DMA((2,)),
        ],
    )(block_count, *(in_hbm(x) for x in (block_rows, block_cols, blocks)))

    far = list(range(n_row - 2, 0, -2))
    mine_order = [0] + [k ^ 1 for k in far]
    others_order = [1] + far

    def gather(v):
        got = [swap(v, "row", k ^ 1) for k in far]
        head, tail = jnp.stack([v] + got[:-1]), got[-1][None]
        return head, tail

    send_rows = width // LANES * count

    def halves(head, tail, dense, extra, name):
        other = [swap(head, "row", 1), swap(tail, "row", 1)]
        mine = jnp.concatenate([head, tail])
        half = call(
            functools.partial(first_half_kernel, pb, mine_order),
            shape(n_col, count, width),
            [VMEM] * 2,
            name + "_a",
        )(mine, dense)
        others = jnp.concatenate(other)
        n_probes = n_col if extra else 0
        outs = [shape(count, width)]
        outs += [shape(send_rows + (16 if extra else 0), LANES, dtype=BF16)] * (n_col - 1)
        if extra:
            outs.append(shape(8, LANES))
        return call(
            functools.partial(second_half_kernel, pb, others_order, n_probes),
            outs,
            [VMEM] * (3 + (1 + n_probes if extra else 0)),
            name + "_b",
        )(others, dense, half, *(extra or []))

    reduce_order = [2, 1, 3] if n_col == 4 else list(range(1, n_col))

    def exchange(sends):
        got = {m: swap(sends[m - 1], "col", m) for m in reduce_order}
        return [got[m] for m in reduce_order]

    head, tail = gather(barrier(t_cur.astype(BF16)))
    probe_pieces = {0: probes}
    stages = [n_col >> (i + 1) for i in range(n_col.bit_length() - 1)]
    k = stages[0]
    probe_pieces[k] = swap(probes, "col", k)
    head, tail, dense = barrier((head, tail, dense))
    own, *sends = halves(head, tail, dense, None, "first")
    received = exchange(sends)
    rounded, tile = call(
        functools.partial(next_kernel, n_col),
        [shape(count, width, dtype=BF16), shape(8, LANES)],
        [VMEM] * (n_col + 3),
        "next",
    )(own, *received, t_prev, t_cur, probes)
    t_next = call(
        functools.partial(value_kernel, n_col), shape(count, width), [VMEM] * (n_col + 1), "value"
    )(own, *received, t_prev)

    head, tail = gather(rounded)
    rounded, probe_pieces = barrier((rounded, probe_pieces))
    for k in stages[1:]:
        keys = list(probe_pieces)
        got = swap(jnp.stack([probe_pieces[m] for m in keys]), "col", k)
        for n, m in enumerate(keys):
            probe_pieces[m ^ k] = got[n]
    extra = [tile] + [probe_pieces[m] for m in range(n_col)]
    own, *sends, mine = halves(head, tail, dense, extra, "second")
    received = exchange(sends)
    tile = call(
        functools.partial(tile_kernel, send_rows), shape(8, LANES), [VMEM] * n_col, "sums"
    )(mine, *received)
    t_after, accum_out = call(
        functools.partial(last_kernel, n_col),
        [shape(count, width), shape(count, width)],
        [SMEM] + [VMEM] * (n_col + 3),
        "last",
    )(coeffs, own, *received, t_cur, t_next, accum)

    total = tile
    for k in far:
        total = total + swap(tile, "row", k ^ 1)
    total = total + swap(total, "row", 1)
    moments = total[:2, :count] * float(total_rows) ** (-0.5)
    return (t_next, t_after, accum_out, moments)


def solution(mesh):
    vector = P(None, ("row", "col"))
    return jax.shard_map(
        functools.partial(local, mesh.shape["row"], mesh.shape["col"]),
        mesh=mesh,
        in_specs=(
            P("row", "col", None, None, None),
            P("row", "col", None),
            P("row", "col", None),
            P("row", "col"),
            vector,
            vector,
            vector,
            vector,
            P(),
        ),
        out_specs=(vector, vector, vector, P()),
        check_vma=False,
    )
```

time: 183 us -> 49.7 us (0.27)
  blocking collectives: 61.2 us -> 0 us
  waiting for transfers between devices: 69.5 us -> 16.4 us
  starting transfers between devices: 0.08 us -> 22.1 us
  other arithmetic: 19 us -> 1.52 us
  between operations: 14.8 us -> 1.48 us
  local copies, waits for them, and re-layouts: 8.95 us -> 0.88 us
  matrix products: 7.92 us -> 0 us
  Pallas kernels: 0 us -> 7.15 us
    psum x2 -> x0, waiting for transfers between devices: 69.5 us -> none  [product(): summed = lax.psum(partial_value, 'col')]
    psum x1 -> x0, blocking collectives: 40.2 us -> none  [moment_one(): return lax.psum(local_sum, ('row', 'col'))]
    ppermute x0 -> x22, starting transfers between devices: none -> 22.1 us  [swap(): return lax.ppermute(x, axis, [(i, i ^ k) for i in range(n)])]
    all_gather x2 -> x0, blocking collectives: 21.1 us -> none  [product(): lax.all_gather(vectors.astype(jnp.bfloat16), 'row', axis=1, tiled=True)]
    ppermute x0 -> x22, waiting for transfers between devices: none -> 16.4 us  [swap(): return lax.ppermute(x, axis, [(i, i ^ k) for i in range(n)])]
    scatter-add x4 -> x0, other arithmetic: 8.56 us -> none  [add_group(): return total.at[:, group_rows, :].add(contrib)]
    dot_general x4 -> x0, matrix products: 7.92 us -> none  [add_group(): jnp.einsum('pgj,gij->pgi', picked, tile_group, preferred_element_type=jnp...]
    pallas_call x0 -> x9, Pallas kernels: none -> 7.15 us  [the longest x1 2.02 us: local(): call(functools.partial(place_kernel, pb, group), shape(n_row, pb, n_col *...]
  transfers between devices with their start and end apart: 2 -> 22, of which waited for: 2 -> 12; matrix products, arithmetic and copies ran while one was open for 0% -> 0% of each run, Pallas kernels for 0% -> 13%
where the time goes in v1:
time: 49.7 us; the launch traced here: 49.5 us
  starting transfers between devices  22.1 us (44%)
  waiting for transfers between devices  16.4 us (33%)
  Pallas kernels  7.15 us (14%)
  other arithmetic  1.52 us (3%)
  between operations  1.48 us (3%)
  local copies, waits for them, and re-layouts  0.88 us (2%)
    ppermute x22, starting transfers between devices, swap(): return lax.ppermute(x, axis, [(i, i ^ k) for i in range(n)])  22.1 us
    ppermute x22, waiting for transfers between devices, swap(): return lax.ppermute(x, axis, [(i, i ^ k) for i in range(n)])  16.4 us
    pallas_call x1, Pallas kernels, local(): call(functools.partial(place_kernel, pb, group), shape(n_row, pb, n_col *...  2.02 us
    pallas_call x2, Pallas kernels, halves(): call(functools.partial(second_half_kernel, pb, others_order, n_probes), o...  1.62 us
    pallas_call x2, Pallas kernels, halves(): call(functools.partial(first_half_kernel, pb, mine_order), shape(n_col, c...  1.5 us
    pallas_call x1, Pallas kernels, local(): call(functools.partial(last_kernel, n_col), [shape(count, width), shape(c...  1.22 us
  transfers between devices with their start and end apart: 22, of which 12 were waited for; matrix products, arithmetic and copies ran while one was open for 0% of the time, Pallas kernels for 13%

profile of v1, /device:TPU:0, one launch (start us, length us, event | category | flops | bytes accessed | tf_op | source)
XLA Modules:
  0.0 49.5 jit_solution(17468704666508573839)
XLA Ops:
  0.6 0.8 %convert_element_type.3 = bf16[64,256]{1,0:T(8,128)(2,1)S(1)} convert(f32[64,256]{1,0:T(8,128)} %refs_3_.5) | non-fusion elementwise | flops 16384 | bytes 98304 | tf_op jit(solution)/shard_map/convert_element_type | solution.py:238
  1.5 2.4 %collective-permute-start.1 = (bf16[64,256]{1,0:T(8,128)(2,1)S(1)}, bf16[64,256]{1,0:T(8,128)(2,1)S(1)}, u32[]{:S(2)}, u32[]{:S(2)}) collective-permute-start(bf16[64,256]{1,0:T(8,128)(2,1)S(1)} %convert_element_type.3), channel_id=1, source_target_pairs={{0,20},{4,16},{8,28},{12,24},{16,4},{20,0},{24,12},{28,8},{1,21},{... | collective-permute-start | bytes 98312 | tf_op jit(solution)/shard_map/ppermute | solution.py:164
  3.9 1.7 %collective-permute-start = (bf16[64,256]{1,0:T(8,128)(2,1)S(1)}, bf16[64,256]{1,0:T(8,128)(2,1)S(1)}, u32[]{:S(2)}, u32[]{:S(2)}) collective-permute-start(bf16[64,256]{1,0:T(8,128)(2,1)S(1)} %convert_element_type.3), channel_id=1, source_target_pairs={{0,28},{4,24},{8,20},{12,16},{16,12},{20,8},{24,4},{28,0},{1,29},{... | collective-permute-start | bytes 98312 | tf_op jit(solution)/shard_map/ppermute | solution.py:164
  5.6 0.1 collective-permute-start.2
  5.7 2.6 %collective-permute-start.13 = (f32[64,256]{1,0:T(8,128)}, f32[64,256]{1,0:T(8,128)S(1)}, u32[]{:S(2)}, u32[]{:S(2)}) collective-permute-start(f32[64,256]{1,0:T(8,128)} %refs_1_), channel_id=1, source_target_pairs={{0,2},{1,3},{2,0},{3,1},{4,6},{5,7},{6,4},{7,5},{8,10},{9,11},{10,... | collective-permute-start | bytes 196616 | tf_op jit(solution)/shard_map/ppermute | solution.py:164
  8.9 2.0 %place.1.dense = bf16[8,2,1024,128]{3,2,1,0:T(8,128)(2,1)S(1)} custom-call(s32[1,1]{1,0:T(1,128)S(6)} %copy.13.count, s32[1,1,64]{2,1,0:T(1,128)} %rows_in.1, s32[1,1,64]{2,1,0:T(1,128)} %cols_in.1, bf16[1,1,64,128,128]{4,3,2,1,0:T(8,128)(2,1)} %blocks.1), custom_call_target="tpu_custom_call" | custom-call | tf_op jit(solution)/shard_map/place/pallas_call | solution.py:185
  11.0 0.0 collective-permute-done.1
  11.0 0.0 collective-permute-done
  11.0 0.0 collective-permute-done.2
  11.0 0.4 collective-permute-start.4
  11.4 0.2 collective-permute-start.3
  11.6 0.0 copy-start
  11.6 0.0 copy-start.1
  11.6 0.0 copy-start.2
  11.6 0.8 %first_a.1.half = f32[4,64,256]{2,1,0:T(8,128)S(1)} custom-call(bf16[4,64,256]{2,1,0:T(8,128)(2,1)S(1)} %pad_maximum_fusion.1.vectors, bf16[8,2,1024,128]{3,2,1,0:T(8,128)(2,1)S(1)} %place.1.dense), custom_call_target="tpu_custom_call" | custom-call | tf_op jit(solution)/shard_map/first_a/pallas_call | solution.py:213
  12.4 0.0 collective-permute-done.4
  12.4 0.3 collective-permute-done.3
  12.7 0.8 %first_b.1 = (f32[64,256]{1,0:T(8,128)S(1)}, bf16[128,128]{1,0:T(8,128)(2,1)S(1)}, bf16[128,128]{1,0:T(8,128)(2,1)S(1)}, bf16[128,128]{1,0:T(8,128)(2,1)S(1)}) custom-call(bf16[4,64,256]{2,1,0:T(8,128)(2,1)S(1)} %pad_maximum_fusion.vectors, bf16[8,2,1024,128]{3,2,1,0:T(8,128)(2,1)S(1)} %place.1.dense, f32[4,64,256]{2,1,0:T(8,128)S(1)} %first_a.1.half), custom_call_target="tpu_custom_call" | custom-call | tf_op jit(solution)/shard_map/first_b/pallas_call | solution.py:225
  13.5 0.6 %collective-permute-start.5 = (bf16[128,128]{1,0:T(8,128)(2,1)S(1)}, bf16[128,128]{1,0:T(8,128)(2,1)S(1)}, u32[]{:S(2)}, u32[]{:S(2)}) collective-permute-start(bf16[128,128]{1,0:T(8,128)(2,1)S(1)} %get-tuple-element.26), channel_id=1, source_target_pairs={{0,2},{1,3},{2,0},{3,1},{4,6},{5,7},{6,4},{7,5},{8,10},{9,11},{10,... | collective-permute-start | bytes 98312 | tf_op jit(solution)/shard_map/ppermute | solution.py:164
  14.1 1.6 %collective-permute-start.6 = (bf16[128,128]{1,0:T(8,128)(2,1)S(1)}, bf16[128,128]{1,0:T(8,128)(2,1)S(1)}, u32[]{:S(2)}, u32[]{:S(2)}) collective-permute-start(bf16[128,128]{1,0:T(8,128)(2,1)S(1)} %get-tuple-element.27), channel_id=1, source_target_pairs={{0,1},{1,0},{2,3},{3,2},{4,5},{5,4},{6,7},{7,6},{8,9},{9,8},{10,11... | collective-permute-start | bytes 98312 | tf_op jit(solution)/shard_map/ppermute | solution.py:164
  15.6 2.3 %collective-permute-start.7 = (bf16[128,128]{1,0:T(8,128)(2,1)S(1)}, bf16[128,128]{1,0:T(8,128)(2,1)S(1)}, u32[]{:S(2)}, u32[]{:S(2)}) collective-permute-start(bf16[128,128]{1,0:T(8,128)(2,1)S(1)} %get-tuple-element.28), channel_id=1, source_target_pairs={{0,3},{1,2},{2,1},{3,0},{4,7},{5,6},{6,5},{7,4},{8,11},{9,10},{10,... | collective-permute-start | bytes 98312 | tf_op jit(solution)/shard_map/ppermute | solution.py:164
  18.0 0.4 collective-permute-done.5.refs_0_
  18.4 0.0 collective-permute-done.6.refs_1_
  18.4 3.0 %collective-permute-done.7.refs_2_ = bf16[128,128]{1,0:T(8,128)(2,1)S(1)} collective-permute-done((bf16[128,128]{1,0:T(8,128)(2,1)S(1)}, bf16[128,128]{1,0:T(8,128)(2,1)S(1)}, u32[]{:S(2)}, u32[]{:S(2)}) %collective-permute-start.7) | collective-permute-done | bytes 32800 | tf_op jit(solution)/shard_map/ppermute | solution.py:164
  21.3 0.0 copy-done
  21.4 0.0 copy-done.1
  21.4 0.0 copy-done.2
  21.4 0.1 next.1
  21.5 0.1 collective-permute-start.11
  21.6 2.7 %collective-permute-start.9 = (bf16[64,256]{1,0:T(8,128)(2,1)S(1)}, bf16[64,256]{1,0:T(8,128)(2,1)S(1)}, u32[]{:S(2)}, u32[]{:S(2)}) collective-permute-start(bf16[64,256]{1,0:T(8,128)(2,1)S(1)} %get-tuple-element.29), channel_id=1, source_target_pairs={{0,20},{4,16},{8,28},{12,24},{16,4},{20,0},{24,12},{28,8},{1,21},{... | collective-permute-start | bytes 98312 | tf_op jit(solution)/shard_map/ppermute | solution.py:164
  24.2 0.1 collective-permute-start.8
  24.4 0.0 collective-permute-done.13.refs_3_
  24.4 0.1 collective-permute-start.14
  24.5 0.7 %collective-permute-done.11 = bf16[64,256]{1,0:T(8,128)(2,1)S(1)} collective-permute-done((bf16[64,256]{1,0:T(8,128)(2,1)S(1)}, bf16[64,256]{1,0:T(8,128)(2,1)S(1)}, u32[]{:S(2)}, u32[]{:S(2)}) %collective-permute-start.11) | collective-permute-done | bytes 32800 | tf_op jit(solution)/shard_map/ppermute | solution.py:164
  25.2 0.0 collective-permute-start.12
  25.2 0.6 %collective-permute-done.9 = bf16[64,256]{1,0:T(8,128)(2,1)S(1)} collective-permute-done((bf16[64,256]{1,0:T(8,128)(2,1)S(1)}, bf16[64,256]{1,0:T(8,128)(2,1)S(1)}, u32[]{:S(2)}, u32[]{:S(2)}) %collective-permute-start.9) | collective-permute-done | bytes 32800 | tf_op jit(solution)/shard_map/ppermute | solution.py:164
  25.8 2.6 %collective-permute-done.8 = bf16[64,256]{1,0:T(8,128)(2,1)S(1)} collective-permute-done((bf16[64,256]{1,0:T(8,128)(2,1)S(1)}, bf16[64,256]{1,0:T(8,128)(2,1)S(1)}, u32[]{:S(2)}, u32[]{:S(2)}) %collective-permute-start.8) | collective-permute-done | bytes 32800 | tf_op jit(solution)/shard_map/ppermute | solution.py:164
  28.5 0.1 collective-permute-start.10
  28.6 0.0 copy-start.4
  28.6 0.0 copy-start.5
  28.6 0.8 %second_a.1.half = f32[4,64,256]{2,1,0:T(8,128)S(1)} custom-call(bf16[4,64,256]{2,1,0:T(8,128)(2,1)S(1)} %pad_maximum_fusion.3.vectors, bf16[8,2,1024,128]{3,2,1,0:T(8,128)(2,1)S(1)} %place.1.dense), custom_call_target="tpu_custom_call" | custom-call | tf_op jit(solution)/shard_map/second_a/pallas_call | solution.py:213
  29.4 1.0 %collective-permute-done.14 = f32[2,64,256]{2,1,0:T(8,128)S(1)} collective-permute-done((f32[2,64,256]{2,1,0:T(8,128)S(1)}, f32[2,64,256]{2,1,0:T(8,128)S(1)}, u32[]{:S(2)}, u32[]{:S(2)}) %collective-permute-start.14) | collective-permute-done | bytes 131104 | tf_op jit(solution)/shard_map/ppermute | solution.py:164
  30.4 0.0 collective-permute-done.12
  30.4 0.0 collective-permute-done.10
  30.4 0.9 %second_b.1 = (f32[64,256]{1,0:T(8,128)S(1)}, bf16[144,128]{1,0:T(8,128)(2,1)S(1)}, bf16[144,128]{1,0:T(8,128)(2,1)S(1)}, bf16[144,128]{1,0:T(8,128)(2,1)S(1)}, f32[8,128]{1,0:T(8,128)S(1)}) custom-call(bf16[4,64,256]{2,1,0:T(8,128)(2,1)S(1)} %pad_maximum_fusion.2.vectors, bf16[8,2,1024,128]{3,2,1,0:T(8,128)(2,1)S(1)} %place.1.dense, ...), custom_call_target="tpu_custom_call" | custom-call | tf_op jit(solution)/shard_map/second_b/pallas_call | solution.py:225
  31.3 1.2 %collective-permute-start.15 = (bf16[144,128]{1,0:T(8,128)(2,1)S(1)}, bf16[144,128]{1,0:T(8,128)(2,1)S(1)}, u32[]{:S(2)}, u32[]{:S(2)}) collective-permute-start(bf16[144,128]{1,0:T(8,128)(2,1)S(1)} %get-tuple-element.34), channel_id=1, source_target_pairs={{0,2},{1,3},{2,0},{3,1},{4,6},{5,7},{6,4},{7,5},{8,10},{9,11},{10,... | collective-permute-start | bytes 110600 | tf_op jit(solution)/shard_map/ppermute | solution.py:164
  32.5 1.7 %collective-permute-start.16 = (bf16[144,128]{1,0:T(8,128)(2,1)S(1)}, bf16[144,128]{1,0:T(8,128)(2,1)S(1)}, u32[]{:S(2)}, u32[]{:S(2)}) collective-permute-start(bf16[144,128]{1,0:T(8,128)(2,1)S(1)} %get-tuple-element.35), channel_id=1, source_target_pairs={{0,1},{1,0},{2,3},{3,2},{4,5},{5,4},{6,7},{7,6},{8,9},{9,8},{10,11... | collective-permute-start | bytes 110600 | tf_op jit(solution)/shard_map/ppermute | solution.py:164
  34.2 1.5 %collective-permute-start.17 = (bf16[144,128]{1,0:T(8,128)(2,1)S(1)}, bf16[144,128]{1,0:T(8,128)(2,1)S(1)}, u32[]{:S(2)}, u32[]{:S(2)}) collective-permute-start(bf16[144,128]{1,0:T(8,128)(2,1)S(1)} %get-tuple-element.36), channel_id=1, source_target_pairs={{0,3},{1,2},{2,1},{3,0},{4,7},{5,6},{6,5},{7,4},{8,11},{9,10},{10,... | collective-permute-start | bytes 110600 | tf_op jit(solution)/shard_map/ppermute | solution.py:164
  35.7 1.0 %collective-permute-done.15.refs_0_ = bf16[144,128]{1,0:T(8,128)(2,1)S(1)} collective-permute-done((bf16[144,128]{1,0:T(8,128)(2,1)S(1)}, bf16[144,128]{1,0:T(8,128)(2,1)S(1)}, u32[]{:S(2)}, u32[]{:S(2)}) %collective-permute-start.15) | collective-permute-done | bytes 36896 | tf_op jit(solution)/shard_map/ppermute | solution.py:164
  36.7 0.0 collective-permute-done.16.refs_1_
  36.8 3.2 %collective-permute-done.17.refs_2_ = bf16[144,128]{1,0:T(8,128)(2,1)S(1)} collective-permute-done((bf16[144,128]{1,0:T(8,128)(2,1)S(1)}, bf16[144,128]{1,0:T(8,128)(2,1)S(1)}, u32[]{:S(2)}, u32[]{:S(2)}) %collective-permute-start.17) | collective-permute-done | bytes 36896 | tf_op jit(solution)/shard_map/ppermute | solution.py:164
  40.0 0.1 collective-permute-start.20
  40.1 2.2 %collective-permute-start.19 = (f32[8,128]{1,0:T(8,128)S(1)}, f32[8,128]{1,0:T(8,128)S(1)}, u32[]{:S(2)}, u32[]{:S(2)}) collective-permute-start(f32[8,128]{1,0:T(8,128)S(1)} %sums.1), channel_id=1, source_target_pairs={{0,20},{4,16},{8,28},{12,24},{16,4},{20,0},{24,12},{28,8},{1,21},{... | collective-permute-start | bytes 12296 | tf_op jit(solution)/shard_map/ppermute | solution.py:164
  42.2 0.5 %collective-permute-start.18 = (f32[8,128]{1,0:T(8,128)S(1)}, f32[8,128]{1,0:T(8,128)S(1)}, u32[]{:S(2)}, u32[]{:S(2)}) collective-permute-start(f32[8,128]{1,0:T(8,128)S(1)} %sums.1), channel_id=1, source_target_pairs={{0,28},{4,24},{8,20},{12,16},{16,12},{20,8},{24,4},{28,0},{1,29},{... | collective-permute-start | bytes 12296 | tf_op jit(solution)/shard_map/ppermute | solution.py:164
  42.7 0.4 collective-permute-done.20
  43.1 0.5 collective-permute-done.19
  43.6 2.6 %collective-permute-done.18 = f32[8,128]{1,0:T(8,128)S(1)} collective-permute-done((f32[8,128]{1,0:T(8,128)S(1)}, f32[8,128]{1,0:T(8,128)S(1)}, u32[]{:S(2)}, u32[]{:S(2)}) %collective-permute-start.18) | collective-permute-done | bytes 4128 | tf_op jit(solution)/shard_map/ppermute | solution.py:164
  46.2 0.0 collective-permute-start.21
  46.2 0.7 %value.1.refs_4_ = f32[64,256]{1,0:T(8,128)} custom-call(f32[64,256]{1,0:T(8,128)S(1)} %get-tuple-element.25.own, bf16[128,128]{1,0:T(8,128)(2,1)S(1)} %collective-permute-done.5.refs_0_, bf16[128,128]{1,0:T(8,128)(2,1)S(1)} %collective-permute-done.6.refs_1_, bf16[128,128]{1,0:T(8,128)(2,1)S(1)} %collective-permute-done.7.refs_2_, f32[64,256]{1,0:T(8,128)S(1)} %copy-done.2), custom_call_target="tpu_custom_call" | custom-call | tf_op jit(solution)/shard_map/value/pallas_call | solution.py:252
  46.8 0.0 copy-done.4
  46.8 0.8 %copy-done.3 = f32[64,256]{1,0:T(8,128)S(1)} copy-done((f32[64,256]{1,0:T(8,128)S(1)}, f32[64,256]{1,0:T(8,128)}, u32[]{:S(2)}) %copy-start.3) | copy-done | bytes 65560
  47.7 1.2 %last.1 = (f32[64,256]{1,0:T(8,128)}, f32[64,256]{1,0:T(8,128)}) custom-call(f32[2]{0:T(128)S(1)} %copy-done.5, f32[64,256]{1,0:T(8,128)S(1)} %get-tuple-element.33.own, bf16[144,128]{1,0:T(8,128)(2,1)S(1)} %collective-permute-done.15.refs_0_, bf16[144,128]{1,0:T(8,128)(2,1)S(1)} %collective-permute-done.16.refs_1_, ...), custom_call_target="tpu_custom_call" | custom-call | tf_op jit(solution)/shard_map/last/pallas_call | solution.py:269
  48.9 0.0 collective-permute-done.21
  48.9 0.6 %slice_multiply_fusion = f32[2,64]{1,0:T(2,128)} fusion(f32[8,128]{1,0:T(8,128)S(1)} %add.15), kind=kLoop, calls=%fused_computation.10 | loop fusion | flops 128 | bytes 1024 | tf_op jit(solution)/shard_map/mul | solution.py:280
  (13 shorter events, 0.1 us)
Async XLA Ops:
  1.5 9.5 %collective-permute-start.1 = (bf16[64,256]{1,0:T(8,128)(2,1)S(1)}, bf16[64,256]{1,0:T(8,128)(2,1)S(1)}, u32[]{:S(2)}, u32[]{:S(2)}) collective-permute-start(bf16[64,256]{1,0:T(8,128)(2,1)S(1)} %convert_element_type.3), channel_id=1, source_target_pairs={{0,20},{4,16},{8,28},{12,24},{16,4},{20,0},{24,12},{28,8},{1,21},{... | collective-permute-start | bytes 98312 | tf_op jit(solution)/shard_map/ppermute | solution.py:164
  3.9 7.1 %collective-permute-start = (bf16[64,256]{1,0:T(8,128)(2,1)S(1)}, bf16[64,256]{1,0:T(8,128)(2,1)S(1)}, u32[]{:S(2)}, u32[]{:S(2)}) collective-permute-start(bf16[64,256]{1,0:T(8,128)(2,1)S(1)} %convert_element_type.3), channel_id=1, source_target_pairs={{0,28},{4,24},{8,20},{12,16},{16,12},{20,8},{24,4},{28,0},{1,29},{... | collective-permute-start | bytes 98312 | tf_op jit(solution)/shard_map/ppermute | solution.py:164
  5.6 5.4 %collective-permute-start.2 = (bf16[64,256]{1,0:T(8,128)(2,1)S(1)}, bf16[64,256]{1,0:T(8,128)(2,1)S(1)}, u32[]{:S(2)}, u32[]{:S(2)}) collective-permute-start(bf16[64,256]{1,0:T(8,128)(2,1)S(1)} %convert_element_type.3), channel_id=1, source_target_pairs={{0,12},{4,8},{8,4},{12,0},{16,28},{20,24},{24,20},{28,16},{1,13},{... | collective-permute-start | bytes 98312 | tf_op jit(solution)/shard_map/ppermute | solution.py:164
  5.7 18.7 %collective-permute-start.13 = (f32[64,256]{1,0:T(8,128)}, f32[64,256]{1,0:T(8,128)S(1)}, u32[]{:S(2)}, u32[]{:S(2)}) collective-permute-start(f32[64,256]{1,0:T(8,128)} %refs_1_), channel_id=1, source_target_pairs={{0,2},{1,3},{2,0},{3,1},{4,6},{5,7},{6,4},{7,5},{8,10},{9,11},{10,... | collective-permute-start | bytes 196616 | tf_op jit(solution)/shard_map/ppermute | solution.py:164
  11.0 1.4 %collective-permute-start.4 = (bf16[1,64,256]{2,1,0:T(8,128)(2,1)S(1)}, bf16[1,64,256]{2,1,0:T(8,128)(2,1)S(1)}, u32[]{:S(2)}, u32[]{:S(2)}) collective-permute-start(bf16[1,64,256]{2,1,0:T(8,128)(2,1)S(1)} %bitcast.27), channel_id=1, source_target_pairs={{0,4},{4,0},{8,12},{12,8},{16,20},{20,16},{24,28},{28,24},{1,5},{5... | collective-permute-start | bytes 98312 | tf_op jit(solution)/shard_map/ppermute | solution.py:164
  11.4 1.3 %collective-permute-start.3 = (bf16[3,64,256]{2,1,0:T(8,128)(2,1)S(1)}, bf16[3,64,256]{2,1,0:T(8,128)(2,1)S(1)}, u32[]{:S(2)}, u32[]{:S(2)}) collective-permute-start(bf16[3,64,256]{2,1,0:T(8,128)(2,1)S(1)} %pad_maximum_fusion.5), channel_id=1, source_target_pairs={{0,4},{4,0},{8,12},{12,8},{16,20},{20,16},{24,28},{28,24},{1,5},{5... | collective-permute-start | bytes 294920 | tf_op jit(solution)/shard_map/ppermute | solution.py:164
  11.6 9.7 %copy-start = (f32[64,256]{1,0:T(8,128)S(1)}, f32[64,256]{1,0:T(8,128)}, u32[]{:S(2)}) copy-start(f32[64,256]{1,0:T(8,128)} %refs_1_) | copy-start | bytes 196612
  11.6 9.7 %copy-start.1 = (f32[64,256]{1,0:T(8,128)S(1)}, f32[64,256]{1,0:T(8,128)}, u32[]{:S(2)}) copy-start(f32[64,256]{1,0:T(8,128)} %refs_3_.5) | copy-start | bytes 196612
  11.6 9.7 %copy-start.2 = (f32[64,256]{1,0:T(8,128)S(1)}, f32[64,256]{1,0:T(8,128)}, u32[]{:S(2)}) copy-start(f32[64,256]{1,0:T(8,128)} %refs_3_.4) | copy-start | bytes 196612
  13.5 4.9 %collective-permute-start.5 = (bf16[128,128]{1,0:T(8,128)(2,1)S(1)}, bf16[128,128]{1,0:T(8,128)(2,1)S(1)}, u32[]{:S(2)}, u32[]{:S(2)}) collective-permute-start(bf16[128,128]{1,0:T(8,128)(2,1)S(1)} %get-tuple-element.26), channel_id=1, source_target_pairs={{0,2},{1,3},{2,0},{3,1},{4,6},{5,7},{6,4},{7,5},{8,10},{9,11},{10,... | collective-permute-start | bytes 98312 | tf_op jit(solution)/shard_map/ppermute | solution.py:164
  14.1 4.3 %collective-permute-start.6 = (bf16[128,128]{1,0:T(8,128)(2,1)S(1)}, bf16[128,128]{1,0:T(8,128)(2,1)S(1)}, u32[]{:S(2)}, u32[]{:S(2)}) collective-permute-start(bf16[128,128]{1,0:T(8,128)(2,1)S(1)} %get-tuple-element.27), channel_id=1, source_target_pairs={{0,1},{1,0},{2,3},{3,2},{4,5},{5,4},{6,7},{7,6},{8,9},{9,8},{10,11... | collective-permute-start | bytes 98312 | tf_op jit(solution)/shard_map/ppermute | solution.py:164
  15.6 5.7 %collective-permute-start.7 = (bf16[128,128]{1,0:T(8,128)(2,1)S(1)}, bf16[128,128]{1,0:T(8,128)(2,1)S(1)}, u32[]{:S(2)}, u32[]{:S(2)}) collective-permute-start(bf16[128,128]{1,0:T(8,128)(2,1)S(1)} %get-tuple-element.28), channel_id=1, source_target_pairs={{0,3},{1,2},{2,1},{3,0},{4,7},{5,6},{6,5},{7,4},{8,11},{9,10},{10,... | collective-permute-start | bytes 98312 | tf_op jit(solution)/shard_map/ppermute | solution.py:164
  21.5 3.7 %collective-permute-start.11 = (bf16[64,256]{1,0:T(8,128)(2,1)S(1)}, bf16[64,256]{1,0:T(8,128)(2,1)S(1)}, u32[]{:S(2)}, u32[]{:S(2)}) collective-permute-start(bf16[64,256]{1,0:T(8,128)(2,1)S(1)} %get-tuple-element.29), channel_id=1, source_target_pairs={{0,12},{4,8},{8,4},{12,0},{16,28},{20,24},{24,20},{28,16},{1,13},{... | collective-permute-start | bytes 98312 | tf_op jit(solution)/shard_map/ppermute | solution.py:164
  21.6 4.3 %collective-permute-start.9 = (bf16[64,256]{1,0:T(8,128)(2,1)S(1)}, bf16[64,256]{1,0:T(8,128)(2,1)S(1)}, u32[]{:S(2)}, u32[]{:S(2)}) collective-permute-start(bf16[64,256]{1,0:T(8,128)(2,1)S(1)} %get-tuple-element.29), channel_id=1, source_target_pairs={{0,20},{4,16},{8,28},{12,24},{16,4},{20,0},{24,12},{28,8},{1,21},{... | collective-permute-start | bytes 98312 | tf_op jit(solution)/shard_map/ppermute | solution.py:164
  24.2 4.2 %collective-permute-start.8 = (bf16[64,256]{1,0:T(8,128)(2,1)S(1)}, bf16[64,256]{1,0:T(8,128)(2,1)S(1)}, u32[]{:S(2)}, u32[]{:S(2)}) collective-permute-start(bf16[64,256]{1,0:T(8,128)(2,1)S(1)} %get-tuple-element.29), channel_id=1, source_target_pairs={{0,28},{4,24},{8,20},{12,16},{16,12},{20,8},{24,4},{28,0},{1,29},{... | collective-permute-start | bytes 98312 | tf_op jit(solution)/shard_map/ppermute | solution.py:164
  24.4 6.0 %collective-permute-start.14 = (f32[2,64,256]{2,1,0:T(8,128)S(1)}, f32[2,64,256]{2,1,0:T(8,128)S(1)}, u32[]{:S(2)}, u32[]{:S(2)}) collective-permute-start(f32[2,64,256]{2,1,0:T(8,128)S(1)} %pad_maximum_fusion.4), channel_id=1, source_target_pairs={{0,1},{1,0},{2,3},{3,2},{4,5},{5,4},{6,7},{7,6},{8,9},{9,8},{10,11... | collective-permute-start | bytes 393224 | tf_op jit(solution)/shard_map/ppermute | solution.py:164
  25.2 5.2 %collective-permute-start.12 = (bf16[1,64,256]{2,1,0:T(8,128)(2,1)S(1)}, bf16[1,64,256]{2,1,0:T(8,128)(2,1)S(1)}, u32[]{:S(2)}, u32[]{:S(2)}) collective-permute-start(bf16[1,64,256]{2,1,0:T(8,128)(2,1)S(1)} %bitcast.25), channel_id=1, source_target_pairs={{0,4},{4,0},{8,12},{12,8},{16,20},{20,16},{24,28},{28,24},{1,5},{5... | collective-permute-start | bytes 98312 | tf_op jit(solution)/shard_map/ppermute | solution.py:164
  28.5 1.9 %collective-permute-start.10 = (bf16[3,64,256]{2,1,0:T(8,128)(2,1)S(1)}, bf16[3,64,256]{2,1,0:T(8,128)(2,1)S(1)}, u32[]{:S(2)}, u32[]{:S(2)}) collective-permute-start(bf16[3,64,256]{2,1,0:T(8,128)(2,1)S(1)} %pad_maximum_fusion.6), channel_id=1, source_target_pairs={{0,4},{4,0},{8,12},{12,8},{16,20},{20,16},{24,28},{28,24},{1,5},{5... | collective-permute-start | bytes 294920 | tf_op jit(solution)/shard_map/ppermute | solution.py:164
  28.6 18.2 %copy-start.4 = (f32[64,256]{1,0:T(8,128)S(1)}, f32[64,256]{1,0:T(8,128)}, u32[]{:S(2)}) copy-start(f32[64,256]{1,0:T(8,128)} %refs_5_.3) | copy-start | bytes 196612
  28.6 18.2 %copy-start.5 = (f32[2]{0:T(128)S(1)}, f32[2]{0:T(128)}, u32[]{:S(2)}) copy-start(f32[2]{0:T(128)} %coeffs.1) | copy-start | bytes 28
  31.3 5.5 %collective-permute-start.15 = (bf16[144,128]{1,0:T(8,128)(2,1)S(1)}, bf16[144,128]{1,0:T(8,128)(2,1)S(1)}, u32[]{:S(2)}, u32[]{:S(2)}) collective-permute-start(bf16[144,128]{1,0:T(8,128)(2,1)S(1)} %get-tuple-element.34), channel_id=1, source_target_pairs={{0,2},{1,3},{2,0},{3,1},{4,6},{5,7},{6,4},{7,5},{8,10},{9,11},{10,... | collective-permute-start | bytes 110600 | tf_op jit(solution)/shard_map/ppermute | solution.py:164
  32.5 4.3 %collective-permute-start.16 = (bf16[144,128]{1,0:T(8,128)(2,1)S(1)}, bf16[144,128]{1,0:T(8,128)(2,1)S(1)}, u32[]{:S(2)}, u32[]{:S(2)}) collective-permute-start(bf16[144,128]{1,0:T(8,128)(2,1)S(1)} %get-tuple-element.35), channel_id=1, source_target_pairs={{0,1},{1,0},{2,3},{3,2},{4,5},{5,4},{6,7},{7,6},{8,9},{9,8},{10,11... | collective-permute-start | bytes 110600 | tf_op jit(solution)/shard_map/ppermute | solution.py:164
  34.2 5.8 %collective-permute-start.17 = (bf16[144,128]{1,0:T(8,128)(2,1)S(1)}, bf16[144,128]{1,0:T(8,128)(2,1)S(1)}, u32[]{:S(2)}, u32[]{:S(2)}) collective-permute-start(bf16[144,128]{1,0:T(8,128)(2,1)S(1)} %get-tuple-element.36), channel_id=1, source_target_pairs={{0,3},{1,2},{2,1},{3,0},{4,7},{5,6},{6,5},{7,4},{8,11},{9,10},{10,... | collective-permute-start | bytes 110600 | tf_op jit(solution)/shard_map/ppermute | solution.py:164
  40.0 3.1 %collective-permute-start.20 = (f32[8,128]{1,0:T(8,128)S(1)}, f32[8,128]{1,0:T(8,128)S(1)}, u32[]{:S(2)}, u32[]{:S(2)}) collective-permute-start(f32[8,128]{1,0:T(8,128)S(1)} %sums.1), channel_id=1, source_target_pairs={{0,12},{4,8},{8,4},{12,0},{16,28},{20,24},{24,20},{28,16},{1,13},{... | collective-permute-start | bytes 12296 | tf_op jit(solution)/shard_map/ppermute | solution.py:164
  40.1 3.5 %collective-permute-start.19 = (f32[8,128]{1,0:T(8,128)S(1)}, f32[8,128]{1,0:T(8,128)S(1)}, u32[]{:S(2)}, u32[]{:S(2)}) collective-permute-start(f32[8,128]{1,0:T(8,128)S(1)} %sums.1), channel_id=1, source_target_pairs={{0,20},{4,16},{8,28},{12,24},{16,4},{20,0},{24,12},{28,8},{1,21},{... | collective-permute-start | bytes 12296 | tf_op jit(solution)/shard_map/ppermute | solution.py:164
  42.2 3.9 %collective-permute-start.18 = (f32[8,128]{1,0:T(8,128)S(1)}, f32[8,128]{1,0:T(8,128)S(1)}, u32[]{:S(2)}, u32[]{:S(2)}) collective-permute-start(f32[8,128]{1,0:T(8,128)S(1)} %sums.1), channel_id=1, source_target_pairs={{0,28},{4,24},{8,20},{12,16},{16,12},{20,8},{24,4},{28,0},{1,29},{... | collective-permute-start | bytes 12296 | tf_op jit(solution)/shard_map/ppermute | solution.py:164
  46.2 2.7 %collective-permute-start.21 = (f32[8,128]{1,0:T(8,128)S(1)}, f32[8,128]{1,0:T(8,128)S(1)}, u32[]{:S(2)}, u32[]{:S(2)}) collective-permute-start(f32[8,128]{1,0:T(8,128)S(1)} %add_add_fusion), channel_id=1, source_target_pairs={{0,4},{4,0},{8,12},{12,8},{16,20},{20,16},{24,28},{28,24},{1,5},{5... | collective-permute-start | bytes 12296 | tf_op jit(solution)/shard_map/ppermute | solution.py:164
  46.8 0.8 %copy-start.3 = (f32[64,256]{1,0:T(8,128)S(1)}, f32[64,256]{1,0:T(8,128)}, u32[]{:S(2)}) copy-start(f32[64,256]{1,0:T(8,128)} %value.1.refs_4_) | copy-start | bytes 196612

commit v2 on v1

--- a/solution.py
+++ b/solution.py
@@ -13,6 +13,9 @@
 CONTRACT_LAST = (((1,), (1,)), ((), ()))
 F32, BF16 = jnp.float32, jnp.bfloat16
 LANES = 128
+ORDER1 = [1, 3, 2]
+ORDER2 = [2, 3, 1]
+FAR = [6, 4, 2]
 
 
 def place_kernel(pb, group, count, rows_in, cols_in, blocks, dense, held, rows, cols, sems, own_sems):
@@ -77,52 +80,86 @@
     return high, x - high
 
 
-def second_half_kernel(pb, order, n_probes, vectors, dense, half, *refs):
-    width = vectors.shape[2]
-    chunks = half.shape[0]
-    tile = None
-    if n_probes:
-        before, probes, refs = refs[0], refs[1 : 1 + n_probes], refs[1 + n_probes :]
-    own, sends = refs[0], refs[1 : chunks]
+def put_halves(ref, start, value):
+    count = value.shape[0]
+    for s in range(value.shape[1] // LANES):
+        ref[pl.ds(start + s * count, count), :] = value[:, s * LANES : (s + 1) * LANES]
+
+
+def get_halves(ref, start, count, width):
+    return jnp.concatenate(
+        [ref[pl.ds(start + s * count, count), :] for s in range(width // LANES)], axis=1
+    )
+
+
+def second_half_kernel(pb, order, send_order, n_carried, vectors, dense, half, *refs):
+    width, chunks = vectors.shape[2], half.shape[0]
+    carried, own = refs[:n_carried], refs[n_carried]
+    sends = dict(zip(send_order, refs[n_carried + 1 :]))
+    for m in range(chunks):
+        total = half[m] + dots(pb, order, vectors, dense, m, width)
+        if m == 0:
+            own[...] = total
+        else:
+            put_halves(sends[m], 0, total.astype(BF16))
+    rows = own.shape[0] * width // LANES
+    for n, piece in enumerate(carried):
+        put_halves(sends[1], (n + 1) * rows, piece[...].astype(BF16))
+
+
+def second_half_moment_kernel(pb, order, send_order, n_kept, vectors, dense, half, before, message, *refs):
+    width, chunks = vectors.shape[2], half.shape[0]
+    kept, own, tile_out = refs[:n_kept], refs[n_kept], refs[-1]
+    sends = dict(zip(send_order, refs[n_kept + 1 : -1]))
+    count = own.shape[0]
+    rows = count * width // LANES
     sums = None
     for m in range(chunks):
         total = half[m] + dots(pb, order, vectors, dense, m, width)
-        if n_probes:
-            part = jnp.sum(probes[m][...] * total, axis=1, keepdims=True)
-            sums = part if sums is None else sums + part
+        if m % 2:
+            probes = get_halves(message, m // 2 * rows, count, width).astype(F32)
+        else:
+            probes = kept[m // 2][...].astype(F32)
+        part = jnp.sum(probes * total, axis=1, keepdims=True)
+        sums = part if sums is None else sums + part
         if m == 0:
             own[...] = total
         else:
-            sends[m - 1][pl.ds(0, total.shape[0]), :] = total.astype(BF16)[:, :LANES]
-            for s in range(1, width // LANES):
-                sends[m - 1][pl.ds(s * total.shape[0], total.shape[0]), :] = total.astype(BF16)[
-                    :, s * LANES : (s + 1) * LANES
-                ]
-    if n_probes:
-        tile_out = refs[chunks]
-        both = before[...][:2] + jnp.concatenate([jnp.zeros((1, LANES), F32), 2.0 * as_row(sums)], axis=0)
-        tile_out[...] = jnp.concatenate([both, jnp.zeros((6, LANES), F32)], axis=0)
-        high, low = two_parts(both)
-        tile = jnp.concatenate([high, low, jnp.zeros((12, LANES), F32)], axis=0).astype(BF16)
-        for m in range(1, chunks):
-            sends[m - 1][pl.ds(width // LANES * own.shape[0], 16), :] = tile
+            put_halves(sends[m], 0, total.astype(BF16))
+    both = before[...][:2] + jnp.concatenate([jnp.zeros((1, LANES), F32), 2.0 * as_row(sums)], axis=0)
+    tile_out[...] = jnp.concatenate([both, jnp.zeros((6, LANES), F32)], axis=0)
+    high, low = two_parts(both)
+    tile = jnp.concatenate([high, low, jnp.zeros((12, LANES), F32)], axis=0).astype(BF16)
+    for send in sends.values():
+        send[pl.ds(rows, 16), :] = tile
+
+
+def cast_kernel(t_cur, probes, rounded_probes, *refs):
+    *outs, held, sems = refs
+    copies = [pltpu.make_async_copy(x, held.at[n], sems.at[n]) for n, x in enumerate((t_cur, probes))]
+    for copy in copies:
+        copy.start()
+    copies[0].wait()
+    for out in outs:
+        out[...] = held[0].astype(BF16)
+    copies[1].wait()
+    rounded_probes[...] = held[1].astype(BF16)
 
 
 def gathered(own, received):
     count, width = own.shape
     total = own[...]
     for r in received:
-        piece = jnp.concatenate(
-            [r[pl.ds(s * count, count), :] for s in range(width // LANES)], axis=1
-        )
-        total = total + piece.astype(F32)
+        total = total + get_halves(r, 0, count, width).astype(F32)
     return total
 
 
-def next_kernel(n_col, own, *refs):
-    received, (prev, cur, probes, rounded, tile) = refs[: n_col - 1], refs[n_col - 1 :]
+def next_kernel(n_col, with_probes, own, *refs):
+    received, (prev, cur, probes, tile, handed, *outs) = refs[: n_col - 1], refs[n_col - 1 :]
+    handed[...] = received[with_probes][pl.ds(own.shape[0] * own.shape[1] // LANES, handed.shape[0]), :]
     value = 2.0 * gathered(own, received) - prev[...]
-    rounded[...] = value.astype(BF16)
+    for out in outs:
+        out[...] = value.astype(BF16)
     ahead = as_row(jnp.sum(probes[...] * value, axis=1, keepdims=True))
     back = as_row(jnp.sum(probes[...] * cur[...], axis=1, keepdims=True))
     tile[...] = jnp.concatenate([ahead, -back, jnp.zeros((6, LANES), F32)], axis=0)
@@ -133,13 +170,14 @@
     out[...] = 2.0 * gathered(own, received) - prev[...]
 
 
-def tile_kernel(start, mine, *refs):
-    received, tile = refs[:-1], refs[-1]
+def tile_kernel(start, n_received, mine, *refs):
+    received, outs = refs[:n_received], refs[n_received:]
     total = mine[...]
     for r in received:
         t = r[pl.ds(start, 16), :].astype(F32)
         total = total + jnp.concatenate([t[0:2] + t[2:4], jnp.zeros((6, LANES), F32)], axis=0)
-    tile[...] = total
+    for out in outs:
+        out[...] = total
 
 
 def last_kernel(n_col, coeffs, own, *refs):
@@ -197,55 +235,73 @@
     )(block_count, *(in_hbm(x) for x in (block_rows, block_cols, blocks)))
 
     far = list(range(n_row - 2, 0, -2))
+    if n_row == 8:
+        far = FAR
+    n_out = len(far) + 1
     mine_order = [0] + [k ^ 1 for k in far]
     others_order = [1] + far
 
-    def gather(v):
-        got = [swap(v, "row", k ^ 1) for k in far]
-        head, tail = jnp.stack([v] + got[:-1]), got[-1][None]
-        return head, tail
-
-    send_rows = width // LANES * count
-
-    def halves(head, tail, dense, extra, name):
+    def gather(v, *copies):
+        got = [swap(copy, "row", k ^ 1) for copy, k in zip(copies, far)]
+        return jnp.stack([v] + got[:-1]), got[-1][None]
+
+    rows = width // LANES * count
+
+    def halves(head, tail, kernel, send_order, carried, extra_rows, tail_shapes, name):
         other = [swap(head, "row", 1), swap(tail, "row", 1)]
-        mine = jnp.concatenate([head, tail])
         half = call(
             functools.partial(first_half_kernel, pb, mine_order),
             shape(n_col, count, width),
             [VMEM] * 2,
             name + "_a",
-        )(mine, dense)
-        others = jnp.concatenate(other)
-        n_probes = n_col if extra else 0
+        )(jnp.concatenate([head, tail]), dense)
         outs = [shape(count, width)]
-        outs += [shape(send_rows + (16 if extra else 0), LANES, dtype=BF16)] * (n_col - 1)
-        if extra:
-            outs.append(shape(8, LANES))
+        outs += [shape(rows + extra_rows.get(m, 0), LANES, dtype=BF16) for m in send_order] + tail_shapes
         return call(
-            functools.partial(second_half_kernel, pb, others_order, n_probes),
+            functools.partial(kernel, pb, others_order, send_order),
             outs,
-            [VMEM] * (3 + (1 + n_probes if extra else 0)),
+            [VMEM] * (3 + len(carried)),
             name + "_b",
-        )(others, dense, half, *(extra or []))
-
-    reduce_order = [2, 1, 3] if n_col == 4 else list(range(1, n_col))
-
-    def exchange(sends):
-        got = {m: swap(sends[m - 1], "col", m) for m in reduce_order}
-        return [got[m] for m in reduce_order]
-
-    head, tail = gather(barrier(t_cur.astype(BF16)))
-    probe_pieces = {0: probes}
-    stages = [n_col >> (i + 1) for i in range(n_col.bit_length() - 1)]
-    k = stages[0]
-    probe_pieces[k] = swap(probes, "col", k)
+        )(jnp.concatenate(other), dense, half, *carried)
+
+    first_order = second_order = list(range(1, n_col))
+    if n_col == 4:
+        first_order, second_order = ORDER1, ORDER2
+
+    def exchange(sends, order):
+        return [swap(send, "col", m) for m, send in zip(order, sends)]
+
+    rounded_probes, *v = call(
+        cast_kernel,
+        [shape(count, width, dtype=BF16)] * (1 + n_out),
+        [HBM] * 2,
+        "cast",
+        scratch_shapes=[pltpu.VMEM((2, count, width), F32), pltpu.SemaphoreType.DMA((2,))],
+    )(in_hbm(t_cur), in_hbm(probes))
+    head, tail = gather(*v)
+    kept = {0: rounded_probes}
+    k = n_col // 2
+    while k > 1:
+        for m in list(kept):
+            kept[m ^ k] = swap(kept[m], "col", k)
+        k //= 2
+    kept = [kept[m] for m in range(0, n_col, 2)]
     head, tail, dense = barrier((head, tail, dense))
-    own, *sends = halves(head, tail, dense, None, "first")
-    received = exchange(sends)
-    rounded, tile = call(
-        functools.partial(next_kernel, n_col),
-        [shape(count, width, dtype=BF16), shape(8, LANES)],
+    own, *sends = halves(
+        head,
+        tail,
+        lambda *a: second_half_kernel(*a[:3], len(kept), *a[3:]),
+        first_order,
+        kept,
+        {1: rows * len(kept)},
+        [],
+        "first",
+    )
+    received = exchange(sends, first_order)
+    tile, handed, *rounded = call(
+        functools.partial(next_kernel, n_col, first_order.index(1)),
+        [shape(8, LANES), shape(rows * len(kept), LANES, dtype=BF16)]
+        + [shape(count, width, dtype=BF16)] * n_out,
         [VMEM] * (n_col + 3),
         "next",
     )(own, *received, t_prev, t_cur, probes)
@@ -253,18 +309,21 @@
         functools.partial(value_kernel, n_col), shape(count, width), [VMEM] * (n_col + 1), "value"
     )(own, *received, t_prev)
 
-    head, tail = gather(rounded)
-    rounded, probe_pieces = barrier((rounded, probe_pieces))
-    for k in stages[1:]:
-        keys = list(probe_pieces)
-        got = swap(jnp.stack([probe_pieces[m] for m in keys]), "col", k)
-        for n, m in enumerate(keys):
-            probe_pieces[m ^ k] = got[n]
-    extra = [tile] + [probe_pieces[m] for m in range(n_col)]
-    own, *sends, mine = halves(head, tail, dense, extra, "second")
-    received = exchange(sends)
-    tile = call(
-        functools.partial(tile_kernel, send_rows), shape(8, LANES), [VMEM] * n_col, "sums"
+    head, tail = gather(*rounded)
+    head, tail, t_next = barrier((head, tail, t_next))
+    own, *sends, mine = halves(
+        head,
+        tail,
+        lambda *a: second_half_moment_kernel(*a[:3], len(kept), *a[3:]),
+        second_order,
+        [tile, handed, probes] + kept[1:],
+        dict.fromkeys(second_order, 16),
+        [shape(8, LANES)],
+        "second",
+    )
+    received = exchange(sends, second_order)
+    total, *tiles = call(
+        functools.partial(tile_kernel, rows, n_col - 1), [shape(8, LANES)] * n_out, [VMEM] * n_col, "sums"
     )(mine, *received)
     t_after, accum_out = call(
         functools.partial(last_kernel, n_col),
@@ -273,9 +332,10 @@
         "last",
     )(coeffs, own, *received, t_cur, t_next, accum)
 
-    total = tile
-    for k in far:
-        total = total + swap(tile, "row", k ^ 1)
+    got = [swap(tile, "row", k ^ 1) for tile, k in zip(tiles, far)]
+    got, t_after, accum_out = barrier((got, t_after, accum_out))
+    for one in got:
+        total = total + one
     total = total + swap(total, "row", 1)
     moments = total[:2, :count] * float(total_rows) ** (-0.5)
     return (t_next, t_after, accum_out, moments)

time: 49.7 us -> 44.2 us (0.89)
  waiting for transfers between devices: 16.4 us -> 11.7 us
  Pallas kernels: 7.15 us -> 8.08 us
  other arithmetic: 1.52 us -> 0.66 us
  local copies, waits for them, and re-layouts: 0.88 us -> 0.04 us
    ppermute x22 -> x21, waiting for transfers between devices: 16.4 us -> 11.7 us  [swap(): return lax.ppermute(x, axis, [(i, i ^ k) for i in range(n)])]
    pallas_call x4 -> x5, Pallas kernels: 1.76 us -> 2.65 us  [the longest x2 1.61 us: halves(): call(functools.partial(kernel, pb, others_order, send_order), outs, [VMEM...]
    convert_element_type x1 -> x0, other arithmetic: 0.85 us -> none  [local(): head, tail = gather(barrier(t_cur.astype(BF16)))]
    unnamed x12, local copies, waits for them, and re-layouts: 0.87 us -> 0.04 us
    ppermute x22 -> x21, starting transfers between devices: 22.1 us -> 21.9 us  [swap(): return lax.ppermute(x, axis, [(i, i ^ k) for i in range(n)])]
  transfers between devices with their start and end apart: 22 -> 21, of which waited for: 12 -> 10; matrix products, arithmetic and copies ran while one was open for 0% -> 0% of each run, Pallas kernels for 13% -> 12%
where the time goes in v2:
time: 44.2 us; the launch traced here: 43.9 us
  starting transfers between devices  21.9 us (50%)
  waiting for transfers between devices  11.7 us (26%)
  Pallas kernels  8.08 us (18%)
  between operations  1.48 us (3%)
  other arithmetic  0.66 us (1%)
    ppermute x21, starting transfers between devices, swap(): return lax.ppermute(x, axis, [(i, i ^ k) for i in range(n)])  21.9 us
    ppermute x21, waiting for transfers between devices, swap(): return lax.ppermute(x, axis, [(i, i ^ k) for i in range(n)])  11.7 us
    pallas_call x1, Pallas kernels, local(): call(functools.partial(place_kernel, pb, group), shape(n_row, pb, n_col *...  2.07 us
    pallas_call x2, Pallas kernels, halves(): call(functools.partial(kernel, pb, others_order, send_order), outs, [VMEM...  1.61 us
    pallas_call x2, Pallas kernels, halves(): call(functools.partial(first_half_kernel, pb, mine_order), shape(n_col, c...  1.49 us
    pallas_call x1, Pallas kernels, local(): call(functools.partial(last_kernel, n_col), [shape(count, width), shape(c...  1.22 us
    pallas_call x1, Pallas kernels, local(): call(cast_kernel, [shape(count, width, dtype=BF16)] * (1 + n_out), [HBM]...  0.9 us
  transfers between devices with their start and end apart: 21, of which 10 were waited for; matrix products, arithmetic and copies ran while one was open for 0% of the time, Pallas kernels for 12%

profile of v2, /device:TPU:0, one launch (start us, length us, event | category | flops | bytes accessed | tf_op | source)
XLA Modules:
  0.0 43.9 jit_solution(8513085095974736579)
XLA Ops:
  0.6 0.9 %cast.1 = (bf16[64,256]{1,0:T(8,128)(2,1)S(1)}, bf16[64,256]{1,0:T(8,128)(2,1)S(1)}, bf16[64,256]{1,0:T(8,128)(2,1)S(1)}, bf16[64,256]{1,0:T(8,128)(2,1)S(1)}, bf16[64,256]{1,0:T(8,128)(2,1)S(1)}) custom-call(f32[64,256]{1,0:T(8,128)} %refs_3_.5, f32[64,256]{1,0:T(8,128)} %a_5_.1), custom_call_target="tpu_custom_call" | custom-call | tf_op jit(solution)/shard_map/cast/pallas_call | solution.py:274
  1.5 3.4 %collective-permute-start = (bf16[64,256]{1,0:T(8,128)(2,1)S(1)}, bf16[64,256]{1,0:T(8,128)(2,1)S(1)}, u32[]{:S(2)}, u32[]{:S(2)}) collective-permute-start(bf16[64,256]{1,0:T(8,128)(2,1)S(1)} %get-tuple-element.42), channel_id=1, source_target_pairs={{0,28},{4,24},{8,20},{12,16},{16,12},{20,8},{24,4},{28,0},{1,29},{... | collective-permute-start | bytes 98312 | tf_op jit(solution)/shard_map/ppermute | solution.py:202
  4.9 0.8 %collective-permute-start.1 = (bf16[64,256]{1,0:T(8,128)(2,1)S(1)}, bf16[64,256]{1,0:T(8,128)(2,1)S(1)}, u32[]{:S(2)}, u32[]{:S(2)}) collective-permute-start(bf16[64,256]{1,0:T(8,128)(2,1)S(1)} %get-tuple-element.43), channel_id=1, source_target_pairs={{0,20},{4,16},{8,28},{12,24},{16,4},{20,0},{24,12},{28,8},{1,21},{... | collective-permute-start | bytes 98312 | tf_op jit(solution)/shard_map/ppermute | solution.py:202
  5.7 0.1 collective-permute-start.2
  5.9 2.6 %collective-permute-start.5 = (bf16[64,256]{1,0:T(8,128)(2,1)S(1)}, bf16[64,256]{1,0:T(8,128)(2,1)S(1)}, u32[]{:S(2)}, u32[]{:S(2)}) collective-permute-start(bf16[64,256]{1,0:T(8,128)(2,1)S(1)} %get-tuple-element.48.a_3_), channel_id=1, source_target_pairs={{0,2},{1,3},{2,0},{3,1},{4,6},{5,7},{6,4},{7,5},{8,10},{9,11},{10,... | collective-permute-start | bytes 98312 | tf_op jit(solution)/shard_map/ppermute | solution.py:202
  9.1 2.1 %place.1.dense.a_1_ = bf16[8,2,1024,128]{3,2,1,0:T(8,128)(2,1)S(1)} custom-call(s32[1,1]{1,0:T(1,128)S(6)} %copy.13.count, s32[1,1,64]{2,1,0:T(1,128)} %rows_in.1, s32[1,1,64]{2,1,0:T(1,128)} %cols_in.1, bf16[1,1,64,128,128]{4,3,2,1,0:T(8,128)(2,1)} %blocks.1), custom_call_target="tpu_custom_call" | custom-call | tf_op jit(solution)/shard_map/place/pallas_call | solution.py:223
  11.2 0.0 collective-permute-done
  11.2 0.0 collective-permute-done.1
  11.2 0.0 collective-permute-done.2
  11.2 0.1 collective-permute-start.4
  11.3 0.5 %collective-permute-start.3 = (bf16[3,64,256]{2,1,0:T(8,128)(2,1)S(1)}, bf16[3,64,256]{2,1,0:T(8,128)(2,1)S(1)}, u32[]{:S(2)}, u32[]{:S(2)}) collective-permute-start(bf16[3,64,256]{2,1,0:T(8,128)(2,1)S(1)} %pad_maximum_fusion.4), channel_id=1, source_target_pairs={{0,4},{4,0},{8,12},{12,8},{16,20},{20,16},{24,28},{28,24},{1,5},{5... | collective-permute-start | bytes 294920 | tf_op jit(solution)/shard_map/ppermute | solution.py:202
  11.8 0.0 copy-start
  11.8 0.0 copy-start.1
  11.8 0.0 copy-start.2
  11.9 0.7 %first_a.1.a_2_ = f32[4,64,256]{2,1,0:T(8,128)S(1)} custom-call(bf16[4,64,256]{2,1,0:T(8,128)(2,1)S(1)} %pad_maximum_fusion.1.vectors, bf16[8,2,1024,128]{3,2,1,0:T(8,128)(2,1)S(1)} %place.1.dense.a_1_), custom_call_target="tpu_custom_call" | custom-call | tf_op jit(solution)/shard_map/first_a/pallas_call | solution.py:252
  12.6 0.0 collective-permute-done.4
  12.6 0.1 collective-permute-done.3
  12.8 0.0 collective-permute-done.5.a_4_.a_6_
  12.8 0.8 %first_b.1 = (f32[64,256]{1,0:T(8,128)S(1)}, bf16[384,128]{1,0:T(8,128)(2,1)S(1)}, bf16[128,128]{1,0:T(8,128)(2,1)S(1)}, bf16[128,128]{1,0:T(8,128)(2,1)S(1)}) custom-call(bf16[4,64,256]{2,1,0:T(8,128)(2,1)S(1)} %pad_maximum_fusion.a_0_, bf16[8,2,1024,128]{3,2,1,0:T(8,128)(2,1)S(1)} %place.1.dense.a_1_, f32[4,64,256]{2,1,0:T(8,128)S(1)} %first_a.1.a_2_, ...), custom_call_target="tpu_custom_call" | custom-call | tf_op jit(solution)/shard_map/first_b/pallas_call | solution.py:260
  13.5 1.6 %collective-permute-start.6 = (bf16[384,128]{1,0:T(8,128)(2,1)S(1)}, bf16[384,128]{1,0:T(8,128)(2,1)S(1)}, u32[]{:S(2)}, u32[]{:S(2)}) collective-permute-start(bf16[384,128]{1,0:T(8,128)(2,1)S(1)} %get-tuple-element.50), channel_id=1, source_target_pairs={{0,1},{1,0},{2,3},{3,2},{4,5},{5,4},{6,7},{7,6},{8,9},{9,8},{10,11... | collective-permute-start | bytes 294920 | tf_op jit(solution)/shard_map/ppermute | solution.py:202
  15.1 0.6 %collective-permute-start.7 = (bf16[128,128]{1,0:T(8,128)(2,1)S(1)}, bf16[128,128]{1,0:T(8,128)(2,1)S(1)}, u32[]{:S(2)}, u32[]{:S(2)}) collective-permute-start(bf16[128,128]{1,0:T(8,128)(2,1)S(1)} %get-tuple-element.51), channel_id=1, source_target_pairs={{0,3},{1,2},{2,1},{3,0},{4,7},{5,6},{6,5},{7,4},{8,11},{9,10},{10,... | collective-permute-start | bytes 98312 | tf_op jit(solution)/shard_map/ppermute | solution.py:202
  15.7 1.4 %collective-permute-start.8 = (bf16[128,128]{1,0:T(8,128)(2,1)S(1)}, bf16[128,128]{1,0:T(8,128)(2,1)S(1)}, u32[]{:S(2)}, u32[]{:S(2)}) collective-permute-start(bf16[128,128]{1,0:T(8,128)(2,1)S(1)} %get-tuple-element.52), channel_id=1, source_target_pairs={{0,2},{1,3},{2,0},{3,1},{4,6},{5,7},{6,4},{7,5},{8,10},{9,11},{10,... | collective-permute-start | bytes 98312 | tf_op jit(solution)/shard_map/ppermute | solution.py:202
  17.1 3.8 %collective-permute-done.7.refs_1_ = bf16[128,128]{1,0:T(8,128)(2,1)S(1)} collective-permute-done((bf16[128,128]{1,0:T(8,128)(2,1)S(1)}, bf16[128,128]{1,0:T(8,128)(2,1)S(1)}, u32[]{:S(2)}, u32[]{:S(2)}) %collective-permute-start.7) | collective-permute-done | bytes 32800 | tf_op jit(solution)/shard_map/ppermute | solution.py:202
  20.9 0.0 collective-permute-done.8.refs_2_
  20.9 0.0 collective-permute-done.6.refs_0_
  20.9 0.0 copy-done
  20.9 0.0 copy-done.1
  20.9 0.0 copy-done.2
  20.9 0.1 next.1
  21.0 1.2 %collective-permute-start.9 = (bf16[64,256]{1,0:T(8,128)(2,1)S(1)}, bf16[64,256]{1,0:T(8,128)(2,1)S(1)}, u32[]{:S(2)}, u32[]{:S(2)}) collective-permute-start(bf16[64,256]{1,0:T(8,128)(2,1)S(1)} %get-tuple-element.54), channel_id=1, source_target_pairs={{0,28},{4,24},{8,20},{12,16},{16,12},{20,8},{24,4},{28,0},{1,29},{... | collective-permute-start | bytes 98312 | tf_op jit(solution)/shard_map/ppermute | solution.py:202
  22.2 1.9 %collective-permute-start.10 = (bf16[64,256]{1,0:T(8,128)(2,1)S(1)}, bf16[64,256]{1,0:T(8,128)(2,1)S(1)}, u32[]{:S(2)}, u32[]{:S(2)}) collective-permute-start(bf16[64,256]{1,0:T(8,128)(2,1)S(1)} %get-tuple-element.55), channel_id=1, source_target_pairs={{0,20},{4,16},{8,28},{12,24},{16,4},{20,0},{24,12},{28,8},{1,21},{... | collective-permute-start | bytes 98312 | tf_op jit(solution)/shard_map/ppermute | solution.py:202
  24.1 0.4 collective-permute-start.11
  24.5 0.7 %value.1.refs_4_ = f32[64,256]{1,0:T(8,128)} custom-call(f32[64,256]{1,0:T(8,128)S(1)} %get-tuple-element.49.own, bf16[384,128]{1,0:T(8,128)(2,1)S(1)} %collective-permute-done.6.refs_0_, bf16[128,128]{1,0:T(8,128)(2,1)S(1)} %collective-permute-done.7.refs_1_, bf16[128,128]{1,0:T(8,128)(2,1)S(1)} %collective-permute-done.8.refs_2_, f32[64,256]{1,0:T(8,128)S(1)} %copy-done.2), custom_call_target="tpu_custom_call" | custom-call | tf_op jit(solution)/shard_map/value/pallas_call | solution.py:308
  25.2 0.2 collective-permute-done.9
  25.3 0.4 collective-permute-done.10
  25.8 1.7 %collective-permute-done.11 = bf16[64,256]{1,0:T(8,128)(2,1)S(1)} collective-permute-done((bf16[64,256]{1,0:T(8,128)(2,1)S(1)}, bf16[64,256]{1,0:T(8,128)(2,1)S(1)}, u32[]{:S(2)}, u32[]{:S(2)}) %collective-permute-start.11) | collective-permute-done | bytes 32800 | tf_op jit(solution)/shard_map/ppermute | solution.py:202
  27.5 0.2 collective-permute-start.13
  27.7 0.3 collective-permute-start.12
  28.0 0.0 copy-start.3
  28.0 0.0 copy-start.4
  28.0 0.0 copy-start.5
  28.1 0.7 %second_a.1.a_2_ = f32[4,64,256]{2,1,0:T(8,128)S(1)} custom-call(bf16[4,64,256]{2,1,0:T(8,128)(2,1)S(1)} %pad_maximum_fusion.3.vectors, bf16[8,2,1024,128]{3,2,1,0:T(8,128)(2,1)S(1)} %place.1.dense.a_1_), custom_call_target="tpu_custom_call" | custom-call | tf_op jit(solution)/shard_map/second_a/pallas_call | solution.py:252
  28.8 0.0 collective-permute-done.13
  28.8 0.2 collective-permute-done.12
  29.0 0.8 %second_b.1 = (f32[64,256]{1,0:T(8,128)S(1)}, bf16[144,128]{1,0:T(8,128)(2,1)S(1)}, bf16[144,128]{1,0:T(8,128)(2,1)S(1)}, bf16[144,128]{1,0:T(8,128)(2,1)S(1)}, f32[8,128]{1,0:T(8,128)S(1)}) custom-call(bf16[4,64,256]{2,1,0:T(8,128)(2,1)S(1)} %pad_maximum_fusion.2.a_0_, bf16[8,2,1024,128]{3,2,1,0:T(8,128)(2,1)S(1)} %place.1.dense.a_1_, ...), custom_call_target="tpu_custom_call" | custom-call | tf_op jit(solution)/shard_map/second_b/pallas_call | solution.py:260
  29.9 1.3 %collective-permute-start.14 = (bf16[144,128]{1,0:T(8,128)(2,1)S(1)}, bf16[144,128]{1,0:T(8,128)(2,1)S(1)}, u32[]{:S(2)}, u32[]{:S(2)}) collective-permute-start(bf16[144,128]{1,0:T(8,128)(2,1)S(1)} %get-tuple-element.63), channel_id=1, source_target_pairs={{0,2},{1,3},{2,0},{3,1},{4,6},{5,7},{6,4},{7,5},{8,10},{9,11},{10,... | collective-permute-start | bytes 110600 | tf_op jit(solution)/shard_map/ppermute | solution.py:202
  31.2 1.5 %collective-permute-start.15 = (bf16[144,128]{1,0:T(8,128)(2,1)S(1)}, bf16[144,128]{1,0:T(8,128)(2,1)S(1)}, u32[]{:S(2)}, u32[]{:S(2)}) collective-permute-start(bf16[144,128]{1,0:T(8,128)(2,1)S(1)} %get-tuple-element.64), channel_id=1, source_target_pairs={{0,3},{1,2},{2,1},{3,0},{4,7},{5,6},{6,5},{7,4},{8,11},{9,10},{10,... | collective-permute-start | bytes 110600 | tf_op jit(solution)/shard_map/ppermute | solution.py:202
  32.7 0.7 %collective-permute-start.16 = (bf16[144,128]{1,0:T(8,128)(2,1)S(1)}, bf16[144,128]{1,0:T(8,128)(2,1)S(1)}, u32[]{:S(2)}, u32[]{:S(2)}) collective-permute-start(bf16[144,128]{1,0:T(8,128)(2,1)S(1)} %get-tuple-element.65), channel_id=1, source_target_pairs={{0,1},{1,0},{2,3},{3,2},{4,5},{5,4},{6,7},{7,6},{8,9},{9,8},{10,11... | collective-permute-start | bytes 110600 | tf_op jit(solution)/shard_map/ppermute | solution.py:202
  33.4 1.8 %collective-permute-done.14.refs_0_ = bf16[144,128]{1,0:T(8,128)(2,1)S(1)} collective-permute-done((bf16[144,128]{1,0:T(8,128)(2,1)S(1)}, bf16[144,128]{1,0:T(8,128)(2,1)S(1)}, u32[]{:S(2)}, u32[]{:S(2)}) %collective-permute-start.14) | collective-permute-done | bytes 36896 | tf_op jit(solution)/shard_map/ppermute | solution.py:202
  35.2 1.8 %collective-permute-done.15.refs_1_ = bf16[144,128]{1,0:T(8,128)(2,1)S(1)} collective-permute-done((bf16[144,128]{1,0:T(8,128)(2,1)S(1)}, bf16[144,128]{1,0:T(8,128)(2,1)S(1)}, u32[]{:S(2)}, u32[]{:S(2)}) %collective-permute-start.15) | collective-permute-done | bytes 36896 | tf_op jit(solution)/shard_map/ppermute | solution.py:202
  37.1 0.0 collective-permute-done.16.refs_2_
  37.1 0.1 collective-permute-start.17
  37.2 1.9 %collective-permute-start.18 = (f32[8,128]{1,0:T(8,128)S(1)}, f32[8,128]{1,0:T(8,128)S(1)}, u32[]{:S(2)}, u32[]{:S(2)}) collective-permute-start(f32[8,128]{1,0:T(8,128)S(1)} %get-tuple-element.67), channel_id=1, source_target_pairs={{0,20},{4,16},{8,28},{12,24},{16,4},{20,0},{24,12},{28,8},{1,21},{... | collective-permute-start | bytes 12296 | tf_op jit(solution)/shard_map/ppermute | solution.py:202
  39.1 1.1 %collective-permute-start.19 = (f32[8,128]{1,0:T(8,128)S(1)}, f32[8,128]{1,0:T(8,128)S(1)}, u32[]{:S(2)}, u32[]{:S(2)}) collective-permute-start(f32[8,128]{1,0:T(8,128)S(1)} %get-tuple-element.68), channel_id=1, source_target_pairs={{0,12},{4,8},{8,4},{12,0},{16,28},{20,24},{24,20},{28,16},{1,13},{... | collective-permute-start | bytes 12296 | tf_op jit(solution)/shard_map/ppermute | solution.py:202
  40.3 0.0 copy-done.3
  40.3 0.0 copy-done.4
  40.3 0.0 copy-done.5
  40.3 1.2 %last.1 = (f32[64,256]{1,0:T(8,128)}, f32[64,256]{1,0:T(8,128)}) custom-call(f32[2]{0:T(128)S(1)} %copy-done.5, f32[64,256]{1,0:T(8,128)S(1)} %get-tuple-element.69.own, bf16[144,128]{1,0:T(8,128)(2,1)S(1)} %collective-permute-done.14.refs_0_, bf16[144,128]{1,0:T(8,128)(2,1)S(1)} %collective-permute-done.15.refs_1_, ...), custom_call_target="tpu_custom_call" | custom-call | tf_op jit(solution)/shard_map/last/pallas_call | solution.py:328
  41.5 0.0 collective-permute-done.17
  41.5 0.0 collective-permute-done.18
  41.5 0.7 %collective-permute-done.19 = f32[8,128]{1,0:T(8,128)S(1)} collective-permute-done((f32[8,128]{1,0:T(8,128)S(1)}, f32[8,128]{1,0:T(8,128)S(1)}, u32[]{:S(2)}, u32[]{:S(2)}) %collective-permute-start.19) | collective-permute-done | bytes 4128 | tf_op jit(solution)/shard_map/ppermute | solution.py:202
  42.1 0.2 collective-permute-start.20
  42.3 1.0 %collective-permute-done.20 = f32[8,128]{1,0:T(8,128)S(1)} collective-permute-done((f32[8,128]{1,0:T(8,128)S(1)}, f32[8,128]{1,0:T(8,128)S(1)}, u32[]{:S(2)}, u32[]{:S(2)}) %collective-permute-start.20) | collective-permute-done | bytes 4128 | tf_op jit(solution)/shard_map/ppermute | solution.py:202
  43.3 0.6 %slice_multiply_fusion = f32[2,64]{1,0:T(2,128)} fusion(f32[8,128]{1,0:T(8,128)S(1)} %add.15), kind=kLoop, calls=%fused_computation.7 | loop fusion | flops 128 | bytes 1024 | tf_op jit(solution)/shard_map/mul | solution.py:340
  (9 shorter events, 0.1 us)
Async XLA Ops:
  1.5 9.6 %collective-permute-start = (bf16[64,256]{1,0:T(8,128)(2,1)S(1)}, bf16[64,256]{1,0:T(8,128)(2,1)S(1)}, u32[]{:S(2)}, u32[]{:S(2)}) collective-permute-start(bf16[64,256]{1,0:T(8,128)(2,1)S(1)} %get-tuple-element.42), channel_id=1, source_target_pairs={{0,28},{4,24},{8,20},{12,16},{16,12},{20,8},{24,4},{28,0},{1,29},{... | collective-permute-start | bytes 98312 | tf_op jit(solution)/shard_map/ppermute | solution.py:202
  4.9 6.3 %collective-permute-start.1 = (bf16[64,256]{1,0:T(8,128)(2,1)S(1)}, bf16[64,256]{1,0:T(8,128)(2,1)S(1)}, u32[]{:S(2)}, u32[]{:S(2)}) collective-permute-start(bf16[64,256]{1,0:T(8,128)(2,1)S(1)} %get-tuple-element.43), channel_id=1, source_target_pairs={{0,20},{4,16},{8,28},{12,24},{16,4},{20,0},{24,12},{28,8},{1,21},{... | collective-permute-start | bytes 98312 | tf_op jit(solution)/shard_map/ppermute | solution.py:202
  5.7 5.5 %collective-permute-start.2 = (bf16[64,256]{1,0:T(8,128)(2,1)S(1)}, bf16[64,256]{1,0:T(8,128)(2,1)S(1)}, u32[]{:S(2)}, u32[]{:S(2)}) collective-permute-start(bf16[64,256]{1,0:T(8,128)(2,1)S(1)} %get-tuple-element.44), channel_id=1, source_target_pairs={{0,12},{4,8},{8,4},{12,0},{16,28},{20,24},{24,20},{28,16},{1,13},{... | collective-permute-start | bytes 98312 | tf_op jit(solution)/shard_map/ppermute | solution.py:202
  5.9 6.9 %collective-permute-start.5 = (bf16[64,256]{1,0:T(8,128)(2,1)S(1)}, bf16[64,256]{1,0:T(8,128)(2,1)S(1)}, u32[]{:S(2)}, u32[]{:S(2)}) collective-permute-start(bf16[64,256]{1,0:T(8,128)(2,1)S(1)} %get-tuple-element.48.a_3_), channel_id=1, source_target_pairs={{0,2},{1,3},{2,0},{3,1},{4,6},{5,7},{6,4},{7,5},{8,10},{9,11},{10,... | collective-permute-start | bytes 98312 | tf_op jit(solution)/shard_map/ppermute | solution.py:202
  11.2 1.4 %collective-permute-start.4 = (bf16[1,64,256]{2,1,0:T(8,128)(2,1)S(1)}, bf16[1,64,256]{2,1,0:T(8,128)(2,1)S(1)}, u32[]{:S(2)}, u32[]{:S(2)}) collective-permute-start(bf16[1,64,256]{2,1,0:T(8,128)(2,1)S(1)} %bitcast.14), channel_id=1, source_target_pairs={{0,4},{4,0},{8,12},{12,8},{16,20},{20,16},{24,28},{28,24},{1,5},{5... | collective-permute-start | bytes 98312 | tf_op jit(solution)/shard_map/ppermute | solution.py:202
  11.3 1.4 %collective-permute-start.3 = (bf16[3,64,256]{2,1,0:T(8,128)(2,1)S(1)}, bf16[3,64,256]{2,1,0:T(8,128)(2,1)S(1)}, u32[]{:S(2)}, u32[]{:S(2)}) collective-permute-start(bf16[3,64,256]{2,1,0:T(8,128)(2,1)S(1)} %pad_maximum_fusion.4), channel_id=1, source_target_pairs={{0,4},{4,0},{8,12},{12,8},{16,20},{20,16},{24,28},{28,24},{1,5},{5... | collective-permute-start | bytes 294920 | tf_op jit(solution)/shard_map/ppermute | solution.py:202
  11.8 9.1 %copy-start = (f32[64,256]{1,0:T(8,128)S(1)}, f32[64,256]{1,0:T(8,128)}, u32[]{:S(2)}) copy-start(f32[64,256]{1,0:T(8,128)} %a_5_.1) | copy-start | bytes 196612
  11.8 9.1 %copy-start.1 = (f32[64,256]{1,0:T(8,128)S(1)}, f32[64,256]{1,0:T(8,128)}, u32[]{:S(2)}) copy-start(f32[64,256]{1,0:T(8,128)} %refs_3_.5) | copy-start | bytes 196612
  11.8 9.1 %copy-start.2 = (f32[64,256]{1,0:T(8,128)S(1)}, f32[64,256]{1,0:T(8,128)}, u32[]{:S(2)}) copy-start(f32[64,256]{1,0:T(8,128)} %refs_3_.4) | copy-start | bytes 196612
  13.5 7.3 %collective-permute-start.6 = (bf16[384,128]{1,0:T(8,128)(2,1)S(1)}, bf16[384,128]{1,0:T(8,128)(2,1)S(1)}, u32[]{:S(2)}, u32[]{:S(2)}) collective-permute-start(bf16[384,128]{1,0:T(8,128)(2,1)S(1)} %get-tuple-element.50), channel_id=1, source_target_pairs={{0,1},{1,0},{2,3},{3,2},{4,5},{5,4},{6,7},{7,6},{8,9},{9,8},{10,11... | collective-permute-start | bytes 294920 | tf_op jit(solution)/shard_map/ppermute | solution.py:202
  15.1 5.8 %collective-permute-start.7 = (bf16[128,128]{1,0:T(8,128)(2,1)S(1)}, bf16[128,128]{1,0:T(8,128)(2,1)S(1)}, u32[]{:S(2)}, u32[]{:S(2)}) collective-permute-start(bf16[128,128]{1,0:T(8,128)(2,1)S(1)} %get-tuple-element.51), channel_id=1, source_target_pairs={{0,3},{1,2},{2,1},{3,0},{4,7},{5,6},{6,5},{7,4},{8,11},{9,10},{10,... | collective-permute-start | bytes 98312 | tf_op jit(solution)/shard_map/ppermute | solution.py:202
  15.7 5.2 %collective-permute-start.8 = (bf16[128,128]{1,0:T(8,128)(2,1)S(1)}, bf16[128,128]{1,0:T(8,128)(2,1)S(1)}, u32[]{:S(2)}, u32[]{:S(2)}) collective-permute-start(bf16[128,128]{1,0:T(8,128)(2,1)S(1)} %get-tuple-element.52), channel_id=1, source_target_pairs={{0,2},{1,3},{2,0},{3,1},{4,6},{5,7},{6,4},{7,5},{8,10},{9,11},{10,... | collective-permute-start | bytes 98312 | tf_op jit(solution)/shard_map/ppermute | solution.py:202
  21.0 4.3 %collective-permute-start.9 = (bf16[64,256]{1,0:T(8,128)(2,1)S(1)}, bf16[64,256]{1,0:T(8,128)(2,1)S(1)}, u32[]{:S(2)}, u32[]{:S(2)}) collective-permute-start(bf16[64,256]{1,0:T(8,128)(2,1)S(1)} %get-tuple-element.54), channel_id=1, source_target_pairs={{0,28},{4,24},{8,20},{12,16},{16,12},{20,8},{24,4},{28,0},{1,29},{... | collective-permute-start | bytes 98312 | tf_op jit(solution)/shard_map/ppermute | solution.py:202
  22.2 3.5 %collective-permute-start.10 = (bf16[64,256]{1,0:T(8,128)(2,1)S(1)}, bf16[64,256]{1,0:T(8,128)(2,1)S(1)}, u32[]{:S(2)}, u32[]{:S(2)}) collective-permute-start(bf16[64,256]{1,0:T(8,128)(2,1)S(1)} %get-tuple-element.55), channel_id=1, source_target_pairs={{0,20},{4,16},{8,28},{12,24},{16,4},{20,0},{24,12},{28,8},{1,21},{... | collective-permute-start | bytes 98312 | tf_op jit(solution)/shard_map/ppermute | solution.py:202
  24.1 3.4 %collective-permute-start.11 = (bf16[64,256]{1,0:T(8,128)(2,1)S(1)}, bf16[64,256]{1,0:T(8,128)(2,1)S(1)}, u32[]{:S(2)}, u32[]{:S(2)}) collective-permute-start(bf16[64,256]{1,0:T(8,128)(2,1)S(1)} %get-tuple-element.56), channel_id=1, source_target_pairs={{0,12},{4,8},{8,4},{12,0},{16,28},{20,24},{24,20},{28,16},{1,13},{... | collective-permute-start | bytes 98312 | tf_op jit(solution)/shard_map/ppermute | solution.py:202
  27.5 1.3 %collective-permute-start.13 = (bf16[1,64,256]{2,1,0:T(8,128)(2,1)S(1)}, bf16[1,64,256]{2,1,0:T(8,128)(2,1)S(1)}, u32[]{:S(2)}, u32[]{:S(2)}) collective-permute-start(bf16[1,64,256]{2,1,0:T(8,128)(2,1)S(1)} %bitcast.16), channel_id=1, source_target_pairs={{0,4},{4,0},{8,12},{12,8},{16,20},{20,16},{24,28},{28,24},{1,5},{5... | collective-permute-start | bytes 98312 | tf_op jit(solution)/shard_map/ppermute | solution.py:202
  27.7 1.3 %collective-permute-start.12 = (bf16[3,64,256]{2,1,0:T(8,128)(2,1)S(1)}, bf16[3,64,256]{2,1,0:T(8,128)(2,1)S(1)}, u32[]{:S(2)}, u32[]{:S(2)}) collective-permute-start(bf16[3,64,256]{2,1,0:T(8,128)(2,1)S(1)} %pad_maximum_fusion.5), channel_id=1, source_target_pairs={{0,4},{4,0},{8,12},{12,8},{16,20},{20,16},{24,28},{28,24},{1,5},{5... | collective-permute-start | bytes 294920 | tf_op jit(solution)/shard_map/ppermute | solution.py:202
  28.0 12.2 %copy-start.3 = (f32[64,256]{1,0:T(8,128)S(1)}, f32[64,256]{1,0:T(8,128)}, u32[]{:S(2)}) copy-start(f32[64,256]{1,0:T(8,128)} %value.1.refs_4_) | copy-start | bytes 196612
  28.0 12.2 %copy-start.4 = (f32[64,256]{1,0:T(8,128)S(1)}, f32[64,256]{1,0:T(8,128)}, u32[]{:S(2)}) copy-start(f32[64,256]{1,0:T(8,128)} %refs_5_.3) | copy-start | bytes 196612
  28.0 12.2 %copy-start.5 = (f32[2]{0:T(128)S(1)}, f32[2]{0:T(128)}, u32[]{:S(2)}) copy-start(f32[2]{0:T(128)} %coeffs.1) | copy-start | bytes 28
  29.9 5.3 %collective-permute-start.14 = (bf16[144,128]{1,0:T(8,128)(2,1)S(1)}, bf16[144,128]{1,0:T(8,128)(2,1)S(1)}, u32[]{:S(2)}, u32[]{:S(2)}) collective-permute-start(bf16[144,128]{1,0:T(8,128)(2,1)S(1)} %get-tuple-element.63), channel_id=1, source_target_pairs={{0,2},{1,3},{2,0},{3,1},{4,6},{5,7},{6,4},{7,5},{8,10},{9,11},{10,... | collective-permute-start | bytes 110600 | tf_op jit(solution)/shard_map/ppermute | solution.py:202
  31.2 5.9 %collective-permute-start.15 = (bf16[144,128]{1,0:T(8,128)(2,1)S(1)}, bf16[144,128]{1,0:T(8,128)(2,1)S(1)}, u32[]{:S(2)}, u32[]{:S(2)}) collective-permute-start(bf16[144,128]{1,0:T(8,128)(2,1)S(1)} %get-tuple-element.64), channel_id=1, source_target_pairs={{0,3},{1,2},{2,1},{3,0},{4,7},{5,6},{6,5},{7,4},{8,11},{9,10},{10,... | collective-permute-start | bytes 110600 | tf_op jit(solution)/shard_map/ppermute | solution.py:202
  32.7 4.4 %collective-permute-start.16 = (bf16[144,128]{1,0:T(8,128)(2,1)S(1)}, bf16[144,128]{1,0:T(8,128)(2,1)S(1)}, u32[]{:S(2)}, u32[]{:S(2)}) collective-permute-start(bf16[144,128]{1,0:T(8,128)(2,1)S(1)} %get-tuple-element.65), channel_id=1, source_target_pairs={{0,1},{1,0},{2,3},{3,2},{4,5},{5,4},{6,7},{7,6},{8,9},{9,8},{10,11... | collective-permute-start | bytes 110600 | tf_op jit(solution)/shard_map/ppermute | solution.py:202
  37.1 4.4 %collective-permute-start.17 = (f32[8,128]{1,0:T(8,128)S(1)}, f32[8,128]{1,0:T(8,128)S(1)}, u32[]{:S(2)}, u32[]{:S(2)}) collective-permute-start(f32[8,128]{1,0:T(8,128)S(1)} %get-tuple-element.66), channel_id=1, source_target_pairs={{0,28},{4,24},{8,20},{12,16},{16,12},{20,8},{24,4},{28,0},{1,29},{... | collective-permute-start | bytes 12296 | tf_op jit(solution)/shard_map/ppermute | solution.py:202
  37.2 4.3 %collective-permute-start.18 = (f32[8,128]{1,0:T(8,128)S(1)}, f32[8,128]{1,0:T(8,128)S(1)}, u32[]{:S(2)}, u32[]{:S(2)}) collective-permute-start(f32[8,128]{1,0:T(8,128)S(1)} %get-tuple-element.67), channel_id=1, source_target_pairs={{0,20},{4,16},{8,28},{12,24},{16,4},{20,0},{24,12},{28,8},{1,21},{... | collective-permute-start | bytes 12296 | tf_op jit(solution)/shard_map/ppermute | solution.py:202
  39.1 3.0 %collective-permute-start.19 = (f32[8,128]{1,0:T(8,128)S(1)}, f32[8,128]{1,0:T(8,128)S(1)}, u32[]{:S(2)}, u32[]{:S(2)}) collective-permute-start(f32[8,128]{1,0:T(8,128)S(1)} %get-tuple-element.68), channel_id=1, source_target_pairs={{0,12},{4,8},{8,4},{12,0},{16,28},{20,24},{24,20},{28,16},{1,13},{... | collective-permute-start | bytes 12296 | tf_op jit(solution)/shard_map/ppermute | solution.py:202
  42.1 1.2 %collective-permute-start.20 = (f32[8,128]{1,0:T(8,128)S(1)}, f32[8,128]{1,0:T(8,128)S(1)}, u32[]{:S(2)}, u32[]{:S(2)}) collective-permute-start(f32[8,128]{1,0:T(8,128)S(1)} %add_add_fusion), channel_id=1, source_target_pairs={{0,4},{4,0},{8,12},{12,8},{16,20},{20,16},{24,28},{28,24},{1,5},{5... | collective-permute-start | bytes 12296 | tf_op jit(solution)/shard_map/ppermute | solution.py:202

commit v3 on v2

--- a/solution.py
+++ b/solution.py
@@ -13,9 +13,9 @@
 CONTRACT_LAST = (((1,), (1,)), ((), ()))
 F32, BF16 = jnp.float32, jnp.bfloat16
 LANES = 128
-ORDER1 = [1, 3, 2]
+ORDER1 = [3, 2, 1]
 ORDER2 = [2, 3, 1]
-FAR = [6, 4, 2]
+FAR_A, FAR_C, FAR_M = [6, 4, 2], [4, 2, 6], [6, 4, 2]
 
 
 def place_kernel(pb, group, count, rows_in, cols_in, blocks, dense, held, rows, cols, sems, own_sems):
@@ -62,10 +62,16 @@
     return total
 
 
-def first_half_kernel(pb, order, vectors, dense, out):
+def start_kernel(pb, order, vectors, dense, out):
     width = vectors.shape[2]
     for m in range(out.shape[0]):
         out[m] = dots(pb, order, vectors, dense, m, width)
+
+
+def more_kernel(pb, order, vectors, dense, before, out):
+    width = vectors.shape[2]
+    for m in range(out.shape[0]):
+        out[m] = before[m] + dots(pb, order, vectors, dense, m, width)
 
 
 def as_row(column):
@@ -92,22 +98,17 @@
     )
 
 
-def second_half_kernel(pb, order, send_order, n_carried, vectors, dense, half, *refs):
-    width, chunks = vectors.shape[2], half.shape[0]
-    carried, own = refs[:n_carried], refs[n_carried]
-    sends = dict(zip(send_order, refs[n_carried + 1 :]))
-    for m in range(chunks):
-        total = half[m] + dots(pb, order, vectors, dense, m, width)
+def end_kernel(pb, order, send_order, vectors, dense, before, own, *refs):
+    width, sends = vectors.shape[2], dict(zip(send_order, refs))
+    for m in range(before.shape[0]):
+        total = before[m] + dots(pb, order, vectors, dense, m, width)
         if m == 0:
             own[...] = total
         else:
             put_halves(sends[m], 0, total.astype(BF16))
-    rows = own.shape[0] * width // LANES
-    for n, piece in enumerate(carried):
-        put_halves(sends[1], (n + 1) * rows, piece[...].astype(BF16))
-
-
-def second_half_moment_kernel(pb, order, send_order, n_kept, vectors, dense, half, before, message, *refs):
+
+
+def end_moment_kernel(pb, order, send_order, n_kept, vectors, dense, half, before, handed, *refs):
     width, chunks = vectors.shape[2], half.shape[0]
     kept, own, tile_out = refs[:n_kept], refs[n_kept], refs[-1]
     sends = dict(zip(send_order, refs[n_kept + 1 : -1]))
@@ -116,10 +117,7 @@
     sums = None
     for m in range(chunks):
         total = half[m] + dots(pb, order, vectors, dense, m, width)
-        if m % 2:
-            probes = get_halves(message, m // 2 * rows, count, width).astype(F32)
-        else:
-            probes = kept[m // 2][...].astype(F32)
+        probes = (handed[m - n_kept] if m >= n_kept else kept[m][...]).astype(F32)
         part = jnp.sum(probes * total, axis=1, keepdims=True)
         sums = part if sums is None else sums + part
         if m == 0:
@@ -154,9 +152,8 @@
     return total
 
 
-def next_kernel(n_col, with_probes, own, *refs):
-    received, (prev, cur, probes, tile, handed, *outs) = refs[: n_col - 1], refs[n_col - 1 :]
-    handed[...] = received[with_probes][pl.ds(own.shape[0] * own.shape[1] // LANES, handed.shape[0]), :]
+def next_kernel(n_col, own, *refs):
+    received, (prev, cur, probes, tile, *outs) = refs[: n_col - 1], refs[n_col - 1 :]
     value = 2.0 * gathered(own, received) - prev[...]
     for out in outs:
         out[...] = value.astype(BF16)
@@ -235,34 +232,35 @@
     )(block_count, *(in_hbm(x) for x in (block_rows, block_cols, blocks)))
 
     far = list(range(n_row - 2, 0, -2))
-    if n_row == 8:
-        far = FAR
+    orders = [FAR_A, FAR_C, FAR_M] if n_row == 8 else [far] * 3
     n_out = len(far) + 1
-    mine_order = [0] + [k ^ 1 for k in far]
-    others_order = [1] + far
-
-    def gather(v, *copies):
+    def gather(far, v, *copies):
         got = [swap(copy, "row", k ^ 1) for copy, k in zip(copies, far)]
         return jnp.stack([v] + got[:-1]), got[-1][None]
 
     rows = width // LANES * count
 
-    def halves(head, tail, kernel, send_order, carried, extra_rows, tail_shapes, name):
-        other = [swap(head, "row", 1), swap(tail, "row", 1)]
-        half = call(
-            functools.partial(first_half_kernel, pb, mine_order),
-            shape(n_col, count, width),
-            [VMEM] * 2,
-            name + "_a",
+    def multiply(early, far, head, tail, kernel, send_order, carried, extra_rows, tail_shapes, name):
+        mine_order, others_order = [0] + [k ^ 1 for k in far], [1] + far
+        other_head, other_tail = swap(head, "row", 1), swap(tail, "row", 1)
+        sums = shape(n_col, count, width)
+        most = call(
+            functools.partial(start_kernel, pb, mine_order), sums, [VMEM] * 2, name + "_start"
         )(jnp.concatenate([head, tail]), dense)
+        last_order, others = others_order, jnp.concatenate([other_head, other_tail])
+        if early:
+            most = call(
+                functools.partial(more_kernel, pb, others_order[:-1]), sums, [VMEM] * 3, name + "_more"
+            )(other_head, dense, most)
+            last_order, others = others_order[-1:], other_tail
         outs = [shape(count, width)]
         outs += [shape(rows + extra_rows.get(m, 0), LANES, dtype=BF16) for m in send_order] + tail_shapes
         return call(
-            functools.partial(kernel, pb, others_order, send_order),
+            functools.partial(kernel, pb, last_order, send_order),
             outs,
             [VMEM] * (3 + len(carried)),
-            name + "_b",
-        )(jnp.concatenate(other), dense, half, *carried)
+            name + "_end",
+        )(others, dense, most, *carried)
 
     first_order = second_order = list(range(1, n_col))
     if n_col == 4:
@@ -278,30 +276,30 @@
         "cast",
         scratch_shapes=[pltpu.VMEM((2, count, width), F32), pltpu.SemaphoreType.DMA((2,))],
     )(in_hbm(t_cur), in_hbm(probes))
-    head, tail = gather(*v)
-    kept = {0: rounded_probes}
-    k = n_col // 2
-    while k > 1:
-        for m in list(kept):
-            kept[m ^ k] = swap(kept[m], "col", k)
-        k //= 2
-    kept = [kept[m] for m in range(0, n_col, 2)]
-    head, tail, dense = barrier((head, tail, dense))
-    own, *sends = halves(
+    head, tail = gather(orders[0], *v)
+    kept, k = [rounded_probes], 1
+    while 2 * k < n_col:
+        kept += [swap(piece, "col", k) for piece in kept]
+        k *= 2
+    tail, dense = barrier((tail, dense))
+    own, *sends = multiply(
+        True,
+        orders[0],
         head,
         tail,
-        lambda *a: second_half_kernel(*a[:3], len(kept), *a[3:]),
+        end_kernel,
         first_order,
-        kept,
-        {1: rows * len(kept)},
+        [],
+        {},
         [],
         "first",
     )
+    sends, kept = barrier((sends, kept))
+    handed = swap(jnp.stack(kept), "col", k)
     received = exchange(sends, first_order)
-    tile, handed, *rounded = call(
-        functools.partial(next_kernel, n_col, first_order.index(1)),
-        [shape(8, LANES), shape(rows * len(kept), LANES, dtype=BF16)]
-        + [shape(count, width, dtype=BF16)] * n_out,
+    tile, *rounded = call(
+        functools.partial(next_kernel, n_col),
+        [shape(8, LANES)] + [shape(count, width, dtype=BF16)] * n_out,
         [VMEM] * (n_col + 3),
         "next",
     )(own, *received, t_prev, t_cur, probes)
@@ -309,12 +307,14 @@
         functools.partial(value_kernel, n_col), shape(count, width), [VMEM] * (n_col + 1), "value"
     )(own, *received, t_prev)
 
-    head, tail = gather(*rounded)
-    head, tail, t_next = barrier((head, tail, t_next))
-    own, *sends, mine = halves(
+    head, tail = gather(orders[1], *rounded)
+    tail, t_next, handed = barrier((tail, t_next, handed))
+    own, *sends, mine = multiply(
+        False,
+        orders[1],
         head,
         tail,
-        lambda *a: second_half_moment_kernel(*a[:3], len(kept), *a[3:]),
+        lambda *a: end_moment_kernel(*a[:3], len(kept), *a[3:]),
         second_order,
         [tile, handed, probes] + kept[1:],
         dict.fromkeys(second_order, 16),
@@ -332,7 +332,7 @@
         "last",
     )(coeffs, own, *received, t_cur, t_next, accum)
 
-    got = [swap(tile, "row", k ^ 1) for tile, k in zip(tiles, far)]
+    got = [swap(tile, "row", k ^ 1) for tile, k in zip(tiles, orders[2])]
     got, t_after, accum_out = barrier((got, t_after, accum_out))
     for one in got:
         total = total + one

time: 44.2 us -> 43.4 us (0.982)
  waiting for transfers between devices: 11.7 us -> 8.9 us
  starting transfers between devices: 21.9 us -> 24.1 us
    ppermute x21 -> x22, waiting for transfers between devices: 11.7 us -> 8.9 us  [swap(): return lax.ppermute(x, axis, [(i, i ^ k) for i in range(n)])]
    ppermute x21 -> x22, starting transfers between devices: 21.9 us -> 24.1 us  [swap(): return lax.ppermute(x, axis, [(i, i ^ k) for i in range(n)])]
    pallas_call x5 -> x6, Pallas kernels: 3.23 us -> 3.36 us  [the longest x2 1.5 us: multiply(): call(functools.partial(start_kernel, pb, mine_order), sums, [VMEM] * 2, n...]
  transfers between devices with their start and end apart: 21 -> 22, of which waited for: 10 -> 11; matrix products, arithmetic and copies ran while one was open for 0% -> 0% of each run, Pallas kernels for 12% -> 15%
where the time goes in v3:
time: 43.4 us; the launch traced here: 43.1 us
  starting transfers between devices  24.1 us (56%)
  waiting for transfers between devices  8.9 us (21%)
  Pallas kernels  8.03 us (19%)
  between operations  1.47 us (3%)
  other arithmetic  0.66 us (2%)
    ppermute x22, starting transfers between devices, swap(): return lax.ppermute(x, axis, [(i, i ^ k) for i in range(n)])  24.1 us
    ppermute x22, waiting for transfers between devices, swap(): return lax.ppermute(x, axis, [(i, i ^ k) for i in range(n)])  8.9 us
    pallas_call x1, Pallas kernels, local(): call(functools.partial(place_kernel, pb, group), shape(n_row, pb, n_col *...  1.9 us
    pallas_call x2, Pallas kernels, multiply(): call(functools.partial(start_kernel, pb, mine_order), sums, [VMEM] * 2, n...  1.5 us
    pallas_call x1, Pallas kernels, local(): call(functools.partial(last_kernel, n_col), [shape(count, width), shape(c...  1.22 us
    pallas_call x2, Pallas kernels, multiply(): call(functools.partial(kernel, pb, last_order, send_order), outs, [VMEM]...  1.14 us
    pallas_call x1, Pallas kernels, local(): call(cast_kernel, [shape(count, width, dtype=BF16)] * (1 + n_out), [HBM]...  0.9 us
  transfers between devices with their start and end apart: 22, of which 11 were waited for; matrix products, arithmetic and copies ran while one was open for 0% of the time, Pallas kernels for 15%

profile of v3, /device:TPU:0, one launch (start us, length us, event | category | flops | bytes accessed | tf_op | source)
XLA Modules:
  0.0 43.1 jit_solution(17834484646967360141)
XLA Ops:
  0.6 0.9 %cast.1 = (bf16[64,256]{1,0:T(8,128)(2,1)S(1)}, bf16[64,256]{1,0:T(8,128)(2,1)S(1)}, bf16[64,256]{1,0:T(8,128)(2,1)S(1)}, bf16[64,256]{1,0:T(8,128)(2,1)S(1)}, bf16[64,256]{1,0:T(8,128)(2,1)S(1)}) custom-call(f32[64,256]{1,0:T(8,128)} %refs_3_.5, f32[64,256]{1,0:T(8,128)} %a_5_.1), custom_call_target="tpu_custom_call" | custom-call | tf_op jit(solution)/shard_map/cast/pallas_call | solution.py:272
  1.5 3.4 %collective-permute-start.2 = (bf16[64,256]{1,0:T(8,128)(2,1)S(1)}, bf16[64,256]{1,0:T(8,128)(2,1)S(1)}, u32[]{:S(2)}, u32[]{:S(2)}) collective-permute-start(bf16[64,256]{1,0:T(8,128)(2,1)S(1)} %get-tuple-element.48), channel_id=1, source_target_pairs={{0,28},{4,24},{8,20},{12,16},{16,12},{20,8},{24,4},{28,0},{1,29},{... | collective-permute-start | bytes 98312 | tf_op jit(solution)/shard_map/ppermute | solution.py:199
  4.9 0.8 %collective-permute-start.3 = (bf16[64,256]{1,0:T(8,128)(2,1)S(1)}, bf16[64,256]{1,0:T(8,128)(2,1)S(1)}, u32[]{:S(2)}, u32[]{:S(2)}) collective-permute-start(bf16[64,256]{1,0:T(8,128)(2,1)S(1)} %get-tuple-element.49), channel_id=1, source_target_pairs={{0,20},{4,16},{8,28},{12,24},{16,4},{20,0},{24,12},{28,8},{1,21},{... | collective-permute-start | bytes 98312 | tf_op jit(solution)/shard_map/ppermute | solution.py:199
  5.7 0.1 collective-permute-start
  5.9 1.6 %collective-permute-start.5 = (bf16[64,256]{1,0:T(8,128)(2,1)S(1)}, bf16[64,256]{1,0:T(8,128)(2,1)S(1)}, u32[]{:S(2)}, u32[]{:S(2)}) collective-permute-start(bf16[64,256]{1,0:T(8,128)(2,1)S(1)} %get-tuple-element.59), channel_id=1, source_target_pairs={{0,1},{1,0},{2,3},{3,2},{4,5},{5,4},{6,7},{7,6},{8,9},{9,8},{10,11... | collective-permute-start | bytes 98312 | tf_op jit(solution)/shard_map/ppermute | solution.py:199
  8.1 1.9 %place.1.dense.a_1_ = bf16[8,2,1024,128]{3,2,1,0:T(8,128)(2,1)S(1)} custom-call(s32[1,1]{1,0:T(1,128)S(6)} %copy.13.count, s32[1,1,64]{2,1,0:T(1,128)} %rows_in.1, s32[1,1,64]{2,1,0:T(1,128)} %cols_in.1, bf16[1,1,64,128,128]{4,3,2,1,0:T(8,128)(2,1)} %blocks.1), custom_call_target="tpu_custom_call" | custom-call | tf_op jit(solution)/shard_map/place/pallas_call | solution.py:220
  10.0 0.0 collective-permute-done.2
  10.0 0.0 collective-permute-done.3
  10.0 0.1 collective-permute-start.4
  10.1 0.0 collective-permute-done
  10.1 0.5 %collective-permute-start.1 = (bf16[1,64,256]{2,1,0:T(8,128)(2,1)S(1)}, bf16[1,64,256]{2,1,0:T(8,128)(2,1)S(1)}, u32[]{:S(2)}, u32[]{:S(2)}) collective-permute-start(bf16[1,64,256]{2,1,0:T(8,128)(2,1)S(1)} %bitcast.26), channel_id=1, source_target_pairs={{0,4},{4,0},{8,12},{12,8},{16,20},{20,16},{24,28},{28,24},{1,5},{5... | collective-permute-start | bytes 98312 | tf_op jit(solution)/shard_map/ppermute | solution.py:199
  10.6 0.8 %first_start.1.before = f32[4,64,256]{2,1,0:T(8,128)S(1)} custom-call(bf16[4,64,256]{2,1,0:T(8,128)(2,1)S(1)} %pad_maximum_fusion.vectors, bf16[8,2,1024,128]{3,2,1,0:T(8,128)(2,1)S(1)} %place.1.dense.a_1_), custom_call_target="tpu_custom_call" | custom-call | tf_op jit(solution)/shard_map/first_start/pallas_call | solution.py:247
  11.4 0.0 copy-start
  11.4 0.0 copy-start.1
  11.4 0.0 copy-start.2
  11.4 0.0 collective-permute-done.4.vectors
  11.4 0.6 %first_more.1.before = f32[4,64,256]{2,1,0:T(8,128)S(1)} custom-call(bf16[3,64,256]{2,1,0:T(8,128)(2,1)S(1)} %collective-permute-done.4.vectors, bf16[8,2,1024,128]{3,2,1,0:T(8,128)(2,1)S(1)} %place.1.dense.a_1_, f32[4,64,256]{2,1,0:T(8,128)S(1)} %first_start.1.before), custom_call_target="tpu_custom_call" | custom-call | tf_op jit(solution)/shard_map/first_more/pallas_call | solution.py:252
  12.0 0.0 collective-permute-done.1.vectors
  12.0 0.3 first_end.1
  12.3 0.0 collective-permute-done.5.a_6_
  12.3 2.6 %collective-permute-start.6 = (bf16[128,128]{1,0:T(8,128)(2,1)S(1)}, bf16[128,128]{1,0:T(8,128)(2,1)S(1)}, u32[]{:S(2)}, u32[]{:S(2)}) collective-permute-start(bf16[128,128]{1,0:T(8,128)(2,1)S(1)} %get-tuple-element.55), channel_id=1, source_target_pairs={{0,3},{1,2},{2,1},{3,0},{4,7},{5,6},{6,5},{7,4},{8,11},{9,10},{10,... | collective-permute-start | bytes 98312 | tf_op jit(solution)/shard_map/ppermute | solution.py:199
  14.9 0.6 %collective-permute-start.7 = (bf16[128,128]{1,0:T(8,128)(2,1)S(1)}, bf16[128,128]{1,0:T(8,128)(2,1)S(1)}, u32[]{:S(2)}, u32[]{:S(2)}) collective-permute-start(bf16[128,128]{1,0:T(8,128)(2,1)S(1)} %get-tuple-element.56), channel_id=1, source_target_pairs={{0,2},{1,3},{2,0},{3,1},{4,6},{5,7},{6,4},{7,5},{8,10},{9,11},{10,... | collective-permute-start | bytes 98312 | tf_op jit(solution)/shard_map/ppermute | solution.py:199
  15.5 1.3 %collective-permute-start.8 = (bf16[128,128]{1,0:T(8,128)(2,1)S(1)}, bf16[128,128]{1,0:T(8,128)(2,1)S(1)}, u32[]{:S(2)}, u32[]{:S(2)}) collective-permute-start(bf16[128,128]{1,0:T(8,128)(2,1)S(1)} %get-tuple-element.57), channel_id=1, source_target_pairs={{0,1},{1,0},{2,3},{3,2},{4,5},{5,4},{6,7},{7,6},{8,9},{9,8},{10,11... | collective-permute-start | bytes 98312 | tf_op jit(solution)/shard_map/ppermute | solution.py:199
  16.8 2.2 %collective-permute-start.10 = (bf16[2,64,256]{2,1,0:T(8,128)(2,1)S(1)}, bf16[2,64,256]{2,1,0:T(8,128)(2,1)S(1)}, u32[]{:S(2)}, u32[]{:S(2)}) collective-permute-start(bf16[2,64,256]{2,1,0:T(8,128)(2,1)S(1)} %pad_maximum_fusion.5), channel_id=1, source_target_pairs={{0,2},{1,3},{2,0},{3,1},{4,6},{5,7},{6,4},{7,5},{8,10},{9,11},{10,... | collective-permute-start | bytes 196616 | tf_op jit(solution)/shard_map/ppermute | solution.py:199
  19.0 0.0 collective-permute-done.6.refs_0_
  19.0 0.9 %collective-permute-done.7.refs_1_ = bf16[128,128]{1,0:T(8,128)(2,1)S(1)} collective-permute-done((bf16[128,128]{1,0:T(8,128)(2,1)S(1)}, bf16[128,128]{1,0:T(8,128)(2,1)S(1)}, u32[]{:S(2)}, u32[]{:S(2)}) %collective-permute-start.7) | collective-permute-done | bytes 32800 | tf_op jit(solution)/shard_map/ppermute | solution.py:199
  19.8 0.0 collective-permute-done.8.refs_2_
  19.8 0.0 copy-done
  19.9 0.0 copy-done.2
  19.9 0.1 next.1
  20.0 1.3 %collective-permute-start.9 = (bf16[64,256]{1,0:T(8,128)(2,1)S(1)}, bf16[64,256]{1,0:T(8,128)(2,1)S(1)}, u32[]{:S(2)}, u32[]{:S(2)}) collective-permute-start(bf16[64,256]{1,0:T(8,128)(2,1)S(1)} %get-tuple-element.58), channel_id=1, source_target_pairs={{0,28},{4,24},{8,20},{12,16},{16,12},{20,8},{24,4},{28,0},{1,29},{... | collective-permute-start | bytes 98312 | tf_op jit(solution)/shard_map/ppermute | solution.py:199
  21.3 1.5 %collective-permute-start.11 = (bf16[64,256]{1,0:T(8,128)(2,1)S(1)}, bf16[64,256]{1,0:T(8,128)(2,1)S(1)}, u32[]{:S(2)}, u32[]{:S(2)}) collective-permute-start(bf16[64,256]{1,0:T(8,128)(2,1)S(1)} %get-tuple-element.63), channel_id=1, source_target_pairs={{0,20},{4,16},{8,28},{12,24},{16,4},{20,0},{24,12},{28,8},{1,21},{... | collective-permute-start | bytes 98312 | tf_op jit(solution)/shard_map/ppermute | solution.py:199
  22.8 0.5 %collective-permute-start.12 = (bf16[64,256]{1,0:T(8,128)(2,1)S(1)}, bf16[64,256]{1,0:T(8,128)(2,1)S(1)}, u32[]{:S(2)}, u32[]{:S(2)}) collective-permute-start(bf16[64,256]{1,0:T(8,128)(2,1)S(1)} %get-tuple-element.64), channel_id=1, source_target_pairs={{0,12},{4,8},{8,4},{12,0},{16,28},{20,24},{24,20},{28,16},{1,13},{... | collective-permute-start | bytes 98312 | tf_op jit(solution)/shard_map/ppermute | solution.py:199
  23.3 0.7 %value.1.refs_4_ = f32[64,256]{1,0:T(8,128)} custom-call(f32[64,256]{1,0:T(8,128)S(1)} %get-tuple-element.50.own, bf16[128,128]{1,0:T(8,128)(2,1)S(1)} %collective-permute-done.6.refs_0_, bf16[128,128]{1,0:T(8,128)(2,1)S(1)} %collective-permute-done.7.refs_1_, bf16[128,128]{1,0:T(8,128)(2,1)S(1)} %collective-permute-done.8.refs_2_, f32[64,256]{1,0:T(8,128)S(1)} %copy-done.2), custom_call_target="tpu_custom_call" | custom-call | tf_op jit(solution)/shard_map/value/pallas_call | solution.py:306
  24.0 0.0 collective-permute-done.10.a_4_
  24.0 0.3 collective-permute-done.9
  24.3 0.5 %collective-permute-start.14 = (bf16[1,64,256]{2,1,0:T(8,128)(2,1)S(1)}, bf16[1,64,256]{2,1,0:T(8,128)(2,1)S(1)}, u32[]{:S(2)}, u32[]{:S(2)}) collective-permute-start(bf16[1,64,256]{2,1,0:T(8,128)(2,1)S(1)} %bitcast.24), channel_id=1, source_target_pairs={{0,4},{4,0},{8,12},{12,8},{16,20},{20,16},{24,28},{28,24},{1,5},{5... | collective-permute-start | bytes 98312 | tf_op jit(solution)/shard_map/ppermute | solution.py:199
  24.8 0.2 collective-permute-done.11
  25.0 1.2 %collective-permute-done.12 = bf16[64,256]{1,0:T(8,128)(2,1)S(1)} collective-permute-done((bf16[64,256]{1,0:T(8,128)(2,1)S(1)}, bf16[64,256]{1,0:T(8,128)(2,1)S(1)}, u32[]{:S(2)}, u32[]{:S(2)}) %collective-permute-start.12) | collective-permute-done | bytes 32800 | tf_op jit(solution)/shard_map/ppermute | solution.py:199
  26.2 0.3 collective-permute-start.13
  26.5 0.0 copy-start.3
  26.5 0.0 copy-start.4
  26.6 0.0 copy-start.5
  26.6 0.8 %second_start.1.a_2_ = f32[4,64,256]{2,1,0:T(8,128)S(1)} custom-call(bf16[4,64,256]{2,1,0:T(8,128)(2,1)S(1)} %pad_maximum_fusion.2.vectors, bf16[8,2,1024,128]{3,2,1,0:T(8,128)(2,1)S(1)} %place.1.dense.a_1_), custom_call_target="tpu_custom_call" | custom-call | tf_op jit(solution)/shard_map/second_start/pallas_call | solution.py:247
  27.3 0.0 collective-permute-done.14
  27.3 0.2 collective-permute-done.13
  27.6 0.9 %second_end.1 = (f32[64,256]{1,0:T(8,128)S(1)}, bf16[144,128]{1,0:T(8,128)(2,1)S(1)}, bf16[144,128]{1,0:T(8,128)(2,1)S(1)}, bf16[144,128]{1,0:T(8,128)(2,1)S(1)}, f32[8,128]{1,0:T(8,128)S(1)}) custom-call(bf16[4,64,256]{2,1,0:T(8,128)(2,1)S(1)} %pad_maximum_fusion.1.a_0_, bf16[8,2,1024,128]{3,2,1,0:T(8,128)(2,1)S(1)} %place.1.dense.a_1_, ...), custom_call_target="tpu_custom_call" | custom-call | tf_op jit(solution)/shard_map/second_end/pallas_call | solution.py:258
  28.4 1.7 %collective-permute-start.15 = (bf16[144,128]{1,0:T(8,128)(2,1)S(1)}, bf16[144,128]{1,0:T(8,128)(2,1)S(1)}, u32[]{:S(2)}, u32[]{:S(2)}) collective-permute-start(bf16[144,128]{1,0:T(8,128)(2,1)S(1)} %get-tuple-element.69), channel_id=1, source_target_pairs={{0,2},{1,3},{2,0},{3,1},{4,6},{5,7},{6,4},{7,5},{8,10},{9,11},{10,... | collective-permute-start | bytes 110600 | tf_op jit(solution)/shard_map/ppermute | solution.py:199
  30.1 2.1 %collective-permute-start.16 = (bf16[144,128]{1,0:T(8,128)(2,1)S(1)}, bf16[144,128]{1,0:T(8,128)(2,1)S(1)}, u32[]{:S(2)}, u32[]{:S(2)}) collective-permute-start(bf16[144,128]{1,0:T(8,128)(2,1)S(1)} %get-tuple-element.70), channel_id=1, source_target_pairs={{0,3},{1,2},{2,1},{3,0},{4,7},{5,6},{6,5},{7,4},{8,11},{9,10},{10,... | collective-permute-start | bytes 110600 | tf_op jit(solution)/shard_map/ppermute | solution.py:199
  32.3 0.0 collective-permute-start.17
  32.3 2.0 %collective-permute-done.15.refs_0_ = bf16[144,128]{1,0:T(8,128)(2,1)S(1)} collective-permute-done((bf16[144,128]{1,0:T(8,128)(2,1)S(1)}, bf16[144,128]{1,0:T(8,128)(2,1)S(1)}, u32[]{:S(2)}, u32[]{:S(2)}) %collective-permute-start.15) | collective-permute-done | bytes 36896 | tf_op jit(solution)/shard_map/ppermute | solution.py:199
  34.3 1.6 %collective-permute-done.16.refs_1_ = bf16[144,128]{1,0:T(8,128)(2,1)S(1)} collective-permute-done((bf16[144,128]{1,0:T(8,128)(2,1)S(1)}, bf16[144,128]{1,0:T(8,128)(2,1)S(1)}, u32[]{:S(2)}, u32[]{:S(2)}) %collective-permute-start.16) | collective-permute-done | bytes 36896 | tf_op jit(solution)/shard_map/ppermute | solution.py:199
  35.9 0.4 collective-permute-done.17.refs_2_
  36.3 0.1 collective-permute-start.18
  36.4 2.0 %collective-permute-start.19 = (f32[8,128]{1,0:T(8,128)S(1)}, f32[8,128]{1,0:T(8,128)S(1)}, u32[]{:S(2)}, u32[]{:S(2)}) collective-permute-start(f32[8,128]{1,0:T(8,128)S(1)} %get-tuple-element.73), channel_id=1, source_target_pairs={{0,20},{4,16},{8,28},{12,24},{16,4},{20,0},{24,12},{28,8},{1,21},{... | collective-permute-start | bytes 12296 | tf_op jit(solution)/shard_map/ppermute | solution.py:199
  38.4 0.6 %collective-permute-start.20 = (f32[8,128]{1,0:T(8,128)S(1)}, f32[8,128]{1,0:T(8,128)S(1)}, u32[]{:S(2)}, u32[]{:S(2)}) collective-permute-start(f32[8,128]{1,0:T(8,128)S(1)} %get-tuple-element.74), channel_id=1, source_target_pairs={{0,12},{4,8},{8,4},{12,0},{16,28},{20,24},{24,20},{28,16},{1,13},{... | collective-permute-start | bytes 12296 | tf_op jit(solution)/shard_map/ppermute | solution.py:199
  39.0 0.0 copy-done.4
  39.0 1.2 %last.1 = (f32[64,256]{1,0:T(8,128)}, f32[64,256]{1,0:T(8,128)}) custom-call(f32[2]{0:T(128)S(1)} %copy-done.5, f32[64,256]{1,0:T(8,128)S(1)} %get-tuple-element.75.own, bf16[144,128]{1,0:T(8,128)(2,1)S(1)} %collective-permute-done.15.refs_0_, bf16[144,128]{1,0:T(8,128)(2,1)S(1)} %collective-permute-done.16.refs_1_, ...), custom_call_target="tpu_custom_call" | custom-call | tf_op jit(solution)/shard_map/last/pallas_call | solution.py:328
  40.2 0.1 collective-permute-done.18
  40.3 0.0 collective-permute-done.19
  40.3 1.1 %collective-permute-done.20 = f32[8,128]{1,0:T(8,128)S(1)} collective-permute-done((f32[8,128]{1,0:T(8,128)S(1)}, f32[8,128]{1,0:T(8,128)S(1)}, u32[]{:S(2)}, u32[]{:S(2)}) %collective-permute-start.20) | collective-permute-done | bytes 4128 | tf_op jit(solution)/shard_map/ppermute | solution.py:199
  41.4 0.2 collective-permute-start.21
  41.6 1.0 %collective-permute-done.21 = f32[8,128]{1,0:T(8,128)S(1)} collective-permute-done((f32[8,128]{1,0:T(8,128)S(1)}, f32[8,128]{1,0:T(8,128)S(1)}, u32[]{:S(2)}, u32[]{:S(2)}) %collective-permute-start.21) | collective-permute-done | bytes 4128 | tf_op jit(solution)/shard_map/ppermute | solution.py:199
  42.6 0.6 %slice_multiply_fusion = f32[2,64]{1,0:T(2,128)} fusion(f32[8,128]{1,0:T(8,128)S(1)} %add.15), kind=kLoop, calls=%fused_computation.7 | loop fusion | flops 128 | bytes 1024 | tf_op jit(solution)/shard_map/mul | solution.py:340
  (12 shorter events, 0.1 us)
Async XLA Ops:
  1.5 8.5 %collective-permute-start.2 = (bf16[64,256]{1,0:T(8,128)(2,1)S(1)}, bf16[64,256]{1,0:T(8,128)(2,1)S(1)}, u32[]{:S(2)}, u32[]{:S(2)}) collective-permute-start(bf16[64,256]{1,0:T(8,128)(2,1)S(1)} %get-tuple-element.48), channel_id=1, source_target_pairs={{0,28},{4,24},{8,20},{12,16},{16,12},{20,8},{24,4},{28,0},{1,29},{... | collective-permute-start | bytes 98312 | tf_op jit(solution)/shard_map/ppermute | solution.py:199
  4.9 5.1 %collective-permute-start.3 = (bf16[64,256]{1,0:T(8,128)(2,1)S(1)}, bf16[64,256]{1,0:T(8,128)(2,1)S(1)}, u32[]{:S(2)}, u32[]{:S(2)}) collective-permute-start(bf16[64,256]{1,0:T(8,128)(2,1)S(1)} %get-tuple-element.49), channel_id=1, source_target_pairs={{0,20},{4,16},{8,28},{12,24},{16,4},{20,0},{24,12},{28,8},{1,21},{... | collective-permute-start | bytes 98312 | tf_op jit(solution)/shard_map/ppermute | solution.py:199
  5.7 4.4 %collective-permute-start = (bf16[64,256]{1,0:T(8,128)(2,1)S(1)}, bf16[64,256]{1,0:T(8,128)(2,1)S(1)}, u32[]{:S(2)}, u32[]{:S(2)}) collective-permute-start(bf16[64,256]{1,0:T(8,128)(2,1)S(1)} %get-tuple-element.44), channel_id=1, source_target_pairs={{0,12},{4,8},{8,4},{12,0},{16,28},{20,24},{24,20},{28,16},{1,13},{... | collective-permute-start | bytes 98312 | tf_op jit(solution)/shard_map/ppermute | solution.py:199
  5.9 6.5 %collective-permute-start.5 = (bf16[64,256]{1,0:T(8,128)(2,1)S(1)}, bf16[64,256]{1,0:T(8,128)(2,1)S(1)}, u32[]{:S(2)}, u32[]{:S(2)}) collective-permute-start(bf16[64,256]{1,0:T(8,128)(2,1)S(1)} %get-tuple-element.59), channel_id=1, source_target_pairs={{0,1},{1,0},{2,3},{3,2},{4,5},{5,4},{6,7},{7,6},{8,9},{9,8},{10,11... | collective-permute-start | bytes 98312 | tf_op jit(solution)/shard_map/ppermute | solution.py:199
  10.0 1.4 %collective-permute-start.4 = (bf16[3,64,256]{2,1,0:T(8,128)(2,1)S(1)}, bf16[3,64,256]{2,1,0:T(8,128)(2,1)S(1)}, u32[]{:S(2)}, u32[]{:S(2)}) collective-permute-start(bf16[3,64,256]{2,1,0:T(8,128)(2,1)S(1)} %pad_maximum_fusion.3), channel_id=1, source_target_pairs={{0,4},{4,0},{8,12},{12,8},{16,20},{20,16},{24,28},{28,24},{1,5},{5... | collective-permute-start | bytes 294920 | tf_op jit(solution)/shard_map/ppermute | solution.py:199
  10.1 1.9 %collective-permute-start.1 = (bf16[1,64,256]{2,1,0:T(8,128)(2,1)S(1)}, bf16[1,64,256]{2,1,0:T(8,128)(2,1)S(1)}, u32[]{:S(2)}, u32[]{:S(2)}) collective-permute-start(bf16[1,64,256]{2,1,0:T(8,128)(2,1)S(1)} %bitcast.26), channel_id=1, source_target_pairs={{0,4},{4,0},{8,12},{12,8},{16,20},{20,16},{24,28},{28,24},{1,5},{5... | collective-permute-start | bytes 98312 | tf_op jit(solution)/shard_map/ppermute | solution.py:199
  11.4 8.5 %copy-start = (f32[64,256]{1,0:T(8,128)S(1)}, f32[64,256]{1,0:T(8,128)}, u32[]{:S(2)}) copy-start(f32[64,256]{1,0:T(8,128)} %a_5_.1) | copy-start | bytes 196612
  11.4 8.5 %copy-start.1 = (f32[64,256]{1,0:T(8,128)S(1)}, f32[64,256]{1,0:T(8,128)}, u32[]{:S(2)}) copy-start(f32[64,256]{1,0:T(8,128)} %refs_3_.5) | copy-start | bytes 196612
  11.4 8.4 %copy-start.2 = (f32[64,256]{1,0:T(8,128)S(1)}, f32[64,256]{1,0:T(8,128)}, u32[]{:S(2)}) copy-start(f32[64,256]{1,0:T(8,128)} %refs_3_.4) | copy-start | bytes 196612
  12.3 6.6 %collective-permute-start.6 = (bf16[128,128]{1,0:T(8,128)(2,1)S(1)}, bf16[128,128]{1,0:T(8,128)(2,1)S(1)}, u32[]{:S(2)}, u32[]{:S(2)}) collective-permute-start(bf16[128,128]{1,0:T(8,128)(2,1)S(1)} %get-tuple-element.55), channel_id=1, source_target_pairs={{0,3},{1,2},{2,1},{3,0},{4,7},{5,6},{6,5},{7,4},{8,11},{9,10},{10,... | collective-permute-start | bytes 98312 | tf_op jit(solution)/shard_map/ppermute | solution.py:199
  14.9 4.9 %collective-permute-start.7 = (bf16[128,128]{1,0:T(8,128)(2,1)S(1)}, bf16[128,128]{1,0:T(8,128)(2,1)S(1)}, u32[]{:S(2)}, u32[]{:S(2)}) collective-permute-start(bf16[128,128]{1,0:T(8,128)(2,1)S(1)} %get-tuple-element.56), channel_id=1, source_target_pairs={{0,2},{1,3},{2,0},{3,1},{4,6},{5,7},{6,4},{7,5},{8,10},{9,11},{10,... | collective-permute-start | bytes 98312 | tf_op jit(solution)/shard_map/ppermute | solution.py:199
  15.5 4.3 %collective-permute-start.8 = (bf16[128,128]{1,0:T(8,128)(2,1)S(1)}, bf16[128,128]{1,0:T(8,128)(2,1)S(1)}, u32[]{:S(2)}, u32[]{:S(2)}) collective-permute-start(bf16[128,128]{1,0:T(8,128)(2,1)S(1)} %get-tuple-element.57), channel_id=1, source_target_pairs={{0,1},{1,0},{2,3},{3,2},{4,5},{5,4},{6,7},{7,6},{8,9},{9,8},{10,11... | collective-permute-start | bytes 98312 | tf_op jit(solution)/shard_map/ppermute | solution.py:199
  16.8 7.2 %collective-permute-start.10 = (bf16[2,64,256]{2,1,0:T(8,128)(2,1)S(1)}, bf16[2,64,256]{2,1,0:T(8,128)(2,1)S(1)}, u32[]{:S(2)}, u32[]{:S(2)}) collective-permute-start(bf16[2,64,256]{2,1,0:T(8,128)(2,1)S(1)} %pad_maximum_fusion.5), channel_id=1, source_target_pairs={{0,2},{1,3},{2,0},{3,1},{4,6},{5,7},{6,4},{7,5},{8,10},{9,11},{10,... | collective-permute-start | bytes 196616 | tf_op jit(solution)/shard_map/ppermute | solution.py:199
  20.0 4.3 %collective-permute-start.9 = (bf16[64,256]{1,0:T(8,128)(2,1)S(1)}, bf16[64,256]{1,0:T(8,128)(2,1)S(1)}, u32[]{:S(2)}, u32[]{:S(2)}) collective-permute-start(bf16[64,256]{1,0:T(8,128)(2,1)S(1)} %get-tuple-element.58), channel_id=1, source_target_pairs={{0,28},{4,24},{8,20},{12,16},{16,12},{20,8},{24,4},{28,0},{1,29},{... | collective-permute-start | bytes 98312 | tf_op jit(solution)/shard_map/ppermute | solution.py:199
  21.3 3.7 %collective-permute-start.11 = (bf16[64,256]{1,0:T(8,128)(2,1)S(1)}, bf16[64,256]{1,0:T(8,128)(2,1)S(1)}, u32[]{:S(2)}, u32[]{:S(2)}) collective-permute-start(bf16[64,256]{1,0:T(8,128)(2,1)S(1)} %get-tuple-element.63), channel_id=1, source_target_pairs={{0,20},{4,16},{8,28},{12,24},{16,4},{20,0},{24,12},{28,8},{1,21},{... | collective-permute-start | bytes 98312 | tf_op jit(solution)/shard_map/ppermute | solution.py:199
  22.8 3.3 %collective-permute-start.12 = (bf16[64,256]{1,0:T(8,128)(2,1)S(1)}, bf16[64,256]{1,0:T(8,128)(2,1)S(1)}, u32[]{:S(2)}, u32[]{:S(2)}) collective-permute-start(bf16[64,256]{1,0:T(8,128)(2,1)S(1)} %get-tuple-element.64), channel_id=1, source_target_pairs={{0,12},{4,8},{8,4},{12,0},{16,28},{20,24},{24,20},{28,16},{1,13},{... | collective-permute-start | bytes 98312 | tf_op jit(solution)/shard_map/ppermute | solution.py:199
  24.3 3.0 %collective-permute-start.14 = (bf16[1,64,256]{2,1,0:T(8,128)(2,1)S(1)}, bf16[1,64,256]{2,1,0:T(8,128)(2,1)S(1)}, u32[]{:S(2)}, u32[]{:S(2)}) collective-permute-start(bf16[1,64,256]{2,1,0:T(8,128)(2,1)S(1)} %bitcast.24), channel_id=1, source_target_pairs={{0,4},{4,0},{8,12},{12,8},{16,20},{20,16},{24,28},{28,24},{1,5},{5... | collective-permute-start | bytes 98312 | tf_op jit(solution)/shard_map/ppermute | solution.py:199
  26.2 1.4 %collective-permute-start.13 = (bf16[3,64,256]{2,1,0:T(8,128)(2,1)S(1)}, bf16[3,64,256]{2,1,0:T(8,128)(2,1)S(1)}, u32[]{:S(2)}, u32[]{:S(2)}) collective-permute-start(bf16[3,64,256]{2,1,0:T(8,128)(2,1)S(1)} %pad_maximum_fusion.4), channel_id=1, source_target_pairs={{0,4},{4,0},{8,12},{12,8},{16,20},{20,16},{24,28},{28,24},{1,5},{5... | collective-permute-start | bytes 294920 | tf_op jit(solution)/shard_map/ppermute | solution.py:199
  26.5 12.5 %copy-start.3 = (f32[64,256]{1,0:T(8,128)S(1)}, f32[64,256]{1,0:T(8,128)}, u32[]{:S(2)}) copy-start(f32[64,256]{1,0:T(8,128)} %value.1.refs_4_) | copy-start | bytes 196612
  26.5 12.5 %copy-start.4 = (f32[64,256]{1,0:T(8,128)S(1)}, f32[64,256]{1,0:T(8,128)}, u32[]{:S(2)}) copy-start(f32[64,256]{1,0:T(8,128)} %refs_5_.3) | copy-start | bytes 196612
  26.6 12.5 %copy-start.5 = (f32[2]{0:T(128)S(1)}, f32[2]{0:T(128)}, u32[]{:S(2)}) copy-start(f32[2]{0:T(128)} %coeffs.1) | copy-start | bytes 28
  28.4 5.9 %collective-permute-start.15 = (bf16[144,128]{1,0:T(8,128)(2,1)S(1)}, bf16[144,128]{1,0:T(8,128)(2,1)S(1)}, u32[]{:S(2)}, u32[]{:S(2)}) collective-permute-start(bf16[144,128]{1,0:T(8,128)(2,1)S(1)} %get-tuple-element.69), channel_id=1, source_target_pairs={{0,2},{1,3},{2,0},{3,1},{4,6},{5,7},{6,4},{7,5},{8,10},{9,11},{10,... | collective-permute-start | bytes 110600 | tf_op jit(solution)/shard_map/ppermute | solution.py:199
  30.1 5.8 %collective-permute-start.16 = (bf16[144,128]{1,0:T(8,128)(2,1)S(1)}, bf16[144,128]{1,0:T(8,128)(2,1)S(1)}, u32[]{:S(2)}, u32[]{:S(2)}) collective-permute-start(bf16[144,128]{1,0:T(8,128)(2,1)S(1)} %get-tuple-element.70), channel_id=1, source_target_pairs={{0,3},{1,2},{2,1},{3,0},{4,7},{5,6},{6,5},{7,4},{8,11},{9,10},{10,... | collective-permute-start | bytes 110600 | tf_op jit(solution)/shard_map/ppermute | solution.py:199
  32.3 4.0 %collective-permute-start.17 = (bf16[144,128]{1,0:T(8,128)(2,1)S(1)}, bf16[144,128]{1,0:T(8,128)(2,1)S(1)}, u32[]{:S(2)}, u32[]{:S(2)}) collective-permute-start(bf16[144,128]{1,0:T(8,128)(2,1)S(1)} %get-tuple-element.71), channel_id=1, source_target_pairs={{0,1},{1,0},{2,3},{3,2},{4,5},{5,4},{6,7},{7,6},{8,9},{9,8},{10,11... | collective-permute-start | bytes 110600 | tf_op jit(solution)/shard_map/ppermute | solution.py:199
  36.3 4.0 %collective-permute-start.18 = (f32[8,128]{1,0:T(8,128)S(1)}, f32[8,128]{1,0:T(8,128)S(1)}, u32[]{:S(2)}, u32[]{:S(2)}) collective-permute-start(f32[8,128]{1,0:T(8,128)S(1)} %get-tuple-element.72), channel_id=1, source_target_pairs={{0,28},{4,24},{8,20},{12,16},{16,12},{20,8},{24,4},{28,0},{1,29},{... | collective-permute-start | bytes 12296 | tf_op jit(solution)/shard_map/ppermute | solution.py:199
  36.4 3.9 %collective-permute-start.19 = (f32[8,128]{1,0:T(8,128)S(1)}, f32[8,128]{1,0:T(8,128)S(1)}, u32[]{:S(2)}, u32[]{:S(2)}) collective-permute-start(f32[8,128]{1,0:T(8,128)S(1)} %get-tuple-element.73), channel_id=1, source_target_pairs={{0,20},{4,16},{8,28},{12,24},{16,4},{20,0},{24,12},{28,8},{1,21},{... | collective-permute-start | bytes 12296 | tf_op jit(solution)/shard_map/ppermute | solution.py:199
  38.4 3.0 %collective-permute-start.20 = (f32[8,128]{1,0:T(8,128)S(1)}, f32[8,128]{1,0:T(8,128)S(1)}, u32[]{:S(2)}, u32[]{:S(2)}) collective-permute-start(f32[8,128]{1,0:T(8,128)S(1)} %get-tuple-element.74), channel_id=1, source_target_pairs={{0,12},{4,8},{8,4},{12,0},{16,28},{20,24},{24,20},{28,16},{1,13},{... | collective-permute-start | bytes 12296 | tf_op jit(solution)/shard_map/ppermute | solution.py:199
  41.4 1.2 %collective-permute-start.21 = (f32[8,128]{1,0:T(8,128)S(1)}, f32[8,128]{1,0:T(8,128)S(1)}, u32[]{:S(2)}, u32[]{:S(2)}) collective-permute-start(f32[8,128]{1,0:T(8,128)S(1)} %add_add_fusion), channel_id=1, source_target_pairs={{0,4},{4,0},{8,12},{12,8},{16,20},{20,16},{24,28},{28,24},{1,5},{5... | collective-permute-start | bytes 12296 | tf_op jit(solution)/shard_map/ppermute | solution.py:199

commit v4 on v3

--- a/solution.py
+++ b/solution.py
@@ -15,7 +15,7 @@
 LANES = 128
 ORDER1 = [3, 2, 1]
 ORDER2 = [2, 3, 1]
-FAR_A, FAR_C, FAR_M = [6, 4, 2], [4, 2, 6], [6, 4, 2]
+FAR_A, FAR_C, FAR_M = [6, 4, 2], [6, 4, 2], [6, 4, 2]
 
 
 def place_kernel(pb, group, count, rows_in, cols_in, blocks, dense, held, rows, cols, sems, own_sems):
@@ -43,9 +43,8 @@
     def put(slot):
         @pl.when(slot < live)
         def _():
-            i, j = rows[0, 0, slot], cols[0, 0, slot]
-            line = ((i // pb) ^ c) * pb + i % pb
-            dense[(j // pb) ^ r, j % pb, pl.ds(pl.multiple_of(line * bs, bs), bs), :] = held[slot]
+            column, line = cols[0, 0, slot] ^ (r * pb), rows[0, 0, slot] ^ (c * pb)
+            dense[column, pl.ds(pl.multiple_of(line * bs, bs), bs), :] = held[slot]
 
     for g in range(groups):
         fetch(g).wait()
@@ -56,7 +55,7 @@
 def dots(pb, order, vectors, dense, m, width):
     total = None
     for h, k in enumerate(order):
-        w = jnp.concatenate([dense[k, s, pl.ds(m * width, width), :] for s in range(pb)], axis=1)
+        w = jnp.concatenate([dense[k * pb + s, pl.ds(m * width, width), :] for s in range(pb)], axis=1)
         part = lax.dot_general(vectors[h], w, CONTRACT_LAST, preferred_element_type=F32)
         total = part if total is None else total + part
     return total
@@ -219,7 +218,7 @@
     group = 8
     dense = call(
         functools.partial(place_kernel, pb, group),
-        shape(n_row, pb, n_col * width, bs, dtype=BF16),
+        shape(n_row * pb, n_col * width, bs, dtype=BF16),
         [SMEM] + [HBM] * 3,
         "place",
         scratch_shapes=[
@@ -235,32 +234,34 @@
     orders = [FAR_A, FAR_C, FAR_M] if n_row == 8 else [far] * 3
     n_out = len(far) + 1
     def gather(far, v, *copies):
-        got = [swap(copy, "row", k ^ 1) for copy, k in zip(copies, far)]
-        return jnp.stack([v] + got[:-1]), got[-1][None]
+        return [v] + [swap(copy, "row", k ^ 1) for copy, k in zip(copies, far)]
 
     rows = width // LANES * count
 
-    def multiply(early, far, head, tail, kernel, send_order, carried, extra_rows, tail_shapes, name):
-        mine_order, others_order = [0] + [k ^ 1 for k in far], [1] + far
-        other_head, other_tail = swap(head, "row", 1), swap(tail, "row", 1)
-        sums = shape(n_col, count, width)
+    def multiply(split, early, late, order, kernel, send_order, carried, extra_rows, tail_shapes, name):
+        other_early, other_late = swap(early, "row", 1), swap(late, "row", 1)
+        sums, others_order = shape(n_col, count, width), [k ^ 1 for k in order]
+        n_early = early.shape[0]
+        first, second = (early, jnp.concatenate([late, other_early])) if split else (jnp.concatenate([early, late]), other_early)
+        n_first = first.shape[0]
+        both = order + others_order
         most = call(
-            functools.partial(start_kernel, pb, mine_order), sums, [VMEM] * 2, name + "_start"
-        )(jnp.concatenate([head, tail]), dense)
-        last_order, others = others_order, jnp.concatenate([other_head, other_tail])
-        if early:
-            most = call(
-                functools.partial(more_kernel, pb, others_order[:-1]), sums, [VMEM] * 3, name + "_more"
-            )(other_head, dense, most)
-            last_order, others = others_order[-1:], other_tail
+            functools.partial(start_kernel, pb, both[:n_first]), sums, [VMEM] * 2, name + "_start"
+        )(first, dense)
+        most = call(
+            functools.partial(more_kernel, pb, both[n_first : len(order) + n_early]),
+            sums,
+            [VMEM] * 3,
+            name + "_more",
+        )(second, dense, most)
         outs = [shape(count, width)]
         outs += [shape(rows + extra_rows.get(m, 0), LANES, dtype=BF16) for m in send_order] + tail_shapes
         return call(
-            functools.partial(kernel, pb, last_order, send_order),
+            functools.partial(kernel, pb, others_order[n_early:], send_order),
             outs,
             [VMEM] * (3 + len(carried)),
             name + "_end",
-        )(others, dense, most, *carried)
+        )(other_late, dense, most, *carried)
 
     first_order = second_order = list(range(1, n_col))
     if n_col == 4:
@@ -276,17 +277,17 @@
         "cast",
         scratch_shapes=[pltpu.VMEM((2, count, width), F32), pltpu.SemaphoreType.DMA((2,))],
     )(in_hbm(t_cur), in_hbm(probes))
-    head, tail = gather(orders[0], *v)
+    got = gather(orders[0], *v)
     kept, k = [rounded_probes], 1
     while 2 * k < n_col:
         kept += [swap(piece, "col", k) for piece in kept]
         k *= 2
-    tail, dense = barrier((tail, dense))
+    got[-1], dense = barrier((got[-1], dense))
     own, *sends = multiply(
-        True,
-        orders[0],
-        head,
-        tail,
+        False,
+        jnp.stack(got[:-1]),
+        got[-1][None],
+        [0] + [k ^ 1 for k in orders[0]],
         end_kernel,
         first_order,
         [],
@@ -307,13 +308,13 @@
         functools.partial(value_kernel, n_col), shape(count, width), [VMEM] * (n_col + 1), "value"
     )(own, *received, t_prev)
 
-    head, tail = gather(orders[1], *rounded)
-    tail, t_next, handed = barrier((tail, t_next, handed))
+    got = gather(orders[1], *rounded)
+    got[1], t_next, handed = barrier((got[1], t_next, handed))
     own, *sends, mine = multiply(
-        False,
-        orders[1],
-        head,
-        tail,
+        True,
+        jnp.stack(got[:2]),
+        jnp.stack(got[2:]),
+        [0] + [k ^ 1 for k in orders[1]],
         lambda *a: end_moment_kernel(*a[:3], len(kept), *a[3:]),
         second_order,
         [tile, handed, probes] + kept[1:],

time: 43.4 us -> 42.6 us (0.982)
  starting transfers between devices: 24.1 us -> 21.8 us
  waiting for transfers between devices: 8.9 us -> 10.6 us
    ppermute x22, starting transfers between devices: 24.1 us -> 21.8 us  [swap(): return lax.ppermute(x, axis, [(i, i ^ k) for i in range(n)])]
    ppermute x22, waiting for transfers between devices: 8.9 us -> 10.6 us  [swap(): return lax.ppermute(x, axis, [(i, i ^ k) for i in range(n)])]
    pallas_call x6 -> x7, Pallas kernels: 5.14 us -> 4.96 us  [the longest x1 1.6 us: local(): call(functools.partial(place_kernel, pb, group), shape(n_row * pb, n_col...]
  transfers between devices with their start and end apart: 22 -> 22, of which waited for: 11 -> 8; matrix products, arithmetic and copies ran while one was open for 0% -> 0% of each run, Pallas kernels for 15% -> 15%
where the time goes in v4:
time: 42.6 us; the launch traced here: 42.4 us
  starting transfers between devices  21.8 us (51%)
  waiting for transfers between devices  10.6 us (25%)
  Pallas kernels  7.86 us (18%)
  between operations  1.49 us (3%)
  other arithmetic  0.65 us (2%)
    ppermute x22, starting transfers between devices, swap(): return lax.ppermute(x, axis, [(i, i ^ k) for i in range(n)])  21.8 us
    ppermute x22, waiting for transfers between devices, swap(): return lax.ppermute(x, axis, [(i, i ^ k) for i in range(n)])  10.6 us
    pallas_call x1, Pallas kernels, local(): call(functools.partial(place_kernel, pb, group), shape(n_row * pb, n_col...  1.6 us
    pallas_call x2, Pallas kernels, multiply(): call(functools.partial(more_kernel, pb, both[n_first:len(order) + n_early...  1.35 us
    pallas_call x1, Pallas kernels, local(): call(functools.partial(last_kernel, n_col), [shape(count, width), shape(c...  1.22 us
    pallas_call x2, Pallas kernels, multiply(): call(functools.partial(start_kernel, pb, both[:n_first]), sums, [VMEM] *...  1.18 us
    pallas_call x1, Pallas kernels, local(): call(cast_kernel, [shape(count, width, dtype=BF16)] * (1 + n_out), [HBM]...  0.9 us
  transfers between devices with their start and end apart: 22, of which 8 were waited for; matrix products, arithmetic and copies ran while one was open for 0% of the time, Pallas kernels for 15%

profile of v4, /device:TPU:0, one launch (start us, length us, event | category | flops | bytes accessed | tf_op | source)
XLA Modules:
  0.0 42.4 jit_solution(2273722974160965995)
XLA Ops:
  0.6 0.9 %cast.1 = (bf16[64,256]{1,0:T(8,128)(2,1)S(1)}, bf16[64,256]{1,0:T(8,128)(2,1)S(1)}, bf16[64,256]{1,0:T(8,128)(2,1)S(1)}, bf16[64,256]{1,0:T(8,128)(2,1)S(1)}, bf16[64,256]{1,0:T(8,128)(2,1)S(1)}) custom-call(f32[64,256]{1,0:T(8,128)} %refs_3_.5, f32[64,256]{1,0:T(8,128)} %a_5_.1), custom_call_target="tpu_custom_call" | custom-call | tf_op jit(solution)/shard_map/cast/pallas_call | solution.py:273
  1.5 3.4 %collective-permute-start.2 = (bf16[64,256]{1,0:T(8,128)(2,1)S(1)}, bf16[64,256]{1,0:T(8,128)(2,1)S(1)}, u32[]{:S(2)}, u32[]{:S(2)}) collective-permute-start(bf16[64,256]{1,0:T(8,128)(2,1)S(1)} %get-tuple-element.48), channel_id=1, source_target_pairs={{0,28},{4,24},{8,20},{12,16},{16,12},{20,8},{24,4},{28,0},{1,29},{... | collective-permute-start | bytes 98312 | tf_op jit(solution)/shard_map/ppermute | solution.py:198
  4.9 0.8 %collective-permute-start.3 = (bf16[64,256]{1,0:T(8,128)(2,1)S(1)}, bf16[64,256]{1,0:T(8,128)(2,1)S(1)}, u32[]{:S(2)}, u32[]{:S(2)}) collective-permute-start(bf16[64,256]{1,0:T(8,128)(2,1)S(1)} %get-tuple-element.49), channel_id=1, source_target_pairs={{0,20},{4,16},{8,28},{12,24},{16,4},{20,0},{24,12},{28,8},{1,21},{... | collective-permute-start | bytes 98312 | tf_op jit(solution)/shard_map/ppermute | solution.py:198
  5.7 0.1 collective-permute-start
  5.9 1.6 %collective-permute-start.5 = (bf16[64,256]{1,0:T(8,128)(2,1)S(1)}, bf16[64,256]{1,0:T(8,128)(2,1)S(1)}, u32[]{:S(2)}, u32[]{:S(2)}) collective-permute-start(bf16[64,256]{1,0:T(8,128)(2,1)S(1)} %get-tuple-element.59), channel_id=1, source_target_pairs={{0,1},{1,0},{2,3},{3,2},{4,5},{5,4},{6,7},{7,6},{8,9},{9,8},{10,11... | collective-permute-start | bytes 98312 | tf_op jit(solution)/shard_map/ppermute | solution.py:198
  8.1 1.6 %place.1.dense.a_1_ = bf16[16,1024,128]{2,1,0:T(8,128)(2,1)S(1)} custom-call(s32[1,1]{1,0:T(1,128)S(6)} %copy.13.count, s32[1,1,64]{2,1,0:T(1,128)} %rows_in.1, s32[1,1,64]{2,1,0:T(1,128)} %cols_in.1, bf16[1,1,64,128,128]{4,3,2,1,0:T(8,128)(2,1)} %blocks.1), custom_call_target="tpu_custom_call" | custom-call | tf_op jit(solution)/shard_map/place/pallas_call | solution.py:219
  9.7 0.0 collective-permute-done.2
  9.7 0.0 collective-permute-done.3
  9.7 0.3 collective-permute-start.4
  10.1 0.0 collective-permute-done
  10.1 0.3 collective-permute-start.1
  10.3 0.7 %first_start.1.before = f32[4,64,256]{2,1,0:T(8,128)S(1)} custom-call(bf16[4,64,256]{2,1,0:T(8,128)(2,1)S(1)} %pad_maximum_fusion.vectors, bf16[16,1024,128]{2,1,0:T(8,128)(2,1)S(1)} %place.1.dense.a_1_), custom_call_target="tpu_custom_call" | custom-call | tf_op jit(solution)/shard_map/first_start/pallas_call | solution.py:248
  11.1 0.0 copy-start
  11.1 0.0 copy-start.1
  11.1 0.0 copy-start.2
  11.1 0.0 collective-permute-done.4.vectors
  11.1 0.6 %first_more.1.before = f32[4,64,256]{2,1,0:T(8,128)S(1)} custom-call(bf16[3,64,256]{2,1,0:T(8,128)(2,1)S(1)} %collective-permute-done.4.vectors, bf16[16,1024,128]{2,1,0:T(8,128)(2,1)S(1)} %place.1.dense.a_1_, f32[4,64,256]{2,1,0:T(8,128)S(1)} %first_start.1.before), custom_call_target="tpu_custom_call" | custom-call | tf_op jit(solution)/shard_map/first_more/pallas_call | solution.py:251
  11.7 0.0 collective-permute-done.1.vectors
  11.7 0.3 first_end.1
  12.0 0.0 collective-permute-done.5.a_6_
  12.0 2.8 %collective-permute-start.6 = (bf16[128,128]{1,0:T(8,128)(2,1)S(1)}, bf16[128,128]{1,0:T(8,128)(2,1)S(1)}, u32[]{:S(2)}, u32[]{:S(2)}) collective-permute-start(bf16[128,128]{1,0:T(8,128)(2,1)S(1)} %get-tuple-element.55), channel_id=1, source_target_pairs={{0,3},{1,2},{2,1},{3,0},{4,7},{5,6},{6,5},{7,4},{8,11},{9,10},{10,... | collective-permute-start | bytes 98312 | tf_op jit(solution)/shard_map/ppermute | solution.py:198
  14.9 0.0 collective-permute-start.7
  14.9 1.6 %collective-permute-start.8 = (bf16[128,128]{1,0:T(8,128)(2,1)S(1)}, bf16[128,128]{1,0:T(8,128)(2,1)S(1)}, u32[]{:S(2)}, u32[]{:S(2)}) collective-permute-start(bf16[128,128]{1,0:T(8,128)(2,1)S(1)} %get-tuple-element.57), channel_id=1, source_target_pairs={{0,1},{1,0},{2,3},{3,2},{4,5},{5,4},{6,7},{7,6},{8,9},{9,8},{10,11... | collective-permute-start | bytes 98312 | tf_op jit(solution)/shard_map/ppermute | solution.py:198
  16.5 1.7 %collective-permute-start.10 = (bf16[2,64,256]{2,1,0:T(8,128)(2,1)S(1)}, bf16[2,64,256]{2,1,0:T(8,128)(2,1)S(1)}, u32[]{:S(2)}, u32[]{:S(2)}) collective-permute-start(bf16[2,64,256]{2,1,0:T(8,128)(2,1)S(1)} %pad_maximum_fusion.3), channel_id=1, source_target_pairs={{0,2},{1,3},{2,0},{3,1},{4,6},{5,7},{6,4},{7,5},{8,10},{9,11},{10,... | collective-permute-start | bytes 196616 | tf_op jit(solution)/shard_map/ppermute | solution.py:198
  18.2 0.0 collective-permute-done.6.refs_0_
  18.3 2.6 %collective-permute-done.7.refs_1_ = bf16[128,128]{1,0:T(8,128)(2,1)S(1)} collective-permute-done((bf16[128,128]{1,0:T(8,128)(2,1)S(1)}, bf16[128,128]{1,0:T(8,128)(2,1)S(1)}, u32[]{:S(2)}, u32[]{:S(2)}) %collective-permute-start.7) | collective-permute-done | bytes 32800 | tf_op jit(solution)/shard_map/ppermute | solution.py:198
  20.9 0.0 collective-permute-done.8.refs_2_
  20.9 0.0 copy-done.1
  20.9 0.1 next.1
  21.0 0.1 collective-permute-start.9
  21.1 1.4 %collective-permute-start.11 = (bf16[64,256]{1,0:T(8,128)(2,1)S(1)}, bf16[64,256]{1,0:T(8,128)(2,1)S(1)}, u32[]{:S(2)}, u32[]{:S(2)}) collective-permute-start(bf16[64,256]{1,0:T(8,128)(2,1)S(1)} %get-tuple-element.62), channel_id=1, source_target_pairs={{0,20},{4,16},{8,28},{12,24},{16,4},{20,0},{24,12},{28,8},{1,21},{... | collective-permute-start | bytes 98312 | tf_op jit(solution)/shard_map/ppermute | solution.py:198
  22.5 0.9 %collective-permute-start.12 = (bf16[64,256]{1,0:T(8,128)(2,1)S(1)}, bf16[64,256]{1,0:T(8,128)(2,1)S(1)}, u32[]{:S(2)}, u32[]{:S(2)}) collective-permute-start(bf16[64,256]{1,0:T(8,128)(2,1)S(1)} %get-tuple-element.63), channel_id=1, source_target_pairs={{0,12},{4,8},{8,4},{12,0},{16,28},{20,24},{24,20},{28,16},{1,13},{... | collective-permute-start | bytes 98312 | tf_op jit(solution)/shard_map/ppermute | solution.py:198
  23.4 0.7 %value.1.refs_4_ = f32[64,256]{1,0:T(8,128)} custom-call(f32[64,256]{1,0:T(8,128)S(1)} %get-tuple-element.50.own, bf16[128,128]{1,0:T(8,128)(2,1)S(1)} %collective-permute-done.6.refs_0_, bf16[128,128]{1,0:T(8,128)(2,1)S(1)} %collective-permute-done.7.refs_1_, bf16[128,128]{1,0:T(8,128)(2,1)S(1)} %collective-permute-done.8.refs_2_, f32[64,256]{1,0:T(8,128)S(1)} %copy-done.2), custom_call_target="tpu_custom_call" | custom-call | tf_op jit(solution)/shard_map/value/pallas_call | solution.py:307
  24.1 0.0 collective-permute-done.10.a_4_
  24.1 1.2 %collective-permute-done.9 = bf16[64,256]{1,0:T(8,128)(2,1)S(1)} collective-permute-done((bf16[64,256]{1,0:T(8,128)(2,1)S(1)}, bf16[64,256]{1,0:T(8,128)(2,1)S(1)}, u32[]{:S(2)}, u32[]{:S(2)}) %collective-permute-start.9) | collective-permute-done | bytes 32800 | tf_op jit(solution)/shard_map/ppermute | solution.py:198
  25.4 0.1 collective-permute-start.14
  25.4 0.4 %second_start.1.before = f32[4,64,256]{2,1,0:T(8,128)S(1)} custom-call(bf16[2,64,256]{2,1,0:T(8,128)(2,1)S(1)} %pad_maximum_fusion.5.vectors, bf16[16,1024,128]{2,1,0:T(8,128)(2,1)S(1)} %place.1.dense.a_1_), custom_call_target="tpu_custom_call" | custom-call | tf_op jit(solution)/shard_map/second_start/pallas_call | solution.py:248
  25.9 0.0 collective-permute-done.11
  25.9 0.0 collective-permute-done.12
  25.9 0.7 %collective-permute-start.13 = (bf16[2,64,256]{2,1,0:T(8,128)(2,1)S(1)}, bf16[2,64,256]{2,1,0:T(8,128)(2,1)S(1)}, u32[]{:S(2)}, u32[]{:S(2)}) collective-permute-start(bf16[2,64,256]{2,1,0:T(8,128)(2,1)S(1)} %pad_maximum_fusion.4), channel_id=1, source_target_pairs={{0,4},{4,0},{8,12},{12,8},{16,20},{20,16},{24,28},{28,24},{1,5},{5... | collective-permute-start | bytes 196616 | tf_op jit(solution)/shard_map/ppermute | solution.py:198
  26.6 0.1 collective-permute-done.14
  26.7 0.0 copy-start.3
  26.7 0.0 copy-start.4
  26.7 0.0 copy-start.5
  26.7 0.8 %second_more.1.a_2_ = f32[4,64,256]{2,1,0:T(8,128)S(1)} custom-call(bf16[4,64,256]{2,1,0:T(8,128)(2,1)S(1)} %pad_maximum_fusion.1.vectors, bf16[16,1024,128]{2,1,0:T(8,128)(2,1)S(1)} %place.1.dense.a_1_, f32[4,64,256]{2,1,0:T(8,128)S(1)} %second_start.1.before), custom_call_target="tpu_custom_call" | custom-call | tf_op jit(solution)/shard_map/second_more/pallas_call | solution.py:251
  27.5 0.0 collective-permute-done.13.a_0_
  27.5 0.5 %second_end.1 = (f32[64,256]{1,0:T(8,128)S(1)}, bf16[144,128]{1,0:T(8,128)(2,1)S(1)}, bf16[144,128]{1,0:T(8,128)(2,1)S(1)}, bf16[144,128]{1,0:T(8,128)(2,1)S(1)}, f32[8,128]{1,0:T(8,128)S(1)}) custom-call(bf16[2,64,256]{2,1,0:T(8,128)(2,1)S(1)} %collective-permute-done.13.a_0_, bf16[16,1024,128]{2,1,0:T(8,128)(2,1)S(1)} %place.1.dense.a_1_, ...), custom_call_target="tpu_custom_call" | custom-call | tf_op jit(solution)/shard_map/second_end/pallas_call | solution.py:259
  28.1 1.8 %collective-permute-start.15 = (bf16[144,128]{1,0:T(8,128)(2,1)S(1)}, bf16[144,128]{1,0:T(8,128)(2,1)S(1)}, u32[]{:S(2)}, u32[]{:S(2)}) collective-permute-start(bf16[144,128]{1,0:T(8,128)(2,1)S(1)} %get-tuple-element.69), channel_id=1, source_target_pairs={{0,2},{1,3},{2,0},{3,1},{4,6},{5,7},{6,4},{7,5},{8,10},{9,11},{10,... | collective-permute-start | bytes 110600 | tf_op jit(solution)/shard_map/ppermute | solution.py:198
  29.9 1.2 %collective-permute-start.16 = (bf16[144,128]{1,0:T(8,128)(2,1)S(1)}, bf16[144,128]{1,0:T(8,128)(2,1)S(1)}, u32[]{:S(2)}, u32[]{:S(2)}) collective-permute-start(bf16[144,128]{1,0:T(8,128)(2,1)S(1)} %get-tuple-element.70), channel_id=1, source_target_pairs={{0,3},{1,2},{2,1},{3,0},{4,7},{5,6},{6,5},{7,4},{8,11},{9,10},{10,... | collective-permute-start | bytes 110600 | tf_op jit(solution)/shard_map/ppermute | solution.py:198
  31.1 0.5 %collective-permute-start.17 = (bf16[144,128]{1,0:T(8,128)(2,1)S(1)}, bf16[144,128]{1,0:T(8,128)(2,1)S(1)}, u32[]{:S(2)}, u32[]{:S(2)}) collective-permute-start(bf16[144,128]{1,0:T(8,128)(2,1)S(1)} %get-tuple-element.71), channel_id=1, source_target_pairs={{0,1},{1,0},{2,3},{3,2},{4,5},{5,4},{6,7},{7,6},{8,9},{9,8},{10,11... | collective-permute-start | bytes 110600 | tf_op jit(solution)/shard_map/ppermute | solution.py:198
  31.6 2.2 %collective-permute-done.15.refs_0_ = bf16[144,128]{1,0:T(8,128)(2,1)S(1)} collective-permute-done((bf16[144,128]{1,0:T(8,128)(2,1)S(1)}, bf16[144,128]{1,0:T(8,128)(2,1)S(1)}, u32[]{:S(2)}, u32[]{:S(2)}) %collective-permute-start.15) | collective-permute-done | bytes 36896 | tf_op jit(solution)/shard_map/ppermute | solution.py:198
  33.8 1.9 %collective-permute-done.16.refs_1_ = bf16[144,128]{1,0:T(8,128)(2,1)S(1)} collective-permute-done((bf16[144,128]{1,0:T(8,128)(2,1)S(1)}, bf16[144,128]{1,0:T(8,128)(2,1)S(1)}, u32[]{:S(2)}, u32[]{:S(2)}) %collective-permute-start.16) | collective-permute-done | bytes 36896 | tf_op jit(solution)/shard_map/ppermute | solution.py:198
  35.7 0.0 collective-permute-done.17.refs_2_
  35.7 0.1 collective-permute-start.18
  35.8 1.9 %collective-permute-start.19 = (f32[8,128]{1,0:T(8,128)S(1)}, f32[8,128]{1,0:T(8,128)S(1)}, u32[]{:S(2)}, u32[]{:S(2)}) collective-permute-start(f32[8,128]{1,0:T(8,128)S(1)} %get-tuple-element.73), channel_id=1, source_target_pairs={{0,20},{4,16},{8,28},{12,24},{16,4},{20,0},{24,12},{28,8},{1,21},{... | collective-permute-start | bytes 12296 | tf_op jit(solution)/shard_map/ppermute | solution.py:198
  37.7 0.4 collective-permute-start.20
  38.1 0.0 copy-done.4
  38.1 1.2 %last.1 = (f32[64,256]{1,0:T(8,128)}, f32[64,256]{1,0:T(8,128)}) custom-call(f32[2]{0:T(128)S(1)} %copy-done.5, f32[64,256]{1,0:T(8,128)S(1)} %get-tuple-element.75.own, bf16[144,128]{1,0:T(8,128)(2,1)S(1)} %collective-permute-done.15.refs_0_, bf16[144,128]{1,0:T(8,128)(2,1)S(1)} %collective-permute-done.16.refs_1_, ...), custom_call_target="tpu_custom_call" | custom-call | tf_op jit(solution)/shard_map/last/pallas_call | solution.py:329
  39.3 0.4 collective-permute-done.18
  39.7 0.0 collective-permute-done.19
  39.7 1.0 %collective-permute-done.20 = f32[8,128]{1,0:T(8,128)S(1)} collective-permute-done((f32[8,128]{1,0:T(8,128)S(1)}, f32[8,128]{1,0:T(8,128)S(1)}, u32[]{:S(2)}, u32[]{:S(2)}) %collective-permute-start.20) | collective-permute-done | bytes 4128 | tf_op jit(solution)/shard_map/ppermute | solution.py:198
  40.7 0.0 collective-permute-start.21
  40.7 1.2 %collective-permute-done.21 = f32[8,128]{1,0:T(8,128)S(1)} collective-permute-done((f32[8,128]{1,0:T(8,128)S(1)}, f32[8,128]{1,0:T(8,128)S(1)}, u32[]{:S(2)}, u32[]{:S(2)}) %collective-permute-start.21) | collective-permute-done | bytes 4128 | tf_op jit(solution)/shard_map/ppermute | solution.py:198
  41.9 0.6 %slice_multiply_fusion = f32[2,64]{1,0:T(2,128)} fusion(f32[8,128]{1,0:T(8,128)S(1)} %add.15), kind=kLoop, calls=%fused_computation.7 | loop fusion | flops 128 | bytes 1024 | tf_op jit(solution)/shard_map/mul | solution.py:341
  (13 shorter events, 0.1 us)
Async XLA Ops:
  1.5 8.2 %collective-permute-start.2 = (bf16[64,256]{1,0:T(8,128)(2,1)S(1)}, bf16[64,256]{1,0:T(8,128)(2,1)S(1)}, u32[]{:S(2)}, u32[]{:S(2)}) collective-permute-start(bf16[64,256]{1,0:T(8,128)(2,1)S(1)} %get-tuple-element.48), channel_id=1, source_target_pairs={{0,28},{4,24},{8,20},{12,16},{16,12},{20,8},{24,4},{28,0},{1,29},{... | collective-permute-start | bytes 98312 | tf_op jit(solution)/shard_map/ppermute | solution.py:198
  4.9 4.8 %collective-permute-start.3 = (bf16[64,256]{1,0:T(8,128)(2,1)S(1)}, bf16[64,256]{1,0:T(8,128)(2,1)S(1)}, u32[]{:S(2)}, u32[]{:S(2)}) collective-permute-start(bf16[64,256]{1,0:T(8,128)(2,1)S(1)} %get-tuple-element.49), channel_id=1, source_target_pairs={{0,20},{4,16},{8,28},{12,24},{16,4},{20,0},{24,12},{28,8},{1,21},{... | collective-permute-start | bytes 98312 | tf_op jit(solution)/shard_map/ppermute | solution.py:198
  5.7 4.3 %collective-permute-start = (bf16[64,256]{1,0:T(8,128)(2,1)S(1)}, bf16[64,256]{1,0:T(8,128)(2,1)S(1)}, u32[]{:S(2)}, u32[]{:S(2)}) collective-permute-start(bf16[64,256]{1,0:T(8,128)(2,1)S(1)} %get-tuple-element.44), channel_id=1, source_target_pairs={{0,12},{4,8},{8,4},{12,0},{16,28},{20,24},{24,20},{28,16},{1,13},{... | collective-permute-start | bytes 98312 | tf_op jit(solution)/shard_map/ppermute | solution.py:198
  5.9 6.2 %collective-permute-start.5 = (bf16[64,256]{1,0:T(8,128)(2,1)S(1)}, bf16[64,256]{1,0:T(8,128)(2,1)S(1)}, u32[]{:S(2)}, u32[]{:S(2)}) collective-permute-start(bf16[64,256]{1,0:T(8,128)(2,1)S(1)} %get-tuple-element.59), channel_id=1, source_target_pairs={{0,1},{1,0},{2,3},{3,2},{4,5},{5,4},{6,7},{7,6},{8,9},{9,8},{10,11... | collective-permute-start | bytes 98312 | tf_op jit(solution)/shard_map/ppermute | solution.py:198
  9.7 1.4 %collective-permute-start.4 = (bf16[3,64,256]{2,1,0:T(8,128)(2,1)S(1)}, bf16[3,64,256]{2,1,0:T(8,128)(2,1)S(1)}, u32[]{:S(2)}, u32[]{:S(2)}) collective-permute-start(bf16[3,64,256]{2,1,0:T(8,128)(2,1)S(1)} %pad_maximum_fusion.2), channel_id=1, source_target_pairs={{0,4},{4,0},{8,12},{12,8},{16,20},{20,16},{24,28},{28,24},{1,5},{5... | collective-permute-start | bytes 294920 | tf_op jit(solution)/shard_map/ppermute | solution.py:198
  10.1 1.7 %collective-permute-start.1 = (bf16[1,64,256]{2,1,0:T(8,128)(2,1)S(1)}, bf16[1,64,256]{2,1,0:T(8,128)(2,1)S(1)}, u32[]{:S(2)}, u32[]{:S(2)}) collective-permute-start(bf16[1,64,256]{2,1,0:T(8,128)(2,1)S(1)} %bitcast.24), channel_id=1, source_target_pairs={{0,4},{4,0},{8,12},{12,8},{16,20},{20,16},{24,28},{28,24},{1,5},{5... | collective-permute-start | bytes 98312 | tf_op jit(solution)/shard_map/ppermute | solution.py:198
  11.1 9.8 %copy-start = (f32[64,256]{1,0:T(8,128)S(1)}, f32[64,256]{1,0:T(8,128)}, u32[]{:S(2)}) copy-start(f32[64,256]{1,0:T(8,128)} %a_5_.1) | copy-start | bytes 196612
  11.1 9.8 %copy-start.1 = (f32[64,256]{1,0:T(8,128)S(1)}, f32[64,256]{1,0:T(8,128)}, u32[]{:S(2)}) copy-start(f32[64,256]{1,0:T(8,128)} %refs_3_.5) | copy-start | bytes 196612
  11.1 9.8 %copy-start.2 = (f32[64,256]{1,0:T(8,128)S(1)}, f32[64,256]{1,0:T(8,128)}, u32[]{:S(2)}) copy-start(f32[64,256]{1,0:T(8,128)} %refs_3_.4) | copy-start | bytes 196612
  12.0 6.2 %collective-permute-start.6 = (bf16[128,128]{1,0:T(8,128)(2,1)S(1)}, bf16[128,128]{1,0:T(8,128)(2,1)S(1)}, u32[]{:S(2)}, u32[]{:S(2)}) collective-permute-start(bf16[128,128]{1,0:T(8,128)(2,1)S(1)} %get-tuple-element.55), channel_id=1, source_target_pairs={{0,3},{1,2},{2,1},{3,0},{4,7},{5,6},{6,5},{7,4},{8,11},{9,10},{10,... | collective-permute-start | bytes 98312 | tf_op jit(solution)/shard_map/ppermute | solution.py:198
  14.9 6.0 %collective-permute-start.7 = (bf16[128,128]{1,0:T(8,128)(2,1)S(1)}, bf16[128,128]{1,0:T(8,128)(2,1)S(1)}, u32[]{:S(2)}, u32[]{:S(2)}) collective-permute-start(bf16[128,128]{1,0:T(8,128)(2,1)S(1)} %get-tuple-element.56), channel_id=1, source_target_pairs={{0,2},{1,3},{2,0},{3,1},{4,6},{5,7},{6,4},{7,5},{8,10},{9,11},{10,... | collective-permute-start | bytes 98312 | tf_op jit(solution)/shard_map/ppermute | solution.py:198
  14.9 6.0 %collective-permute-start.8 = (bf16[128,128]{1,0:T(8,128)(2,1)S(1)}, bf16[128,128]{1,0:T(8,128)(2,1)S(1)}, u32[]{:S(2)}, u32[]{:S(2)}) collective-permute-start(bf16[128,128]{1,0:T(8,128)(2,1)S(1)} %get-tuple-element.57), channel_id=1, source_target_pairs={{0,1},{1,0},{2,3},{3,2},{4,5},{5,4},{6,7},{7,6},{8,9},{9,8},{10,11... | collective-permute-start | bytes 98312 | tf_op jit(solution)/shard_map/ppermute | solution.py:198
  16.5 7.6 %collective-permute-start.10 = (bf16[2,64,256]{2,1,0:T(8,128)(2,1)S(1)}, bf16[2,64,256]{2,1,0:T(8,128)(2,1)S(1)}, u32[]{:S(2)}, u32[]{:S(2)}) collective-permute-start(bf16[2,64,256]{2,1,0:T(8,128)(2,1)S(1)} %pad_maximum_fusion.3), channel_id=1, source_target_pairs={{0,2},{1,3},{2,0},{3,1},{4,6},{5,7},{6,4},{7,5},{8,10},{9,11},{10,... | collective-permute-start | bytes 196616 | tf_op jit(solution)/shard_map/ppermute | solution.py:198
  21.0 4.3 %collective-permute-start.9 = (bf16[64,256]{1,0:T(8,128)(2,1)S(1)}, bf16[64,256]{1,0:T(8,128)(2,1)S(1)}, u32[]{:S(2)}, u32[]{:S(2)}) collective-permute-start(bf16[64,256]{1,0:T(8,128)(2,1)S(1)} %get-tuple-element.58), channel_id=1, source_target_pairs={{0,28},{4,24},{8,20},{12,16},{16,12},{20,8},{24,4},{28,0},{1,29},{... | collective-permute-start | bytes 98312 | tf_op jit(solution)/shard_map/ppermute | solution.py:198
  21.1 4.8 %collective-permute-start.11 = (bf16[64,256]{1,0:T(8,128)(2,1)S(1)}, bf16[64,256]{1,0:T(8,128)(2,1)S(1)}, u32[]{:S(2)}, u32[]{:S(2)}) collective-permute-start(bf16[64,256]{1,0:T(8,128)(2,1)S(1)} %get-tuple-element.62), channel_id=1, source_target_pairs={{0,20},{4,16},{8,28},{12,24},{16,4},{20,0},{24,12},{28,8},{1,21},{... | collective-permute-start | bytes 98312 | tf_op jit(solution)/shard_map/ppermute | solution.py:198
  22.5 3.4 %collective-permute-start.12 = (bf16[64,256]{1,0:T(8,128)(2,1)S(1)}, bf16[64,256]{1,0:T(8,128)(2,1)S(1)}, u32[]{:S(2)}, u32[]{:S(2)}) collective-permute-start(bf16[64,256]{1,0:T(8,128)(2,1)S(1)} %get-tuple-element.63), channel_id=1, source_target_pairs={{0,12},{4,8},{8,4},{12,0},{16,28},{20,24},{24,20},{28,16},{1,13},{... | collective-permute-start | bytes 98312 | tf_op jit(solution)/shard_map/ppermute | solution.py:198
  25.4 1.3 %collective-permute-start.14 = (bf16[2,64,256]{2,1,0:T(8,128)(2,1)S(1)}, bf16[2,64,256]{2,1,0:T(8,128)(2,1)S(1)}, u32[]{:S(2)}, u32[]{:S(2)}) collective-permute-start(bf16[2,64,256]{2,1,0:T(8,128)(2,1)S(1)} %pad_maximum_fusion.5.vectors), channel_id=1, source_target_pairs={{0,4},{4,0},{8,12},{12,8},{16,20},{20,16},{24,28},{28,24},{1,5},{5... | collective-permute-start | bytes 196616 | tf_op jit(solution)/shard_map/ppermute | solution.py:198
  25.9 1.6 %collective-permute-start.13 = (bf16[2,64,256]{2,1,0:T(8,128)(2,1)S(1)}, bf16[2,64,256]{2,1,0:T(8,128)(2,1)S(1)}, u32[]{:S(2)}, u32[]{:S(2)}) collective-permute-start(bf16[2,64,256]{2,1,0:T(8,128)(2,1)S(1)} %pad_maximum_fusion.4), channel_id=1, source_target_pairs={{0,4},{4,0},{8,12},{12,8},{16,20},{20,16},{24,28},{28,24},{1,5},{5... | collective-permute-start | bytes 196616 | tf_op jit(solution)/shard_map/ppermute | solution.py:198
  26.7 11.4 %copy-start.3 = (f32[64,256]{1,0:T(8,128)S(1)}, f32[64,256]{1,0:T(8,128)}, u32[]{:S(2)}) copy-start(f32[64,256]{1,0:T(8,128)} %value.1.refs_4_) | copy-start | bytes 196612
  26.7 11.4 %copy-start.4 = (f32[64,256]{1,0:T(8,128)S(1)}, f32[64,256]{1,0:T(8,128)}, u32[]{:S(2)}) copy-start(f32[64,256]{1,0:T(8,128)} %refs_5_.3) | copy-start | bytes 196612
  26.7 11.4 %copy-start.5 = (f32[2]{0:T(128)S(1)}, f32[2]{0:T(128)}, u32[]{:S(2)}) copy-start(f32[2]{0:T(128)} %coeffs.1) | copy-start | bytes 28
  28.1 5.7 %collective-permute-start.15 = (bf16[144,128]{1,0:T(8,128)(2,1)S(1)}, bf16[144,128]{1,0:T(8,128)(2,1)S(1)}, u32[]{:S(2)}, u32[]{:S(2)}) collective-permute-start(bf16[144,128]{1,0:T(8,128)(2,1)S(1)} %get-tuple-element.69), channel_id=1, source_target_pairs={{0,2},{1,3},{2,0},{3,1},{4,6},{5,7},{6,4},{7,5},{8,10},{9,11},{10,... | collective-permute-start | bytes 110600 | tf_op jit(solution)/shard_map/ppermute | solution.py:198
  29.9 5.8 %collective-permute-start.16 = (bf16[144,128]{1,0:T(8,128)(2,1)S(1)}, bf16[144,128]{1,0:T(8,128)(2,1)S(1)}, u32[]{:S(2)}, u32[]{:S(2)}) collective-permute-start(bf16[144,128]{1,0:T(8,128)(2,1)S(1)} %get-tuple-element.70), channel_id=1, source_target_pairs={{0,3},{1,2},{2,1},{3,0},{4,7},{5,6},{6,5},{7,4},{8,11},{9,10},{10,... | collective-permute-start | bytes 110600 | tf_op jit(solution)/shard_map/ppermute | solution.py:198
  31.1 4.5 %collective-permute-start.17 = (bf16[144,128]{1,0:T(8,128)(2,1)S(1)}, bf16[144,128]{1,0:T(8,128)(2,1)S(1)}, u32[]{:S(2)}, u32[]{:S(2)}) collective-permute-start(bf16[144,128]{1,0:T(8,128)(2,1)S(1)} %get-tuple-element.71), channel_id=1, source_target_pairs={{0,1},{1,0},{2,3},{3,2},{4,5},{5,4},{6,7},{7,6},{8,9},{9,8},{10,11... | collective-permute-start | bytes 110600 | tf_op jit(solution)/shard_map/ppermute | solution.py:198
  35.7 4.0 %collective-permute-start.18 = (f32[8,128]{1,0:T(8,128)S(1)}, f32[8,128]{1,0:T(8,128)S(1)}, u32[]{:S(2)}, u32[]{:S(2)}) collective-permute-start(f32[8,128]{1,0:T(8,128)S(1)} %get-tuple-element.72), channel_id=1, source_target_pairs={{0,28},{4,24},{8,20},{12,16},{16,12},{20,8},{24,4},{28,0},{1,29},{... | collective-permute-start | bytes 12296 | tf_op jit(solution)/shard_map/ppermute | solution.py:198
  35.8 3.9 %collective-permute-start.19 = (f32[8,128]{1,0:T(8,128)S(1)}, f32[8,128]{1,0:T(8,128)S(1)}, u32[]{:S(2)}, u32[]{:S(2)}) collective-permute-start(f32[8,128]{1,0:T(8,128)S(1)} %get-tuple-element.73), channel_id=1, source_target_pairs={{0,20},{4,16},{8,28},{12,24},{16,4},{20,0},{24,12},{28,8},{1,21},{... | collective-permute-start | bytes 12296 | tf_op jit(solution)/shard_map/ppermute | solution.py:198
  37.7 3.0 %collective-permute-start.20 = (f32[8,128]{1,0:T(8,128)S(1)}, f32[8,128]{1,0:T(8,128)S(1)}, u32[]{:S(2)}, u32[]{:S(2)}) collective-permute-start(f32[8,128]{1,0:T(8,128)S(1)} %get-tuple-element.74), channel_id=1, source_target_pairs={{0,12},{4,8},{8,4},{12,0},{16,28},{20,24},{24,20},{28,16},{1,13},{... | collective-permute-start | bytes 12296 | tf_op jit(solution)/shard_map/ppermute | solution.py:198
  40.7 1.2 %collective-permute-start.21 = (f32[8,128]{1,0:T(8,128)S(1)}, f32[8,128]{1,0:T(8,128)S(1)}, u32[]{:S(2)}, u32[]{:S(2)}) collective-permute-start(f32[8,128]{1,0:T(8,128)S(1)} %add_add_fusion), channel_id=1, source_target_pairs={{0,4},{4,0},{8,12},{12,8},{16,20},{20,16},{24,28},{28,24},{1,5},{5... | collective-permute-start | bytes 12296 | tf_op jit(solution)/shard_map/ppermute | solution.py:198

commit v5 on v4

--- a/solution.py
+++ b/solution.py
@@ -11,10 +11,11 @@
 SMEM = pl.BlockSpec(memory_space=pltpu.SMEM)
 HBM = pl.BlockSpec(memory_space=pltpu.HBM)
 CONTRACT_LAST = (((1,), (1,)), ((), ()))
-F32, BF16 = jnp.float32, jnp.bfloat16
+F32, BF16, F16 = jnp.float32, jnp.bfloat16, jnp.float16
+SCALE, TILE_SCALE = 2.0**-6, 2.0**-16
 LANES = 128
-ORDER1 = [3, 2, 1]
-ORDER2 = [2, 3, 1]
+ORDER1 = [1, 2, 3]
+ORDER2 = [2, 1, 3]
 FAR_A, FAR_C, FAR_M = [6, 4, 2], [6, 4, 2], [6, 4, 2]
 
 
@@ -104,7 +105,7 @@
         if m == 0:
             own[...] = total
         else:
-            put_halves(sends[m], 0, total.astype(BF16))
+            put_halves(sends[m], 0, total * SCALE)
 
 
 def end_moment_kernel(pb, order, send_order, n_kept, vectors, dense, half, before, handed, *refs):
@@ -122,11 +123,11 @@
         if m == 0:
             own[...] = total
         else:
-            put_halves(sends[m], 0, total.astype(BF16))
+            put_halves(sends[m], 0, total * SCALE)
     both = before[...][:2] + jnp.concatenate([jnp.zeros((1, LANES), F32), 2.0 * as_row(sums)], axis=0)
     tile_out[...] = jnp.concatenate([both, jnp.zeros((6, LANES), F32)], axis=0)
-    high, low = two_parts(both)
-    tile = jnp.concatenate([high, low, jnp.zeros((12, LANES), F32)], axis=0).astype(BF16)
+    high, low = two_parts(both * TILE_SCALE)
+    tile = jnp.concatenate([high, low, jnp.zeros((12, LANES), F32)], axis=0)
     for send in sends.values():
         send[pl.ds(rows, 16), :] = tile
 
@@ -147,7 +148,7 @@
     count, width = own.shape
     total = own[...]
     for r in received:
-        total = total + get_halves(r, 0, count, width).astype(F32)
+        total = total + get_halves(r, 0, count, width) * (1 / SCALE)
     return total
 
 
@@ -170,7 +171,7 @@
     received, outs = refs[:n_received], refs[n_received:]
     total = mine[...]
     for r in received:
-        t = r[pl.ds(start, 16), :].astype(F32)
+        t = r[pl.ds(start, 16), :] * (1 / TILE_SCALE)
         total = total + jnp.concatenate([t[0:2] + t[2:4], jnp.zeros((6, LANES), F32)], axis=0)
     for out in outs:
         out[...] = total
@@ -255,7 +256,7 @@
             name + "_more",
         )(second, dense, most)
         outs = [shape(count, width)]
-        outs += [shape(rows + extra_rows.get(m, 0), LANES, dtype=BF16) for m in send_order] + tail_shapes
+        outs += [shape(rows + extra_rows.get(m, 0), LANES) for m in send_order] + tail_shapes
         return call(
             functools.partial(kernel, pb, others_order[n_early:], send_order),
             outs,
@@ -268,7 +269,7 @@
         first_order, second_order = ORDER1, ORDER2
 
     def exchange(sends, order):
-        return [swap(send, "col", m) for m, send in zip(order, sends)]
+        return [swap(send.astype(F16), "col", m).astype(F32) for m, send in zip(order, sends)]
 
     rounded_probes, *v = call(
         cast_kernel,
@@ -337,8 +338,9 @@
     got, t_after, accum_out = barrier((got, t_after, accum_out))
     for one in got:
         total = total + one
-    total = total + swap(total, "row", 1)
-    moments = total[:2, :count] * float(total_rows) ** (-0.5)
+    scale = float(total_rows) ** (-0.5)
+    other = swap(total, "row", 1)
+    moments = (total[:2, :count] + other[:2, :count]) * scale
     return (t_next, t_after, accum_out, moments)
 
 

time: 42.6 us -> 43.4 us (1.019)
  starting transfers between devices: 21.8 us -> 22.4 us
    ppermute x22, starting transfers between devices: 21.8 us -> 22.4 us  [swap(): return lax.ppermute(x, axis, [(i, i ^ k) for i in range(n)])]
  transfers between devices with their start and end apart: 22 -> 22, of which waited for: 8 -> 10; matrix products, arithmetic and copies ran while one was open for 0% -> 0% of each run, Pallas kernels for 15% -> 15%
where the time goes in v5:
time: 43.4 us; the launch traced here: 43.1 us
  starting transfers between devices  22.4 us (52%)
  waiting for transfers between devices  10.5 us (24%)
  Pallas kernels  7.87 us (18%)
  between operations  1.57 us (4%)
  other arithmetic  0.74 us (2%)
    ppermute x22, starting transfers between devices, swap(): return lax.ppermute(x, axis, [(i, i ^ k) for i in range(n)])  22.4 us
    ppermute x22, waiting for transfers between devices, swap(): return lax.ppermute(x, axis, [(i, i ^ k) for i in range(n)])  10.5 us
    pallas_call x1, Pallas kernels, local(): call(functools.partial(place_kernel, pb, group), shape(n_row * pb, n_col...  1.6 us
    pallas_call x2, Pallas kernels, multiply(): call(functools.partial(more_kernel, pb, both[n_first:len(order) + n_early...  1.35 us
    pallas_call x1, Pallas kernels, local(): call(functools.partial(last_kernel, n_col), [shape(count, width), shape(c...  1.22 us
    pallas_call x2, Pallas kernels, multiply(): call(functools.partial(start_kernel, pb, both[:n_first]), sums, [VMEM] *...  1.18 us
    pallas_call x1, Pallas kernels, local(): call(cast_kernel, [shape(count, width, dtype=BF16)] * (1 + n_out), [HBM]...  0.9 us
  transfers between devices with their start and end apart: 22, of which 10 were waited for; matrix products, arithmetic and copies ran while one was open for 0% of the time, Pallas kernels for 15%

profile of v5, /device:TPU:0, one launch (start us, length us, event | category | flops | bytes accessed | tf_op | source)
XLA Modules:
  0.0 43.1 jit_solution(6955493191003863985)
XLA Ops:
  0.6 0.9 %cast.1 = (bf16[64,256]{1,0:T(8,128)(2,1)S(1)}, bf16[64,256]{1,0:T(8,128)(2,1)S(1)}, bf16[64,256]{1,0:T(8,128)(2,1)S(1)}, bf16[64,256]{1,0:T(8,128)(2,1)S(1)}, bf16[64,256]{1,0:T(8,128)(2,1)S(1)}) custom-call(f32[64,256]{1,0:T(8,128)} %refs_3_.5, f32[64,256]{1,0:T(8,128)} %a_5_.1), custom_call_target="tpu_custom_call" | custom-call | tf_op jit(solution)/shard_map/cast/pallas_call | solution.py:274
  1.5 3.4 %collective-permute-start.2 = (bf16[64,256]{1,0:T(8,128)(2,1)S(1)}, bf16[64,256]{1,0:T(8,128)(2,1)S(1)}, u32[]{:S(2)}, u32[]{:S(2)}) collective-permute-start(bf16[64,256]{1,0:T(8,128)(2,1)S(1)} %get-tuple-element.48), channel_id=1, source_target_pairs={{0,28},{4,24},{8,20},{12,16},{16,12},{20,8},{24,4},{28,0},{1,29},{... | collective-permute-start | bytes 98312 | tf_op jit(solution)/shard_map/ppermute | solution.py:199
  4.9 0.8 %collective-permute-start.3 = (bf16[64,256]{1,0:T(8,128)(2,1)S(1)}, bf16[64,256]{1,0:T(8,128)(2,1)S(1)}, u32[]{:S(2)}, u32[]{:S(2)}) collective-permute-start(bf16[64,256]{1,0:T(8,128)(2,1)S(1)} %get-tuple-element.49), channel_id=1, source_target_pairs={{0,20},{4,16},{8,28},{12,24},{16,4},{20,0},{24,12},{28,8},{1,21},{... | collective-permute-start | bytes 98312 | tf_op jit(solution)/shard_map/ppermute | solution.py:199
  5.7 0.1 collective-permute-start
  5.9 1.6 %collective-permute-start.5 = (bf16[64,256]{1,0:T(8,128)(2,1)S(1)}, bf16[64,256]{1,0:T(8,128)(2,1)S(1)}, u32[]{:S(2)}, u32[]{:S(2)}) collective-permute-start(bf16[64,256]{1,0:T(8,128)(2,1)S(1)} %get-tuple-element.59), channel_id=1, source_target_pairs={{0,1},{1,0},{2,3},{3,2},{4,5},{5,4},{6,7},{7,6},{8,9},{9,8},{10,11... | collective-permute-start | bytes 98312 | tf_op jit(solution)/shard_map/ppermute | solution.py:199
  8.1 1.6 %place.1.dense.a_1_ = bf16[16,1024,128]{2,1,0:T(8,128)(2,1)S(1)} custom-call(s32[1,1]{1,0:T(1,128)S(6)} %copy.13.count, s32[1,1,64]{2,1,0:T(1,128)} %rows_in.1, s32[1,1,64]{2,1,0:T(1,128)} %cols_in.1, bf16[1,1,64,128,128]{4,3,2,1,0:T(8,128)(2,1)} %blocks.1), custom_call_target="tpu_custom_call" | custom-call | tf_op jit(solution)/shard_map/place/pallas_call | solution.py:220
  9.7 0.0 collective-permute-done.2
  9.7 0.0 collective-permute-done.3
  9.7 0.3 collective-permute-start.4
  10.1 0.0 collective-permute-done
  10.1 0.2 collective-permute-start.1
  10.3 0.7 %first_start.1.before = f32[4,64,256]{2,1,0:T(8,128)S(1)} custom-call(bf16[4,64,256]{2,1,0:T(8,128)(2,1)S(1)} %pad_maximum_fusion.vectors, bf16[16,1024,128]{2,1,0:T(8,128)(2,1)S(1)} %place.1.dense.a_1_), custom_call_target="tpu_custom_call" | custom-call | tf_op jit(solution)/shard_map/first_start/pallas_call | solution.py:249
  11.1 0.0 copy-start
  11.1 0.0 copy-start.1
  11.1 0.0 copy-start.2
  11.1 0.0 collective-permute-done.4.vectors
  11.1 0.6 %first_more.1.before = f32[4,64,256]{2,1,0:T(8,128)S(1)} custom-call(bf16[3,64,256]{2,1,0:T(8,128)(2,1)S(1)} %collective-permute-done.4.vectors, bf16[16,1024,128]{2,1,0:T(8,128)(2,1)S(1)} %place.1.dense.a_1_, f32[4,64,256]{2,1,0:T(8,128)S(1)} %first_start.1.before), custom_call_target="tpu_custom_call" | custom-call | tf_op jit(solution)/shard_map/first_more/pallas_call | solution.py:252
  11.7 0.0 collective-permute-done.1.vectors
  11.7 0.3 first_end.1
  12.0 0.0 collective-permute-done.5.a_6_
  12.1 2.8 %collective-permute-start.8 = (f16[128,128]{1,0:T(8,128)(2,1)S(1)}, f16[128,128]{1,0:T(8,128)(2,1)S(1)}, u32[]{:S(2)}, u32[]{:S(2)}) collective-permute-start(f16[128,128]{1,0:T(8,128)(2,1)S(1)} %convert_element_type.40), channel_id=1, source_target_pairs={{0,3},{1,2},{2,1},{3,0},{4,7},{5,6},{6,5},{7,4},{8,11},{9,10},{10,... | collective-permute-start | bytes 98312 | tf_op jit(solution)/shard_map/ppermute | solution.py:199
  14.9 0.0 collective-permute-start.7
  14.9 1.6 %collective-permute-start.6 = (f16[128,128]{1,0:T(8,128)(2,1)S(1)}, f16[128,128]{1,0:T(8,128)(2,1)S(1)}, u32[]{:S(2)}, u32[]{:S(2)}) collective-permute-start(f16[128,128]{1,0:T(8,128)(2,1)S(1)} %convert_element_type.36), channel_id=1, source_target_pairs={{0,1},{1,0},{2,3},{3,2},{4,5},{5,4},{6,7},{7,6},{8,9},{9,8},{10,11... | collective-permute-start | bytes 98312 | tf_op jit(solution)/shard_map/ppermute | solution.py:199
  16.5 1.8 %collective-permute-start.10 = (bf16[2,64,256]{2,1,0:T(8,128)(2,1)S(1)}, bf16[2,64,256]{2,1,0:T(8,128)(2,1)S(1)}, u32[]{:S(2)}, u32[]{:S(2)}) collective-permute-start(bf16[2,64,256]{2,1,0:T(8,128)(2,1)S(1)} %pad_maximum_fusion.3), channel_id=1, source_target_pairs={{0,2},{1,3},{2,0},{3,1},{4,6},{5,7},{6,4},{7,5},{8,10},{9,11},{10,... | collective-permute-start | bytes 196616 | tf_op jit(solution)/shard_map/ppermute | solution.py:199
  18.3 0.0 collective-permute-done.8
  18.3 2.6 %collective-permute-done.7 = f16[128,128]{1,0:T(8,128)(2,1)S(1)} collective-permute-done((f16[128,128]{1,0:T(8,128)(2,1)S(1)}, f16[128,128]{1,0:T(8,128)(2,1)S(1)}, u32[]{:S(2)}, u32[]{:S(2)}) %collective-permute-start.7) | collective-permute-done | bytes 32800 | tf_op jit(solution)/shard_map/ppermute | solution.py:199
  21.0 0.0 collective-permute-done.6
  21.0 0.0 copy-done
  21.0 0.0 copy-done.1
  21.0 0.1 next.1
  21.1 0.1 collective-permute-start.9
  21.2 0.7 %value.1.refs_4_ = f32[64,256]{1,0:T(8,128)} custom-call(f32[64,256]{1,0:T(8,128)S(1)} %get-tuple-element.50.own, f32[128,128]{1,0:T(8,128)S(1)} %convert_element_type.37.refs_0_, f32[128,128]{1,0:T(8,128)S(1)} %convert_element_type.39.refs_1_, f32[128,128]{1,0:T(8,128)S(1)} %convert_element_type.41.refs_2_, f32[64,256]{1,0:T(8,128)S(1)} %copy-done.2), custom_call_target="tpu_custom_call" | custom-call | tf_op jit(solution)/shard_map/value/pallas_call | solution.py:308
  21.9 2.3 %collective-permute-start.11 = (bf16[64,256]{1,0:T(8,128)(2,1)S(1)}, bf16[64,256]{1,0:T(8,128)(2,1)S(1)}, u32[]{:S(2)}, u32[]{:S(2)}) collective-permute-start(bf16[64,256]{1,0:T(8,128)(2,1)S(1)} %get-tuple-element.62), channel_id=1, source_target_pairs={{0,20},{4,16},{8,28},{12,24},{16,4},{20,0},{24,12},{28,8},{1,21},{... | collective-permute-start | bytes 98312 | tf_op jit(solution)/shard_map/ppermute | solution.py:199
  24.1 0.0 collective-permute-start.12
  24.1 0.0 collective-permute-done.10.a_4_
  24.1 1.3 %collective-permute-done.9 = bf16[64,256]{1,0:T(8,128)(2,1)S(1)} collective-permute-done((bf16[64,256]{1,0:T(8,128)(2,1)S(1)}, bf16[64,256]{1,0:T(8,128)(2,1)S(1)}, u32[]{:S(2)}, u32[]{:S(2)}) %collective-permute-start.9) | collective-permute-done | bytes 32800 | tf_op jit(solution)/shard_map/ppermute | solution.py:199
  25.5 0.1 collective-permute-start.14
  25.5 0.4 %second_start.1.before = f32[4,64,256]{2,1,0:T(8,128)S(1)} custom-call(bf16[2,64,256]{2,1,0:T(8,128)(2,1)S(1)} %pad_maximum_fusion.5.vectors, bf16[16,1024,128]{2,1,0:T(8,128)(2,1)S(1)} %place.1.dense.a_1_), custom_call_target="tpu_custom_call" | custom-call | tf_op jit(solution)/shard_map/second_start/pallas_call | solution.py:249
  26.0 0.0 collective-permute-done.11
  26.0 1.5 %collective-permute-done.12 = bf16[64,256]{1,0:T(8,128)(2,1)S(1)} collective-permute-done((bf16[64,256]{1,0:T(8,128)(2,1)S(1)}, bf16[64,256]{1,0:T(8,128)(2,1)S(1)}, u32[]{:S(2)}, u32[]{:S(2)}) %collective-permute-start.12) | collective-permute-done | bytes 32800 | tf_op jit(solution)/shard_map/ppermute | solution.py:199
  27.5 0.1 collective-permute-start.13
  27.6 0.0 collective-permute-done.14
  27.6 0.0 copy-start.3
  27.6 0.0 copy-start.4
  27.6 0.0 copy-start.5
  27.6 0.8 %second_more.1.a_2_ = f32[4,64,256]{2,1,0:T(8,128)S(1)} custom-call(bf16[4,64,256]{2,1,0:T(8,128)(2,1)S(1)} %pad_maximum_fusion.1.vectors, bf16[16,1024,128]{2,1,0:T(8,128)(2,1)S(1)} %place.1.dense.a_1_, f32[4,64,256]{2,1,0:T(8,128)S(1)} %second_start.1.before), custom_call_target="tpu_custom_call" | custom-call | tf_op jit(solution)/shard_map/second_more/pallas_call | solution.py:252
  28.4 0.4 collective-permute-done.13.a_0_
  28.8 0.5 %second_end.1 = (f32[64,256]{1,0:T(8,128)S(1)}, f32[144,128]{1,0:T(8,128)S(1)}, f32[144,128]{1,0:T(8,128)S(1)}, f32[144,128]{1,0:T(8,128)S(1)}, f32[8,128]{1,0:T(8,128)S(1)}) custom-call(bf16[2,64,256]{2,1,0:T(8,128)(2,1)S(1)} %collective-permute-done.13.a_0_, bf16[16,1024,128]{2,1,0:T(8,128)(2,1)S(1)} %place.1.dense.a_1_, ...), custom_call_target="tpu_custom_call" | custom-call | tf_op jit(solution)/shard_map/second_end/pallas_call | solution.py:260
  29.4 1.7 %collective-permute-start.17 = (f16[144,128]{1,0:T(8,128)(2,1)S(1)}, f16[144,128]{1,0:T(8,128)(2,1)S(1)}, u32[]{:S(2)}, u32[]{:S(2)}) collective-permute-start(f16[144,128]{1,0:T(8,128)(2,1)S(1)} %convert_element_type.46), channel_id=1, source_target_pairs={{0,3},{1,2},{2,1},{3,0},{4,7},{5,6},{6,5},{7,4},{8,11},{9,10},{10,... | collective-permute-start | bytes 110600 | tf_op jit(solution)/shard_map/ppermute | solution.py:199
  31.1 0.1 collective-permute-start.16
  31.2 2.8 %collective-permute-start.15 = (f16[144,128]{1,0:T(8,128)(2,1)S(1)}, f16[144,128]{1,0:T(8,128)(2,1)S(1)}, u32[]{:S(2)}, u32[]{:S(2)}) collective-permute-start(f16[144,128]{1,0:T(8,128)(2,1)S(1)} %convert_element_type.42), channel_id=1, source_target_pairs={{0,2},{1,3},{2,0},{3,1},{4,6},{5,7},{6,4},{7,5},{8,10},{9,11},{10,... | collective-permute-start | bytes 110600 | tf_op jit(solution)/shard_map/ppermute | solution.py:199
  33.9 1.5 %collective-permute-done.17 = f16[144,128]{1,0:T(8,128)(2,1)S(1)} collective-permute-done((f16[144,128]{1,0:T(8,128)(2,1)S(1)}, f16[144,128]{1,0:T(8,128)(2,1)S(1)}, u32[]{:S(2)}, u32[]{:S(2)}) %collective-permute-start.17) | collective-permute-done | bytes 36896 | tf_op jit(solution)/shard_map/ppermute | solution.py:199
  35.4 0.3 collective-permute-done.16
  35.7 0.7 %collective-permute-done.15 = f16[144,128]{1,0:T(8,128)(2,1)S(1)} collective-permute-done((f16[144,128]{1,0:T(8,128)(2,1)S(1)}, f16[144,128]{1,0:T(8,128)(2,1)S(1)}, u32[]{:S(2)}, u32[]{:S(2)}) %collective-permute-start.15) | collective-permute-done | bytes 36896 | tf_op jit(solution)/shard_map/ppermute | solution.py:199
  36.5 0.1 collective-permute-start.18
  36.6 1.7 %collective-permute-start.19 = (f32[8,128]{1,0:T(8,128)S(1)}, f32[8,128]{1,0:T(8,128)S(1)}, u32[]{:S(2)}, u32[]{:S(2)}) collective-permute-start(f32[8,128]{1,0:T(8,128)S(1)} %get-tuple-element.73), channel_id=1, source_target_pairs={{0,20},{4,16},{8,28},{12,24},{16,4},{20,0},{24,12},{28,8},{1,21},{... | collective-permute-start | bytes 12296 | tf_op jit(solution)/shard_map/ppermute | solution.py:199
  38.3 0.8 %collective-permute-start.20 = (f32[8,128]{1,0:T(8,128)S(1)}, f32[8,128]{1,0:T(8,128)S(1)}, u32[]{:S(2)}, u32[]{:S(2)}) collective-permute-start(f32[8,128]{1,0:T(8,128)S(1)} %get-tuple-element.74), channel_id=1, source_target_pairs={{0,12},{4,8},{8,4},{12,0},{16,28},{20,24},{24,20},{28,16},{1,13},{... | collective-permute-start | bytes 12296 | tf_op jit(solution)/shard_map/ppermute | solution.py:199
  39.1 1.2 %last.1 = (f32[64,256]{1,0:T(8,128)}, f32[64,256]{1,0:T(8,128)}) custom-call(f32[2]{0:T(128)S(1)} %copy-done.5, f32[64,256]{1,0:T(8,128)S(1)} %get-tuple-element.75.own, f32[144,128]{1,0:T(8,128)S(1)} %convert_element_type.43.refs_0_, f32[144,128]{1,0:T(8,128)S(1)} %convert_element_type.45.refs_1_, f32[144,128]{1,0:T(8,128)S(1)} %convert_element_type.47.refs_2_, ...), custom_call_target="tpu_custom_call" | custom-call | tf_op jit(solution)/shard_map/last/pallas_call | solution.py:330
  40.3 0.1 collective-permute-done.18
  40.5 0.0 collective-permute-done.19
  40.5 0.9 %collective-permute-done.20 = f32[8,128]{1,0:T(8,128)S(1)} collective-permute-done((f32[8,128]{1,0:T(8,128)S(1)}, f32[8,128]{1,0:T(8,128)S(1)}, u32[]{:S(2)}, u32[]{:S(2)}) %collective-permute-start.20) | collective-permute-done | bytes 4128 | tf_op jit(solution)/shard_map/ppermute | solution.py:199
  41.4 0.1 collective-permute-start.21
  41.5 1.1 %collective-permute-done.21 = f32[8,128]{1,0:T(8,128)S(1)} collective-permute-done((f32[8,128]{1,0:T(8,128)S(1)}, f32[8,128]{1,0:T(8,128)S(1)}, u32[]{:S(2)}, u32[]{:S(2)}) %collective-permute-start.21) | collective-permute-done | bytes 4128 | tf_op jit(solution)/shard_map/ppermute | solution.py:199
  42.6 0.6 %add_multiply_fusion = f32[2,64]{1,0:T(2,128)} fusion(f32[8,128]{1,0:T(8,128)S(1)} %collective-permute-done.21, f32[8,128]{1,0:T(8,128)S(1)} %add_add_fusion), kind=kLoop, calls=%fused_computation.7 | loop fusion | flops 256 | bytes 1536 | tf_op jit(solution)/shard_map/mul | solution.py:343
  (24 shorter events, 0.2 us)
Async XLA Ops:
  1.5 8.2 %collective-permute-start.2 = (bf16[64,256]{1,0:T(8,128)(2,1)S(1)}, bf16[64,256]{1,0:T(8,128)(2,1)S(1)}, u32[]{:S(2)}, u32[]{:S(2)}) collective-permute-start(bf16[64,256]{1,0:T(8,128)(2,1)S(1)} %get-tuple-element.48), channel_id=1, source_target_pairs={{0,28},{4,24},{8,20},{12,16},{16,12},{20,8},{24,4},{28,0},{1,29},{... | collective-permute-start | bytes 98312 | tf_op jit(solution)/shard_map/ppermute | solution.py:199
  4.9 4.8 %collective-permute-start.3 = (bf16[64,256]{1,0:T(8,128)(2,1)S(1)}, bf16[64,256]{1,0:T(8,128)(2,1)S(1)}, u32[]{:S(2)}, u32[]{:S(2)}) collective-permute-start(bf16[64,256]{1,0:T(8,128)(2,1)S(1)} %get-tuple-element.49), channel_id=1, source_target_pairs={{0,20},{4,16},{8,28},{12,24},{16,4},{20,0},{24,12},{28,8},{1,21},{... | collective-permute-start | bytes 98312 | tf_op jit(solution)/shard_map/ppermute | solution.py:199
  5.7 4.4 %collective-permute-start = (bf16[64,256]{1,0:T(8,128)(2,1)S(1)}, bf16[64,256]{1,0:T(8,128)(2,1)S(1)}, u32[]{:S(2)}, u32[]{:S(2)}) collective-permute-start(bf16[64,256]{1,0:T(8,128)(2,1)S(1)} %get-tuple-element.44), channel_id=1, source_target_pairs={{0,12},{4,8},{8,4},{12,0},{16,28},{20,24},{24,20},{28,16},{1,13},{... | collective-permute-start | bytes 98312 | tf_op jit(solution)/shard_map/ppermute | solution.py:199
  5.9 6.2 %collective-permute-start.5 = (bf16[64,256]{1,0:T(8,128)(2,1)S(1)}, bf16[64,256]{1,0:T(8,128)(2,1)S(1)}, u32[]{:S(2)}, u32[]{:S(2)}) collective-permute-start(bf16[64,256]{1,0:T(8,128)(2,1)S(1)} %get-tuple-element.59), channel_id=1, source_target_pairs={{0,1},{1,0},{2,3},{3,2},{4,5},{5,4},{6,7},{7,6},{8,9},{9,8},{10,11... | collective-permute-start | bytes 98312 | tf_op jit(solution)/shard_map/ppermute | solution.py:199
  9.7 1.4 %collective-permute-start.4 = (bf16[3,64,256]{2,1,0:T(8,128)(2,1)S(1)}, bf16[3,64,256]{2,1,0:T(8,128)(2,1)S(1)}, u32[]{:S(2)}, u32[]{:S(2)}) collective-permute-start(bf16[3,64,256]{2,1,0:T(8,128)(2,1)S(1)} %pad_maximum_fusion.2), channel_id=1, source_target_pairs={{0,4},{4,0},{8,12},{12,8},{16,20},{20,16},{24,28},{28,24},{1,5},{5... | collective-permute-start | bytes 294920 | tf_op jit(solution)/shard_map/ppermute | solution.py:199
  10.1 1.7 %collective-permute-start.1 = (bf16[1,64,256]{2,1,0:T(8,128)(2,1)S(1)}, bf16[1,64,256]{2,1,0:T(8,128)(2,1)S(1)}, u32[]{:S(2)}, u32[]{:S(2)}) collective-permute-start(bf16[1,64,256]{2,1,0:T(8,128)(2,1)S(1)} %bitcast.24), channel_id=1, source_target_pairs={{0,4},{4,0},{8,12},{12,8},{16,20},{20,16},{24,28},{28,24},{1,5},{5... | collective-permute-start | bytes 98312 | tf_op jit(solution)/shard_map/ppermute | solution.py:199
  11.1 9.9 %copy-start = (f32[64,256]{1,0:T(8,128)S(1)}, f32[64,256]{1,0:T(8,128)}, u32[]{:S(2)}) copy-start(f32[64,256]{1,0:T(8,128)} %a_5_.1) | copy-start | bytes 196612
  11.1 9.9 %copy-start.1 = (f32[64,256]{1,0:T(8,128)S(1)}, f32[64,256]{1,0:T(8,128)}, u32[]{:S(2)}) copy-start(f32[64,256]{1,0:T(8,128)} %refs_3_.5) | copy-start | bytes 196612
  11.1 9.9 %copy-start.2 = (f32[64,256]{1,0:T(8,128)S(1)}, f32[64,256]{1,0:T(8,128)}, u32[]{:S(2)}) copy-start(f32[64,256]{1,0:T(8,128)} %refs_3_.4) | copy-start | bytes 196612
  12.1 6.2 %collective-permute-start.8 = (f16[128,128]{1,0:T(8,128)(2,1)S(1)}, f16[128,128]{1,0:T(8,128)(2,1)S(1)}, u32[]{:S(2)}, u32[]{:S(2)}) collective-permute-start(f16[128,128]{1,0:T(8,128)(2,1)S(1)} %convert_element_type.40), channel_id=1, source_target_pairs={{0,3},{1,2},{2,1},{3,0},{4,7},{5,6},{6,5},{7,4},{8,11},{9,10},{10,... | collective-permute-start | bytes 98312 | tf_op jit(solution)/shard_map/ppermute | solution.py:199
  14.9 6.0 %collective-permute-start.7 = (f16[128,128]{1,0:T(8,128)(2,1)S(1)}, f16[128,128]{1,0:T(8,128)(2,1)S(1)}, u32[]{:S(2)}, u32[]{:S(2)}) collective-permute-start(f16[128,128]{1,0:T(8,128)(2,1)S(1)} %convert_element_type.38), channel_id=1, source_target_pairs={{0,2},{1,3},{2,0},{3,1},{4,6},{5,7},{6,4},{7,5},{8,10},{9,11},{10,... | collective-permute-start | bytes 98312 | tf_op jit(solution)/shard_map/ppermute | solution.py:199
  14.9 6.0 %collective-permute-start.6 = (f16[128,128]{1,0:T(8,128)(2,1)S(1)}, f16[128,128]{1,0:T(8,128)(2,1)S(1)}, u32[]{:S(2)}, u32[]{:S(2)}) collective-permute-start(f16[128,128]{1,0:T(8,128)(2,1)S(1)} %convert_element_type.36), channel_id=1, source_target_pairs={{0,1},{1,0},{2,3},{3,2},{4,5},{5,4},{6,7},{7,6},{8,9},{9,8},{10,11... | collective-permute-start | bytes 98312 | tf_op jit(solution)/shard_map/ppermute | solution.py:199
  16.5 7.6 %collective-permute-start.10 = (bf16[2,64,256]{2,1,0:T(8,128)(2,1)S(1)}, bf16[2,64,256]{2,1,0:T(8,128)(2,1)S(1)}, u32[]{:S(2)}, u32[]{:S(2)}) collective-permute-start(bf16[2,64,256]{2,1,0:T(8,128)(2,1)S(1)} %pad_maximum_fusion.3), channel_id=1, source_target_pairs={{0,2},{1,3},{2,0},{3,1},{4,6},{5,7},{6,4},{7,5},{8,10},{9,11},{10,... | collective-permute-start | bytes 196616 | tf_op jit(solution)/shard_map/ppermute | solution.py:199
  21.1 4.3 %collective-permute-start.9 = (bf16[64,256]{1,0:T(8,128)(2,1)S(1)}, bf16[64,256]{1,0:T(8,128)(2,1)S(1)}, u32[]{:S(2)}, u32[]{:S(2)}) collective-permute-start(bf16[64,256]{1,0:T(8,128)(2,1)S(1)} %get-tuple-element.58), channel_id=1, source_target_pairs={{0,28},{4,24},{8,20},{12,16},{16,12},{20,8},{24,4},{28,0},{1,29},{... | collective-permute-start | bytes 98312 | tf_op jit(solution)/shard_map/ppermute | solution.py:199
  21.9 4.1 %collective-permute-start.11 = (bf16[64,256]{1,0:T(8,128)(2,1)S(1)}, bf16[64,256]{1,0:T(8,128)(2,1)S(1)}, u32[]{:S(2)}, u32[]{:S(2)}) collective-permute-start(bf16[64,256]{1,0:T(8,128)(2,1)S(1)} %get-tuple-element.62), channel_id=1, source_target_pairs={{0,20},{4,16},{8,28},{12,24},{16,4},{20,0},{24,12},{28,8},{1,21},{... | collective-permute-start | bytes 98312 | tf_op jit(solution)/shard_map/ppermute | solution.py:199
  24.1 3.3 %collective-permute-start.12 = (bf16[64,256]{1,0:T(8,128)(2,1)S(1)}, bf16[64,256]{1,0:T(8,128)(2,1)S(1)}, u32[]{:S(2)}, u32[]{:S(2)}) collective-permute-start(bf16[64,256]{1,0:T(8,128)(2,1)S(1)} %get-tuple-element.63), channel_id=1, source_target_pairs={{0,12},{4,8},{8,4},{12,0},{16,28},{20,24},{24,20},{28,16},{1,13},{... | collective-permute-start | bytes 98312 | tf_op jit(solution)/shard_map/ppermute | solution.py:199
  25.5 2.1 %collective-permute-start.14 = (bf16[2,64,256]{2,1,0:T(8,128)(2,1)S(1)}, bf16[2,64,256]{2,1,0:T(8,128)(2,1)S(1)}, u32[]{:S(2)}, u32[]{:S(2)}) collective-permute-start(bf16[2,64,256]{2,1,0:T(8,128)(2,1)S(1)} %pad_maximum_fusion.5.vectors), channel_id=1, source_target_pairs={{0,4},{4,0},{8,12},{12,8},{16,20},{20,16},{24,28},{28,24},{1,5},{5... | collective-permute-start | bytes 196616 | tf_op jit(solution)/shard_map/ppermute | solution.py:199
  27.5 1.3 %collective-permute-start.13 = (bf16[2,64,256]{2,1,0:T(8,128)(2,1)S(1)}, bf16[2,64,256]{2,1,0:T(8,128)(2,1)S(1)}, u32[]{:S(2)}, u32[]{:S(2)}) collective-permute-start(bf16[2,64,256]{2,1,0:T(8,128)(2,1)S(1)} %pad_maximum_fusion.4), channel_id=1, source_target_pairs={{0,4},{4,0},{8,12},{12,8},{16,20},{20,16},{24,28},{28,24},{1,5},{5... | collective-permute-start | bytes 196616 | tf_op jit(solution)/shard_map/ppermute | solution.py:199
  27.6 11.5 %copy-start.3 = (f32[64,256]{1,0:T(8,128)S(1)}, f32[64,256]{1,0:T(8,128)}, u32[]{:S(2)}) copy-start(f32[64,256]{1,0:T(8,128)} %value.1.refs_4_) | copy-start | bytes 196612
  27.6 11.5 %copy-start.4 = (f32[64,256]{1,0:T(8,128)S(1)}, f32[64,256]{1,0:T(8,128)}, u32[]{:S(2)}) copy-start(f32[64,256]{1,0:T(8,128)} %refs_5_.3) | copy-start | bytes 196612
  27.6 11.5 %copy-start.5 = (f32[2]{0:T(128)S(1)}, f32[2]{0:T(128)}, u32[]{:S(2)}) copy-start(f32[2]{0:T(128)} %coeffs.1) | copy-start | bytes 28
  29.4 6.0 %collective-permute-start.17 = (f16[144,128]{1,0:T(8,128)(2,1)S(1)}, f16[144,128]{1,0:T(8,128)(2,1)S(1)}, u32[]{:S(2)}, u32[]{:S(2)}) collective-permute-start(f16[144,128]{1,0:T(8,128)(2,1)S(1)} %convert_element_type.46), channel_id=1, source_target_pairs={{0,3},{1,2},{2,1},{3,0},{4,7},{5,6},{6,5},{7,4},{8,11},{9,10},{10,... | collective-permute-start | bytes 110600 | tf_op jit(solution)/shard_map/ppermute | solution.py:199
  31.1 4.7 %collective-permute-start.16 = (f16[144,128]{1,0:T(8,128)(2,1)S(1)}, f16[144,128]{1,0:T(8,128)(2,1)S(1)}, u32[]{:S(2)}, u32[]{:S(2)}) collective-permute-start(f16[144,128]{1,0:T(8,128)(2,1)S(1)} %convert_element_type.44), channel_id=1, source_target_pairs={{0,1},{1,0},{2,3},{3,2},{4,5},{5,4},{6,7},{7,6},{8,9},{9,8},{10,11... | collective-permute-start | bytes 110600 | tf_op jit(solution)/shard_map/ppermute | solution.py:199
  31.2 5.3 %collective-permute-start.15 = (f16[144,128]{1,0:T(8,128)(2,1)S(1)}, f16[144,128]{1,0:T(8,128)(2,1)S(1)}, u32[]{:S(2)}, u32[]{:S(2)}) collective-permute-start(f16[144,128]{1,0:T(8,128)(2,1)S(1)} %convert_element_type.42), channel_id=1, source_target_pairs={{0,2},{1,3},{2,0},{3,1},{4,6},{5,7},{6,4},{7,5},{8,10},{9,11},{10,... | collective-permute-start | bytes 110600 | tf_op jit(solution)/shard_map/ppermute | solution.py:199
  36.5 4.0 %collective-permute-start.18 = (f32[8,128]{1,0:T(8,128)S(1)}, f32[8,128]{1,0:T(8,128)S(1)}, u32[]{:S(2)}, u32[]{:S(2)}) collective-permute-start(f32[8,128]{1,0:T(8,128)S(1)} %get-tuple-element.72), channel_id=1, source_target_pairs={{0,28},{4,24},{8,20},{12,16},{16,12},{20,8},{24,4},{28,0},{1,29},{... | collective-permute-start | bytes 12296 | tf_op jit(solution)/shard_map/ppermute | solution.py:199
  36.6 3.9 %collective-permute-start.19 = (f32[8,128]{1,0:T(8,128)S(1)}, f32[8,128]{1,0:T(8,128)S(1)}, u32[]{:S(2)}, u32[]{:S(2)}) collective-permute-start(f32[8,128]{1,0:T(8,128)S(1)} %get-tuple-element.73), channel_id=1, source_target_pairs={{0,20},{4,16},{8,28},{12,24},{16,4},{20,0},{24,12},{28,8},{1,21},{... | collective-permute-start | bytes 12296 | tf_op jit(solution)/shard_map/ppermute | solution.py:199
  38.3 3.1 %collective-permute-start.20 = (f32[8,128]{1,0:T(8,128)S(1)}, f32[8,128]{1,0:T(8,128)S(1)}, u32[]{:S(2)}, u32[]{:S(2)}) collective-permute-start(f32[8,128]{1,0:T(8,128)S(1)} %get-tuple-element.74), channel_id=1, source_target_pairs={{0,12},{4,8},{8,4},{12,0},{16,28},{20,24},{24,20},{28,16},{1,13},{... | collective-permute-start | bytes 12296 | tf_op jit(solution)/shard_map/ppermute | solution.py:199
  41.4 1.2 %collective-permute-start.21 = (f32[8,128]{1,0:T(8,128)S(1)}, f32[8,128]{1,0:T(8,128)S(1)}, u32[]{:S(2)}, u32[]{:S(2)}) collective-permute-start(f32[8,128]{1,0:T(8,128)S(1)} %add_add_fusion), channel_id=1, source_target_pairs={{0,4},{4,0},{8,12},{12,8},{16,20},{20,16},{24,28},{28,24},{1,5},{5... | collective-permute-start | bytes 12296 | tf_op jit(solution)/shard_map/ppermute | solution.py:199

commit v6 on v4

--- a/solution.py
+++ b/solution.py
@@ -14,7 +14,7 @@
 F32, BF16 = jnp.float32, jnp.bfloat16
 LANES = 128
 ORDER1 = [3, 2, 1]
-ORDER2 = [2, 3, 1]
+ORDER2 = [3, 1, 2]
 FAR_A, FAR_C, FAR_M = [6, 4, 2], [6, 4, 2], [6, 4, 2]
 
 
@@ -337,8 +337,9 @@
     got, t_after, accum_out = barrier((got, t_after, accum_out))
     for one in got:
         total = total + one
-    total = total + swap(total, "row", 1)
-    moments = total[:2, :count] * float(total_rows) ** (-0.5)
+    scale = float(total_rows) ** (-0.5)
+    other = swap(total, "row", 1)
+    moments = (total[:2, :count] + other[:2, :count]) * scale
     return (t_next, t_after, accum_out, moments)
 
 

time: 42.6 us -> 42.6 us (level)
  waiting for transfers between devices: 10.6 us -> 9.67 us
  starting transfers between devices: 21.8 us -> 22.7 us
    ppermute x22, waiting for transfers between devices: 10.6 us -> 9.67 us  [swap(): return lax.ppermute(x, axis, [(i, i ^ k) for i in range(n)])]
    ppermute x22, starting transfers between devices: 21.8 us -> 22.7 us  [swap(): return lax.ppermute(x, axis, [(i, i ^ k) for i in range(n)])]
  transfers between devices with their start and end apart: 22 -> 22, of which waited for: 8 -> 10; matrix products, arithmetic and copies ran while one was open for 0% -> 0% of each run, Pallas kernels for 15% -> 15%
where the time goes in v6:
time: 42.6 us; the launch traced here: 42.4 us
  starting transfers between devices  22.7 us (53%)
  waiting for transfers between devices  9.67 us (23%)
  Pallas kernels  7.86 us (18%)
  between operations  1.47 us (3%)
  other arithmetic  0.64 us (2%)
    ppermute x22, starting transfers between devices, swap(): return lax.ppermute(x, axis, [(i, i ^ k) for i in range(n)])  22.7 us
    ppermute x22, waiting for transfers between devices, swap(): return lax.ppermute(x, axis, [(i, i ^ k) for i in range(n)])  9.67 us
    pallas_call x1, Pallas kernels, local(): call(functools.partial(place_kernel, pb, group), shape(n_row * pb, n_col...  1.6 us
    pallas_call x2, Pallas kernels, multiply(): call(functools.partial(more_kernel, pb, both[n_first:len(order) + n_early...  1.35 us
    pallas_call x1, Pallas kernels, local(): call(functools.partial(last_kernel, n_col), [shape(count, width), shape(c...  1.22 us
    pallas_call x2, Pallas kernels, multiply(): call(functools.partial(start_kernel, pb, both[:n_first]), sums, [VMEM] *...  1.18 us
    pallas_call x1, Pallas kernels, local(): call(cast_kernel, [shape(count, width, dtype=BF16)] * (1 + n_out), [HBM]...  0.9 us
  transfers between devices with their start and end apart: 22, of which 10 were waited for; matrix products, arithmetic and copies ran while one was open for 0% of the time, Pallas kernels for 15%

profile of v6, /device:TPU:0, one launch (start us, length us, event | category | flops | bytes accessed | tf_op | source)
XLA Modules:
  0.0 42.4 jit_solution(5791062678235008707)
XLA Ops:
  0.6 0.9 %cast.1 = (bf16[64,256]{1,0:T(8,128)(2,1)S(1)}, bf16[64,256]{1,0:T(8,128)(2,1)S(1)}, bf16[64,256]{1,0:T(8,128)(2,1)S(1)}, bf16[64,256]{1,0:T(8,128)(2,1)S(1)}, bf16[64,256]{1,0:T(8,128)(2,1)S(1)}) custom-call(f32[64,256]{1,0:T(8,128)} %refs_3_.5, f32[64,256]{1,0:T(8,128)} %a_5_.1), custom_call_target="tpu_custom_call" | custom-call | tf_op jit(solution)/shard_map/cast/pallas_call | solution.py:273
  1.5 3.4 %collective-permute-start.2 = (bf16[64,256]{1,0:T(8,128)(2,1)S(1)}, bf16[64,256]{1,0:T(8,128)(2,1)S(1)}, u32[]{:S(2)}, u32[]{:S(2)}) collective-permute-start(bf16[64,256]{1,0:T(8,128)(2,1)S(1)} %get-tuple-element.48), channel_id=1, source_target_pairs={{0,28},{4,24},{8,20},{12,16},{16,12},{20,8},{24,4},{28,0},{1,29},{... | collective-permute-start | bytes 98312 | tf_op jit(solution)/shard_map/ppermute | solution.py:198
  4.9 0.8 %collective-permute-start.3 = (bf16[64,256]{1,0:T(8,128)(2,1)S(1)}, bf16[64,256]{1,0:T(8,128)(2,1)S(1)}, u32[]{:S(2)}, u32[]{:S(2)}) collective-permute-start(bf16[64,256]{1,0:T(8,128)(2,1)S(1)} %get-tuple-element.49), channel_id=1, source_target_pairs={{0,20},{4,16},{8,28},{12,24},{16,4},{20,0},{24,12},{28,8},{1,21},{... | collective-permute-start | bytes 98312 | tf_op jit(solution)/shard_map/ppermute | solution.py:198
  5.7 0.1 collective-permute-start
  5.9 1.6 %collective-permute-start.5 = (bf16[64,256]{1,0:T(8,128)(2,1)S(1)}, bf16[64,256]{1,0:T(8,128)(2,1)S(1)}, u32[]{:S(2)}, u32[]{:S(2)}) collective-permute-start(bf16[64,256]{1,0:T(8,128)(2,1)S(1)} %get-tuple-element.59), channel_id=1, source_target_pairs={{0,1},{1,0},{2,3},{3,2},{4,5},{5,4},{6,7},{7,6},{8,9},{9,8},{10,11... | collective-permute-start | bytes 98312 | tf_op jit(solution)/shard_map/ppermute | solution.py:198
  8.1 1.6 %place.1.dense.a_1_ = bf16[16,1024,128]{2,1,0:T(8,128)(2,1)S(1)} custom-call(s32[1,1]{1,0:T(1,128)S(6)} %copy.13.count, s32[1,1,64]{2,1,0:T(1,128)} %rows_in.1, s32[1,1,64]{2,1,0:T(1,128)} %cols_in.1, bf16[1,1,64,128,128]{4,3,2,1,0:T(8,128)(2,1)} %blocks.1), custom_call_target="tpu_custom_call" | custom-call | tf_op jit(solution)/shard_map/place/pallas_call | solution.py:219
  9.7 0.0 collective-permute-done.2
  9.7 0.0 collective-permute-done.3
  9.7 0.3 collective-permute-start.4
  10.0 0.0 collective-permute-done
  10.0 0.3 collective-permute-start.1
  10.3 0.7 %first_start.1.before = f32[4,64,256]{2,1,0:T(8,128)S(1)} custom-call(bf16[4,64,256]{2,1,0:T(8,128)(2,1)S(1)} %pad_maximum_fusion.vectors, bf16[16,1024,128]{2,1,0:T(8,128)(2,1)S(1)} %place.1.dense.a_1_), custom_call_target="tpu_custom_call" | custom-call | tf_op jit(solution)/shard_map/first_start/pallas_call | solution.py:248
  11.1 0.0 copy-start
  11.1 0.0 copy-start.1
  11.1 0.0 copy-start.2
  11.1 0.0 collective-permute-done.4.vectors
  11.1 0.6 %first_more.1.before = f32[4,64,256]{2,1,0:T(8,128)S(1)} custom-call(bf16[3,64,256]{2,1,0:T(8,128)(2,1)S(1)} %collective-permute-done.4.vectors, bf16[16,1024,128]{2,1,0:T(8,128)(2,1)S(1)} %place.1.dense.a_1_, f32[4,64,256]{2,1,0:T(8,128)S(1)} %first_start.1.before), custom_call_target="tpu_custom_call" | custom-call | tf_op jit(solution)/shard_map/first_more/pallas_call | solution.py:251
  11.7 0.0 collective-permute-done.1.vectors
  11.7 0.3 first_end.1
  12.0 0.0 collective-permute-done.5.a_6_
  12.0 2.8 %collective-permute-start.6 = (bf16[128,128]{1,0:T(8,128)(2,1)S(1)}, bf16[128,128]{1,0:T(8,128)(2,1)S(1)}, u32[]{:S(2)}, u32[]{:S(2)}) collective-permute-start(bf16[128,128]{1,0:T(8,128)(2,1)S(1)} %get-tuple-element.55), channel_id=1, source_target_pairs={{0,3},{1,2},{2,1},{3,0},{4,7},{5,6},{6,5},{7,4},{8,11},{9,10},{10,... | collective-permute-start | bytes 98312 | tf_op jit(solution)/shard_map/ppermute | solution.py:198
  14.9 0.0 collective-permute-start.7
  14.9 1.6 %collective-permute-start.8 = (bf16[128,128]{1,0:T(8,128)(2,1)S(1)}, bf16[128,128]{1,0:T(8,128)(2,1)S(1)}, u32[]{:S(2)}, u32[]{:S(2)}) collective-permute-start(bf16[128,128]{1,0:T(8,128)(2,1)S(1)} %get-tuple-element.57), channel_id=1, source_target_pairs={{0,1},{1,0},{2,3},{3,2},{4,5},{5,4},{6,7},{7,6},{8,9},{9,8},{10,11... | collective-permute-start | bytes 98312 | tf_op jit(solution)/shard_map/ppermute | solution.py:198
  16.5 1.8 %collective-permute-start.10 = (bf16[2,64,256]{2,1,0:T(8,128)(2,1)S(1)}, bf16[2,64,256]{2,1,0:T(8,128)(2,1)S(1)}, u32[]{:S(2)}, u32[]{:S(2)}) collective-permute-start(bf16[2,64,256]{2,1,0:T(8,128)(2,1)S(1)} %pad_maximum_fusion.3), channel_id=1, source_target_pairs={{0,2},{1,3},{2,0},{3,1},{4,6},{5,7},{6,4},{7,5},{8,10},{9,11},{10,... | collective-permute-start | bytes 196616 | tf_op jit(solution)/shard_map/ppermute | solution.py:198
  18.3 0.0 collective-permute-done.6.refs_0_
  18.3 2.7 %collective-permute-done.7.refs_1_ = bf16[128,128]{1,0:T(8,128)(2,1)S(1)} collective-permute-done((bf16[128,128]{1,0:T(8,128)(2,1)S(1)}, bf16[128,128]{1,0:T(8,128)(2,1)S(1)}, u32[]{:S(2)}, u32[]{:S(2)}) %collective-permute-start.7) | collective-permute-done | bytes 32800 | tf_op jit(solution)/shard_map/ppermute | solution.py:198
  21.0 0.0 collective-permute-done.8.refs_2_
  21.0 0.0 copy-done
  21.0 0.1 next.1
  21.1 0.1 collective-permute-start.9
  21.2 2.2 %collective-permute-start.11 = (bf16[64,256]{1,0:T(8,128)(2,1)S(1)}, bf16[64,256]{1,0:T(8,128)(2,1)S(1)}, u32[]{:S(2)}, u32[]{:S(2)}) collective-permute-start(bf16[64,256]{1,0:T(8,128)(2,1)S(1)} %get-tuple-element.62), channel_id=1, source_target_pairs={{0,20},{4,16},{8,28},{12,24},{16,4},{20,0},{24,12},{28,8},{1,21},{... | collective-permute-start | bytes 98312 | tf_op jit(solution)/shard_map/ppermute | solution.py:198
  23.4 0.1 collective-permute-start.12
  23.6 0.7 %value.1.refs_4_ = f32[64,256]{1,0:T(8,128)} custom-call(f32[64,256]{1,0:T(8,128)S(1)} %get-tuple-element.50.own, bf16[128,128]{1,0:T(8,128)(2,1)S(1)} %collective-permute-done.6.refs_0_, bf16[128,128]{1,0:T(8,128)(2,1)S(1)} %collective-permute-done.7.refs_1_, bf16[128,128]{1,0:T(8,128)(2,1)S(1)} %collective-permute-done.8.refs_2_, f32[64,256]{1,0:T(8,128)S(1)} %copy-done.2), custom_call_target="tpu_custom_call" | custom-call | tf_op jit(solution)/shard_map/value/pallas_call | solution.py:307
  24.2 0.0 collective-permute-done.10.a_4_
  24.2 1.3 %collective-permute-done.9 = bf16[64,256]{1,0:T(8,128)(2,1)S(1)} collective-permute-done((bf16[64,256]{1,0:T(8,128)(2,1)S(1)}, bf16[64,256]{1,0:T(8,128)(2,1)S(1)}, u32[]{:S(2)}, u32[]{:S(2)}) %collective-permute-start.9) | collective-permute-done | bytes 32800 | tf_op jit(solution)/shard_map/ppermute | solution.py:198
  25.6 0.1 collective-permute-start.14
  25.6 0.4 %second_start.1.before = f32[4,64,256]{2,1,0:T(8,128)S(1)} custom-call(bf16[2,64,256]{2,1,0:T(8,128)(2,1)S(1)} %pad_maximum_fusion.5.vectors, bf16[16,1024,128]{2,1,0:T(8,128)(2,1)S(1)} %place.1.dense.a_1_), custom_call_target="tpu_custom_call" | custom-call | tf_op jit(solution)/shard_map/second_start/pallas_call | solution.py:248
  26.1 0.0 collective-permute-done.11
  26.1 1.0 %collective-permute-done.12 = bf16[64,256]{1,0:T(8,128)(2,1)S(1)} collective-permute-done((bf16[64,256]{1,0:T(8,128)(2,1)S(1)}, bf16[64,256]{1,0:T(8,128)(2,1)S(1)}, u32[]{:S(2)}, u32[]{:S(2)}) %collective-permute-start.12) | collective-permute-done | bytes 32800 | tf_op jit(solution)/shard_map/ppermute | solution.py:198
  27.0 0.2 collective-permute-start.13
  27.2 0.0 collective-permute-done.14
  27.3 0.0 copy-start.3
  27.3 0.0 copy-start.4
  27.3 0.0 copy-start.5
  27.3 0.8 %second_more.1.a_2_ = f32[4,64,256]{2,1,0:T(8,128)S(1)} custom-call(bf16[4,64,256]{2,1,0:T(8,128)(2,1)S(1)} %pad_maximum_fusion.1.vectors, bf16[16,1024,128]{2,1,0:T(8,128)(2,1)S(1)} %place.1.dense.a_1_, f32[4,64,256]{2,1,0:T(8,128)S(1)} %second_start.1.before), custom_call_target="tpu_custom_call" | custom-call | tf_op jit(solution)/shard_map/second_more/pallas_call | solution.py:251
  28.0 0.3 collective-permute-done.13.a_0_
  28.4 0.5 %second_end.1 = (f32[64,256]{1,0:T(8,128)S(1)}, bf16[144,128]{1,0:T(8,128)(2,1)S(1)}, bf16[144,128]{1,0:T(8,128)(2,1)S(1)}, bf16[144,128]{1,0:T(8,128)(2,1)S(1)}, f32[8,128]{1,0:T(8,128)S(1)}) custom-call(bf16[2,64,256]{2,1,0:T(8,128)(2,1)S(1)} %collective-permute-done.13.a_0_, bf16[16,1024,128]{2,1,0:T(8,128)(2,1)S(1)} %place.1.dense.a_1_, ...), custom_call_target="tpu_custom_call" | custom-call | tf_op jit(solution)/shard_map/second_end/pallas_call | solution.py:259
  28.9 1.4 %collective-permute-start.15 = (bf16[144,128]{1,0:T(8,128)(2,1)S(1)}, bf16[144,128]{1,0:T(8,128)(2,1)S(1)}, u32[]{:S(2)}, u32[]{:S(2)}) collective-permute-start(bf16[144,128]{1,0:T(8,128)(2,1)S(1)} %get-tuple-element.69), channel_id=1, source_target_pairs={{0,3},{1,2},{2,1},{3,0},{4,7},{5,6},{6,5},{7,4},{8,11},{9,10},{10,... | collective-permute-start | bytes 110600 | tf_op jit(solution)/shard_map/ppermute | solution.py:198
  30.3 0.1 collective-permute-start.16
  30.4 3.0 %collective-permute-start.17 = (bf16[144,128]{1,0:T(8,128)(2,1)S(1)}, bf16[144,128]{1,0:T(8,128)(2,1)S(1)}, u32[]{:S(2)}, u32[]{:S(2)}) collective-permute-start(bf16[144,128]{1,0:T(8,128)(2,1)S(1)} %get-tuple-element.71), channel_id=1, source_target_pairs={{0,2},{1,3},{2,0},{3,1},{4,6},{5,7},{6,4},{7,5},{8,10},{9,11},{10,... | collective-permute-start | bytes 110600 | tf_op jit(solution)/shard_map/ppermute | solution.py:198
  33.4 1.4 %collective-permute-done.15.refs_0_ = bf16[144,128]{1,0:T(8,128)(2,1)S(1)} collective-permute-done((bf16[144,128]{1,0:T(8,128)(2,1)S(1)}, bf16[144,128]{1,0:T(8,128)(2,1)S(1)}, u32[]{:S(2)}, u32[]{:S(2)}) %collective-permute-start.15) | collective-permute-done | bytes 36896 | tf_op jit(solution)/shard_map/ppermute | solution.py:198
  34.8 0.5 %collective-permute-done.16.refs_1_ = bf16[144,128]{1,0:T(8,128)(2,1)S(1)} collective-permute-done((bf16[144,128]{1,0:T(8,128)(2,1)S(1)}, bf16[144,128]{1,0:T(8,128)(2,1)S(1)}, u32[]{:S(2)}, u32[]{:S(2)}) %collective-permute-start.16) | collective-permute-done | bytes 36896 | tf_op jit(solution)/shard_map/ppermute | solution.py:198
  35.3 0.4 collective-permute-done.17.refs_2_
  35.7 0.1 collective-permute-start.18
  35.8 1.8 %collective-permute-start.19 = (f32[8,128]{1,0:T(8,128)S(1)}, f32[8,128]{1,0:T(8,128)S(1)}, u32[]{:S(2)}, u32[]{:S(2)}) collective-permute-start(f32[8,128]{1,0:T(8,128)S(1)} %get-tuple-element.73), channel_id=1, source_target_pairs={{0,20},{4,16},{8,28},{12,24},{16,4},{20,0},{24,12},{28,8},{1,21},{... | collective-permute-start | bytes 12296 | tf_op jit(solution)/shard_map/ppermute | solution.py:198
  37.6 0.7 %collective-permute-start.20 = (f32[8,128]{1,0:T(8,128)S(1)}, f32[8,128]{1,0:T(8,128)S(1)}, u32[]{:S(2)}, u32[]{:S(2)}) collective-permute-start(f32[8,128]{1,0:T(8,128)S(1)} %get-tuple-element.74), channel_id=1, source_target_pairs={{0,12},{4,8},{8,4},{12,0},{16,28},{20,24},{24,20},{28,16},{1,13},{... | collective-permute-start | bytes 12296 | tf_op jit(solution)/shard_map/ppermute | solution.py:198
  38.3 0.0 copy-done.4
  38.3 1.2 %last.1 = (f32[64,256]{1,0:T(8,128)}, f32[64,256]{1,0:T(8,128)}) custom-call(f32[2]{0:T(128)S(1)} %copy-done.5, f32[64,256]{1,0:T(8,128)S(1)} %get-tuple-element.75.own, bf16[144,128]{1,0:T(8,128)(2,1)S(1)} %collective-permute-done.15.refs_0_, bf16[144,128]{1,0:T(8,128)(2,1)S(1)} %collective-permute-done.16.refs_1_, ...), custom_call_target="tpu_custom_call" | custom-call | tf_op jit(solution)/shard_map/last/pallas_call | solution.py:329
  39.5 0.1 collective-permute-done.18
  39.7 0.0 collective-permute-done.19
  39.7 1.0 %collective-permute-done.20 = f32[8,128]{1,0:T(8,128)S(1)} collective-permute-done((f32[8,128]{1,0:T(8,128)S(1)}, f32[8,128]{1,0:T(8,128)S(1)}, u32[]{:S(2)}, u32[]{:S(2)}) %collective-permute-start.20) | collective-permute-done | bytes 4128 | tf_op jit(solution)/shard_map/ppermute | solution.py:198
  40.6 0.2 collective-permute-start.21
  40.8 1.0 %collective-permute-done.21 = f32[8,128]{1,0:T(8,128)S(1)} collective-permute-done((f32[8,128]{1,0:T(8,128)S(1)}, f32[8,128]{1,0:T(8,128)S(1)}, u32[]{:S(2)}, u32[]{:S(2)}) %collective-permute-start.21) | collective-permute-done | bytes 4128 | tf_op jit(solution)/shard_map/ppermute | solution.py:198
  41.8 0.6 %add_multiply_fusion = f32[2,64]{1,0:T(2,128)} fusion(f32[8,128]{1,0:T(8,128)S(1)} %collective-permute-done.21, f32[8,128]{1,0:T(8,128)S(1)} %add_add_fusion), kind=kLoop, calls=%fused_computation.7 | loop fusion | flops 256 | bytes 1536 | tf_op jit(solution)/shard_map/mul | solution.py:342
  (12 shorter events, 0.1 us)
Async XLA Ops:
  1.5 8.2 %collective-permute-start.2 = (bf16[64,256]{1,0:T(8,128)(2,1)S(1)}, bf16[64,256]{1,0:T(8,128)(2,1)S(1)}, u32[]{:S(2)}, u32[]{:S(2)}) collective-permute-start(bf16[64,256]{1,0:T(8,128)(2,1)S(1)} %get-tuple-element.48), channel_id=1, source_target_pairs={{0,28},{4,24},{8,20},{12,16},{16,12},{20,8},{24,4},{28,0},{1,29},{... | collective-permute-start | bytes 98312 | tf_op jit(solution)/shard_map/ppermute | solution.py:198
  4.9 4.8 %collective-permute-start.3 = (bf16[64,256]{1,0:T(8,128)(2,1)S(1)}, bf16[64,256]{1,0:T(8,128)(2,1)S(1)}, u32[]{:S(2)}, u32[]{:S(2)}) collective-permute-start(bf16[64,256]{1,0:T(8,128)(2,1)S(1)} %get-tuple-element.49), channel_id=1, source_target_pairs={{0,20},{4,16},{8,28},{12,24},{16,4},{20,0},{24,12},{28,8},{1,21},{... | collective-permute-start | bytes 98312 | tf_op jit(solution)/shard_map/ppermute | solution.py:198
  5.7 4.3 %collective-permute-start = (bf16[64,256]{1,0:T(8,128)(2,1)S(1)}, bf16[64,256]{1,0:T(8,128)(2,1)S(1)}, u32[]{:S(2)}, u32[]{:S(2)}) collective-permute-start(bf16[64,256]{1,0:T(8,128)(2,1)S(1)} %get-tuple-element.44), channel_id=1, source_target_pairs={{0,12},{4,8},{8,4},{12,0},{16,28},{20,24},{24,20},{28,16},{1,13},{... | collective-permute-start | bytes 98312 | tf_op jit(solution)/shard_map/ppermute | solution.py:198
  5.9 6.2 %collective-permute-start.5 = (bf16[64,256]{1,0:T(8,128)(2,1)S(1)}, bf16[64,256]{1,0:T(8,128)(2,1)S(1)}, u32[]{:S(2)}, u32[]{:S(2)}) collective-permute-start(bf16[64,256]{1,0:T(8,128)(2,1)S(1)} %get-tuple-element.59), channel_id=1, source_target_pairs={{0,1},{1,0},{2,3},{3,2},{4,5},{5,4},{6,7},{7,6},{8,9},{9,8},{10,11... | collective-permute-start | bytes 98312 | tf_op jit(solution)/shard_map/ppermute | solution.py:198
  9.7 1.4 %collective-permute-start.4 = (bf16[3,64,256]{2,1,0:T(8,128)(2,1)S(1)}, bf16[3,64,256]{2,1,0:T(8,128)(2,1)S(1)}, u32[]{:S(2)}, u32[]{:S(2)}) collective-permute-start(bf16[3,64,256]{2,1,0:T(8,128)(2,1)S(1)} %pad_maximum_fusion.2), channel_id=1, source_target_pairs={{0,4},{4,0},{8,12},{12,8},{16,20},{20,16},{24,28},{28,24},{1,5},{5... | collective-permute-start | bytes 294920 | tf_op jit(solution)/shard_map/ppermute | solution.py:198
  10.0 1.7 %collective-permute-start.1 = (bf16[1,64,256]{2,1,0:T(8,128)(2,1)S(1)}, bf16[1,64,256]{2,1,0:T(8,128)(2,1)S(1)}, u32[]{:S(2)}, u32[]{:S(2)}) collective-permute-start(bf16[1,64,256]{2,1,0:T(8,128)(2,1)S(1)} %bitcast.24), channel_id=1, source_target_pairs={{0,4},{4,0},{8,12},{12,8},{16,20},{20,16},{24,28},{28,24},{1,5},{5... | collective-permute-start | bytes 98312 | tf_op jit(solution)/shard_map/ppermute | solution.py:198
  11.1 9.9 %copy-start = (f32[64,256]{1,0:T(8,128)S(1)}, f32[64,256]{1,0:T(8,128)}, u32[]{:S(2)}) copy-start(f32[64,256]{1,0:T(8,128)} %a_5_.1) | copy-start | bytes 196612
  11.1 9.9 %copy-start.1 = (f32[64,256]{1,0:T(8,128)S(1)}, f32[64,256]{1,0:T(8,128)}, u32[]{:S(2)}) copy-start(f32[64,256]{1,0:T(8,128)} %refs_3_.5) | copy-start | bytes 196612
  11.1 9.9 %copy-start.2 = (f32[64,256]{1,0:T(8,128)S(1)}, f32[64,256]{1,0:T(8,128)}, u32[]{:S(2)}) copy-start(f32[64,256]{1,0:T(8,128)} %refs_3_.4) | copy-start | bytes 196612
  12.0 6.3 %collective-permute-start.6 = (bf16[128,128]{1,0:T(8,128)(2,1)S(1)}, bf16[128,128]{1,0:T(8,128)(2,1)S(1)}, u32[]{:S(2)}, u32[]{:S(2)}) collective-permute-start(bf16[128,128]{1,0:T(8,128)(2,1)S(1)} %get-tuple-element.55), channel_id=1, source_target_pairs={{0,3},{1,2},{2,1},{3,0},{4,7},{5,6},{6,5},{7,4},{8,11},{9,10},{10,... | collective-permute-start | bytes 98312 | tf_op jit(solution)/shard_map/ppermute | solution.py:198
  14.9 6.1 %collective-permute-start.7 = (bf16[128,128]{1,0:T(8,128)(2,1)S(1)}, bf16[128,128]{1,0:T(8,128)(2,1)S(1)}, u32[]{:S(2)}, u32[]{:S(2)}) collective-permute-start(bf16[128,128]{1,0:T(8,128)(2,1)S(1)} %get-tuple-element.56), channel_id=1, source_target_pairs={{0,2},{1,3},{2,0},{3,1},{4,6},{5,7},{6,4},{7,5},{8,10},{9,11},{10,... | collective-permute-start | bytes 98312 | tf_op jit(solution)/shard_map/ppermute | solution.py:198
  14.9 6.1 %collective-permute-start.8 = (bf16[128,128]{1,0:T(8,128)(2,1)S(1)}, bf16[128,128]{1,0:T(8,128)(2,1)S(1)}, u32[]{:S(2)}, u32[]{:S(2)}) collective-permute-start(bf16[128,128]{1,0:T(8,128)(2,1)S(1)} %get-tuple-element.57), channel_id=1, source_target_pairs={{0,1},{1,0},{2,3},{3,2},{4,5},{5,4},{6,7},{7,6},{8,9},{9,8},{10,11... | collective-permute-start | bytes 98312 | tf_op jit(solution)/shard_map/ppermute | solution.py:198
  16.5 7.7 %collective-permute-start.10 = (bf16[2,64,256]{2,1,0:T(8,128)(2,1)S(1)}, bf16[2,64,256]{2,1,0:T(8,128)(2,1)S(1)}, u32[]{:S(2)}, u32[]{:S(2)}) collective-permute-start(bf16[2,64,256]{2,1,0:T(8,128)(2,1)S(1)} %pad_maximum_fusion.3), channel_id=1, source_target_pairs={{0,2},{1,3},{2,0},{3,1},{4,6},{5,7},{6,4},{7,5},{8,10},{9,11},{10,... | collective-permute-start | bytes 196616 | tf_op jit(solution)/shard_map/ppermute | solution.py:198
  21.1 4.4 %collective-permute-start.9 = (bf16[64,256]{1,0:T(8,128)(2,1)S(1)}, bf16[64,256]{1,0:T(8,128)(2,1)S(1)}, u32[]{:S(2)}, u32[]{:S(2)}) collective-permute-start(bf16[64,256]{1,0:T(8,128)(2,1)S(1)} %get-tuple-element.58), channel_id=1, source_target_pairs={{0,28},{4,24},{8,20},{12,16},{16,12},{20,8},{24,4},{28,0},{1,29},{... | collective-permute-start | bytes 98312 | tf_op jit(solution)/shard_map/ppermute | solution.py:198
  21.2 4.9 %collective-permute-start.11 = (bf16[64,256]{1,0:T(8,128)(2,1)S(1)}, bf16[64,256]{1,0:T(8,128)(2,1)S(1)}, u32[]{:S(2)}, u32[]{:S(2)}) collective-permute-start(bf16[64,256]{1,0:T(8,128)(2,1)S(1)} %get-tuple-element.62), channel_id=1, source_target_pairs={{0,20},{4,16},{8,28},{12,24},{16,4},{20,0},{24,12},{28,8},{1,21},{... | collective-permute-start | bytes 98312 | tf_op jit(solution)/shard_map/ppermute | solution.py:198
  23.4 3.6 %collective-permute-start.12 = (bf16[64,256]{1,0:T(8,128)(2,1)S(1)}, bf16[64,256]{1,0:T(8,128)(2,1)S(1)}, u32[]{:S(2)}, u32[]{:S(2)}) collective-permute-start(bf16[64,256]{1,0:T(8,128)(2,1)S(1)} %get-tuple-element.63), channel_id=1, source_target_pairs={{0,12},{4,8},{8,4},{12,0},{16,28},{20,24},{24,20},{28,16},{1,13},{... | collective-permute-start | bytes 98312 | tf_op jit(solution)/shard_map/ppermute | solution.py:198
  25.6 1.7 %collective-permute-start.14 = (bf16[2,64,256]{2,1,0:T(8,128)(2,1)S(1)}, bf16[2,64,256]{2,1,0:T(8,128)(2,1)S(1)}, u32[]{:S(2)}, u32[]{:S(2)}) collective-permute-start(bf16[2,64,256]{2,1,0:T(8,128)(2,1)S(1)} %pad_maximum_fusion.5.vectors), channel_id=1, source_target_pairs={{0,4},{4,0},{8,12},{12,8},{16,20},{20,16},{24,28},{28,24},{1,5},{5... | collective-permute-start | bytes 196616 | tf_op jit(solution)/shard_map/ppermute | solution.py:198
  27.0 1.3 %collective-permute-start.13 = (bf16[2,64,256]{2,1,0:T(8,128)(2,1)S(1)}, bf16[2,64,256]{2,1,0:T(8,128)(2,1)S(1)}, u32[]{:S(2)}, u32[]{:S(2)}) collective-permute-start(bf16[2,64,256]{2,1,0:T(8,128)(2,1)S(1)} %pad_maximum_fusion.4), channel_id=1, source_target_pairs={{0,4},{4,0},{8,12},{12,8},{16,20},{20,16},{24,28},{28,24},{1,5},{5... | collective-permute-start | bytes 196616 | tf_op jit(solution)/shard_map/ppermute | solution.py:198
  27.3 11.0 %copy-start.3 = (f32[64,256]{1,0:T(8,128)S(1)}, f32[64,256]{1,0:T(8,128)}, u32[]{:S(2)}) copy-start(f32[64,256]{1,0:T(8,128)} %value.1.refs_4_) | copy-start | bytes 196612
  27.3 11.0 %copy-start.4 = (f32[64,256]{1,0:T(8,128)S(1)}, f32[64,256]{1,0:T(8,128)}, u32[]{:S(2)}) copy-start(f32[64,256]{1,0:T(8,128)} %refs_5_.3) | copy-start | bytes 196612
  27.3 11.0 %copy-start.5 = (f32[2]{0:T(128)S(1)}, f32[2]{0:T(128)}, u32[]{:S(2)}) copy-start(f32[2]{0:T(128)} %coeffs.1) | copy-start | bytes 28
  28.9 5.9 %collective-permute-start.15 = (bf16[144,128]{1,0:T(8,128)(2,1)S(1)}, bf16[144,128]{1,0:T(8,128)(2,1)S(1)}, u32[]{:S(2)}, u32[]{:S(2)}) collective-permute-start(bf16[144,128]{1,0:T(8,128)(2,1)S(1)} %get-tuple-element.69), channel_id=1, source_target_pairs={{0,3},{1,2},{2,1},{3,0},{4,7},{5,6},{6,5},{7,4},{8,11},{9,10},{10,... | collective-permute-start | bytes 110600 | tf_op jit(solution)/shard_map/ppermute | solution.py:198
  30.3 5.0 %collective-permute-start.16 = (bf16[144,128]{1,0:T(8,128)(2,1)S(1)}, bf16[144,128]{1,0:T(8,128)(2,1)S(1)}, u32[]{:S(2)}, u32[]{:S(2)}) collective-permute-start(bf16[144,128]{1,0:T(8,128)(2,1)S(1)} %get-tuple-element.70), channel_id=1, source_target_pairs={{0,1},{1,0},{2,3},{3,2},{4,5},{5,4},{6,7},{7,6},{8,9},{9,8},{10,11... | collective-permute-start | bytes 110600 | tf_op jit(solution)/shard_map/ppermute | solution.py:198
  30.4 5.3 %collective-permute-start.17 = (bf16[144,128]{1,0:T(8,128)(2,1)S(1)}, bf16[144,128]{1,0:T(8,128)(2,1)S(1)}, u32[]{:S(2)}, u32[]{:S(2)}) collective-permute-start(bf16[144,128]{1,0:T(8,128)(2,1)S(1)} %get-tuple-element.71), channel_id=1, source_target_pairs={{0,2},{1,3},{2,0},{3,1},{4,6},{5,7},{6,4},{7,5},{8,10},{9,11},{10,... | collective-permute-start | bytes 110600 | tf_op jit(solution)/shard_map/ppermute | solution.py:198
  35.7 4.0 %collective-permute-start.18 = (f32[8,128]{1,0:T(8,128)S(1)}, f32[8,128]{1,0:T(8,128)S(1)}, u32[]{:S(2)}, u32[]{:S(2)}) collective-permute-start(f32[8,128]{1,0:T(8,128)S(1)} %get-tuple-element.72), channel_id=1, source_target_pairs={{0,28},{4,24},{8,20},{12,16},{16,12},{20,8},{24,4},{28,0},{1,29},{... | collective-permute-start | bytes 12296 | tf_op jit(solution)/shard_map/ppermute | solution.py:198
  35.8 3.9 %collective-permute-start.19 = (f32[8,128]{1,0:T(8,128)S(1)}, f32[8,128]{1,0:T(8,128)S(1)}, u32[]{:S(2)}, u32[]{:S(2)}) collective-permute-start(f32[8,128]{1,0:T(8,128)S(1)} %get-tuple-element.73), channel_id=1, source_target_pairs={{0,20},{4,16},{8,28},{12,24},{16,4},{20,0},{24,12},{28,8},{1,21},{... | collective-permute-start | bytes 12296 | tf_op jit(solution)/shard_map/ppermute | solution.py:198
  37.6 3.0 %collective-permute-start.20 = (f32[8,128]{1,0:T(8,128)S(1)}, f32[8,128]{1,0:T(8,128)S(1)}, u32[]{:S(2)}, u32[]{:S(2)}) collective-permute-start(f32[8,128]{1,0:T(8,128)S(1)} %get-tuple-element.74), channel_id=1, source_target_pairs={{0,12},{4,8},{8,4},{12,0},{16,28},{20,24},{24,20},{28,16},{1,13},{... | collective-permute-start | bytes 12296 | tf_op jit(solution)/shard_map/ppermute | solution.py:198
  40.6 1.2 %collective-permute-start.21 = (f32[8,128]{1,0:T(8,128)S(1)}, f32[8,128]{1,0:T(8,128)S(1)}, u32[]{:S(2)}, u32[]{:S(2)}) collective-permute-start(f32[8,128]{1,0:T(8,128)S(1)} %add_add_fusion), channel_id=1, source_target_pairs={{0,4},{4,0},{8,12},{12,8},{16,20},{20,16},{24,28},{28,24},{1,5},{5... | collective-permute-start | bytes 12296 | tf_op jit(solution)/shard_map/ppermute | solution.py:198

commit v7 on v4

--- a/solution.py
+++ b/solution.py
@@ -152,18 +152,19 @@
 
 
 def next_kernel(n_col, own, *refs):
-    received, (prev, cur, probes, tile, *outs) = refs[: n_col - 1], refs[n_col - 1 :]
+    received, (prev, *outs) = refs[: n_col - 1], refs[n_col - 1 :]
     value = 2.0 * gathered(own, received) - prev[...]
     for out in outs:
         out[...] = value.astype(BF16)
+
+
+def value_kernel(n_col, own, *refs):
+    received, (prev, cur, probes, out, tile) = refs[: n_col - 1], refs[n_col - 1 :]
+    value = 2.0 * gathered(own, received) - prev[...]
+    out[...] = value
     ahead = as_row(jnp.sum(probes[...] * value, axis=1, keepdims=True))
     back = as_row(jnp.sum(probes[...] * cur[...], axis=1, keepdims=True))
     tile[...] = jnp.concatenate([ahead, -back, jnp.zeros((6, LANES), F32)], axis=0)
-
-
-def value_kernel(n_col, own, *refs):
-    received, (prev, out) = refs[: n_col - 1], refs[n_col - 1 :]
-    out[...] = 2.0 * gathered(own, received) - prev[...]
 
 
 def tile_kernel(start, n_received, mine, *refs):
@@ -298,15 +299,18 @@
     sends, kept = barrier((sends, kept))
     handed = swap(jnp.stack(kept), "col", k)
     received = exchange(sends, first_order)
-    tile, *rounded = call(
+    rounded = call(
         functools.partial(next_kernel, n_col),
-        [shape(8, LANES)] + [shape(count, width, dtype=BF16)] * n_out,
+        [shape(count, width, dtype=BF16)] * n_out,
+        [VMEM] * (n_col + 1),
+        "next",
+    )(own, *received, t_prev)
+    t_next, tile = call(
+        functools.partial(value_kernel, n_col),
+        [shape(count, width), shape(8, LANES)],
         [VMEM] * (n_col + 3),
-        "next",
+        "value",
     )(own, *received, t_prev, t_cur, probes)
-    t_next = call(
-        functools.partial(value_kernel, n_col), shape(count, width), [VMEM] * (n_col + 1), "value"
-    )(own, *received, t_prev)
 
     got = gather(orders[1], *rounded)
     got[1], t_next, handed = barrier((got[1], t_next, handed))

time: 42.6 us -> 42.5 us (level)
  starting transfers between devices: 21.8 us -> 21.3 us
  waiting for transfers between devices: 10.6 us -> 11.1 us
    ppermute x22, starting transfers between devices: 21.8 us -> 21.3 us  [swap(): return lax.ppermute(x, axis, [(i, i ^ k) for i in range(n)])]
    ppermute x22, waiting for transfers between devices: 10.6 us -> 11.1 us  [swap(): return lax.ppermute(x, axis, [(i, i ^ k) for i in range(n)])]
  transfers between devices with their start and end apart: 22 -> 22, of which waited for: 8 -> 9; matrix products, arithmetic and copies ran while one was open for 0% -> 0% of each run, Pallas kernels for 15% -> 15%
where the time goes in v7:
time: 42.5 us; the launch traced here: 42.3 us
  starting transfers between devices  21.3 us (50%)
  waiting for transfers between devices  11.1 us (26%)
  Pallas kernels  7.79 us (18%)
  between operations  1.49 us (4%)
  other arithmetic  0.65 us (2%)
    ppermute x22, starting transfers between devices, swap(): return lax.ppermute(x, axis, [(i, i ^ k) for i in range(n)])  21.3 us
    ppermute x22, waiting for transfers between devices, swap(): return lax.ppermute(x, axis, [(i, i ^ k) for i in range(n)])  11.1 us
    pallas_call x1, Pallas kernels, local(): call(functools.partial(place_kernel, pb, group), shape(n_row * pb, n_col...  1.6 us
    pallas_call x2, Pallas kernels, multiply(): call(functools.partial(more_kernel, pb, both[n_first:len(order) + n_early...  1.35 us
    pallas_call x1, Pallas kernels, local(): call(functools.partial(last_kernel, n_col), [shape(count, width), shape(c...  1.22 us
    pallas_call x2, Pallas kernels, multiply(): call(functools.partial(start_kernel, pb, both[:n_first]), sums, [VMEM] *...  1.18 us
    pallas_call x1, Pallas kernels, local(): call(cast_kernel, [shape(count, width, dtype=BF16)] * (1 + n_out), [HBM]...  0.9 us
  transfers between devices with their start and end apart: 22, of which 9 were waited for; matrix products, arithmetic and copies ran while one was open for 0% of the time, Pallas kernels for 15%

profile of v7, /device:TPU:0, one launch (start us, length us, event | category | flops | bytes accessed | tf_op | source)
XLA Modules:
  0.0 42.3 jit_solution(7823101781879269281)
XLA Ops:
  0.6 0.9 %cast.1 = (bf16[64,256]{1,0:T(8,128)(2,1)S(1)}, bf16[64,256]{1,0:T(8,128)(2,1)S(1)}, bf16[64,256]{1,0:T(8,128)(2,1)S(1)}, bf16[64,256]{1,0:T(8,128)(2,1)S(1)}, bf16[64,256]{1,0:T(8,128)(2,1)S(1)}) custom-call(f32[64,256]{1,0:T(8,128)} %refs_3_.5, f32[64,256]{1,0:T(8,128)} %a_5_.1), custom_call_target="tpu_custom_call" | custom-call | tf_op jit(solution)/shard_map/cast/pallas_call | solution.py:274
  1.5 3.4 %collective-permute-start.2 = (bf16[64,256]{1,0:T(8,128)(2,1)S(1)}, bf16[64,256]{1,0:T(8,128)(2,1)S(1)}, u32[]{:S(2)}, u32[]{:S(2)}) collective-permute-start(bf16[64,256]{1,0:T(8,128)(2,1)S(1)} %get-tuple-element.49), channel_id=1, source_target_pairs={{0,28},{4,24},{8,20},{12,16},{16,12},{20,8},{24,4},{28,0},{1,29},{... | collective-permute-start | bytes 98312 | tf_op jit(solution)/shard_map/ppermute | solution.py:199
  4.9 0.8 %collective-permute-start.3 = (bf16[64,256]{1,0:T(8,128)(2,1)S(1)}, bf16[64,256]{1,0:T(8,128)(2,1)S(1)}, u32[]{:S(2)}, u32[]{:S(2)}) collective-permute-start(bf16[64,256]{1,0:T(8,128)(2,1)S(1)} %get-tuple-element.50), channel_id=1, source_target_pairs={{0,20},{4,16},{8,28},{12,24},{16,4},{20,0},{24,12},{28,8},{1,21},{... | collective-permute-start | bytes 98312 | tf_op jit(solution)/shard_map/ppermute | solution.py:199
  5.7 0.1 collective-permute-start
  5.9 1.6 %collective-permute-start.5 = (bf16[64,256]{1,0:T(8,128)(2,1)S(1)}, bf16[64,256]{1,0:T(8,128)(2,1)S(1)}, u32[]{:S(2)}, u32[]{:S(2)}) collective-permute-start(bf16[64,256]{1,0:T(8,128)(2,1)S(1)} %get-tuple-element.61), channel_id=1, source_target_pairs={{0,1},{1,0},{2,3},{3,2},{4,5},{5,4},{6,7},{7,6},{8,9},{9,8},{10,11... | collective-permute-start | bytes 98312 | tf_op jit(solution)/shard_map/ppermute | solution.py:199
  8.1 1.6 %place.1.dense.a_1_ = bf16[16,1024,128]{2,1,0:T(8,128)(2,1)S(1)} custom-call(s32[1,1]{1,0:T(1,128)S(6)} %copy.13.count, s32[1,1,64]{2,1,0:T(1,128)} %rows_in.1, s32[1,1,64]{2,1,0:T(1,128)} %cols_in.1, bf16[1,1,64,128,128]{4,3,2,1,0:T(8,128)(2,1)} %blocks.1), custom_call_target="tpu_custom_call" | custom-call | tf_op jit(solution)/shard_map/place/pallas_call | solution.py:220
  9.7 0.0 collective-permute-done.2
  9.7 0.0 collective-permute-done.3
  9.7 0.4 collective-permute-start.4
  10.1 0.0 collective-permute-done
  10.1 0.2 collective-permute-start.1
  10.3 0.7 %first_start.1.before = f32[4,64,256]{2,1,0:T(8,128)S(1)} custom-call(bf16[4,64,256]{2,1,0:T(8,128)(2,1)S(1)} %pad_maximum_fusion.vectors, bf16[16,1024,128]{2,1,0:T(8,128)(2,1)S(1)} %place.1.dense.a_1_), custom_call_target="tpu_custom_call" | custom-call | tf_op jit(solution)/shard_map/first_start/pallas_call | solution.py:249
  11.1 0.0 copy-start.2
  11.1 0.0 copy-start
  11.1 0.0 copy-start.1
  11.1 0.0 collective-permute-done.4.vectors
  11.1 0.6 %first_more.1.before = f32[4,64,256]{2,1,0:T(8,128)S(1)} custom-call(bf16[3,64,256]{2,1,0:T(8,128)(2,1)S(1)} %collective-permute-done.4.vectors, bf16[16,1024,128]{2,1,0:T(8,128)(2,1)S(1)} %place.1.dense.a_1_, f32[4,64,256]{2,1,0:T(8,128)S(1)} %first_start.1.before), custom_call_target="tpu_custom_call" | custom-call | tf_op jit(solution)/shard_map/first_more/pallas_call | solution.py:252
  11.7 0.0 collective-permute-done.1.vectors
  11.7 0.3 first_end.1
  12.0 0.0 collective-permute-done.5.a_6_
  12.0 2.8 %collective-permute-start.6 = (bf16[128,128]{1,0:T(8,128)(2,1)S(1)}, bf16[128,128]{1,0:T(8,128)(2,1)S(1)}, u32[]{:S(2)}, u32[]{:S(2)}) collective-permute-start(bf16[128,128]{1,0:T(8,128)(2,1)S(1)} %get-tuple-element.56), channel_id=1, source_target_pairs={{0,3},{1,2},{2,1},{3,0},{4,7},{5,6},{6,5},{7,4},{8,11},{9,10},{10,... | collective-permute-start | bytes 98312 | tf_op jit(solution)/shard_map/ppermute | solution.py:199
  14.9 0.0 collective-permute-start.7
  14.9 1.6 %collective-permute-start.8 = (bf16[128,128]{1,0:T(8,128)(2,1)S(1)}, bf16[128,128]{1,0:T(8,128)(2,1)S(1)}, u32[]{:S(2)}, u32[]{:S(2)}) collective-permute-start(bf16[128,128]{1,0:T(8,128)(2,1)S(1)} %get-tuple-element.58), channel_id=1, source_target_pairs={{0,1},{1,0},{2,3},{3,2},{4,5},{5,4},{6,7},{7,6},{8,9},{9,8},{10,11... | collective-permute-start | bytes 98312 | tf_op jit(solution)/shard_map/ppermute | solution.py:199
  16.5 1.7 %collective-permute-start.10 = (bf16[2,64,256]{2,1,0:T(8,128)(2,1)S(1)}, bf16[2,64,256]{2,1,0:T(8,128)(2,1)S(1)}, u32[]{:S(2)}, u32[]{:S(2)}) collective-permute-start(bf16[2,64,256]{2,1,0:T(8,128)(2,1)S(1)} %pad_maximum_fusion.3), channel_id=1, source_target_pairs={{0,2},{1,3},{2,0},{3,1},{4,6},{5,7},{6,4},{7,5},{8,10},{9,11},{10,... | collective-permute-start | bytes 196616 | tf_op jit(solution)/shard_map/ppermute | solution.py:199
  18.2 0.0 collective-permute-done.6.refs_0_
  18.3 2.6 %collective-permute-done.7.refs_1_ = bf16[128,128]{1,0:T(8,128)(2,1)S(1)} collective-permute-done((bf16[128,128]{1,0:T(8,128)(2,1)S(1)}, bf16[128,128]{1,0:T(8,128)(2,1)S(1)}, u32[]{:S(2)}, u32[]{:S(2)}) %collective-permute-start.7) | collective-permute-done | bytes 32800 | tf_op jit(solution)/shard_map/ppermute | solution.py:199
  20.9 0.0 collective-permute-done.8.refs_2_
  20.9 0.0 copy-done.2
  20.9 0.1 collective-permute-start.9
  21.0 2.3 %collective-permute-start.11 = (bf16[64,256]{1,0:T(8,128)(2,1)S(1)}, bf16[64,256]{1,0:T(8,128)(2,1)S(1)}, u32[]{:S(2)}, u32[]{:S(2)}) collective-permute-start(bf16[64,256]{1,0:T(8,128)(2,1)S(1)} %get-tuple-element.64), channel_id=1, source_target_pairs={{0,20},{4,16},{8,28},{12,24},{16,4},{20,0},{24,12},{28,8},{1,21},{... | collective-permute-start | bytes 98312 | tf_op jit(solution)/shard_map/ppermute | solution.py:199
  23.3 0.0 collective-permute-start.12
  23.3 0.0 copy-done
  23.3 0.0 copy-done.1
  23.3 0.7 %value.1 = (f32[64,256]{1,0:T(8,128)}, f32[8,128]{1,0:T(8,128)S(1)}) custom-call(f32[64,256]{1,0:T(8,128)S(1)} %get-tuple-element.51.own, bf16[128,128]{1,0:T(8,128)(2,1)S(1)} %collective-permute-done.6.refs_0_, bf16[128,128]{1,0:T(8,128)(2,1)S(1)} %collective-permute-done.7.refs_1_, bf16[128,128]{1,0:T(8,128)(2,1)S(1)} %collective-permute-done.8.refs_2_, ...), custom_call_target="tpu_custom_call" | custom-call | tf_op jit(solution)/shard_map/value/pallas_call | solution.py:308
  24.0 0.0 collective-permute-done.10.a_4_
  24.0 1.3 %collective-permute-done.9 = bf16[64,256]{1,0:T(8,128)(2,1)S(1)} collective-permute-done((bf16[64,256]{1,0:T(8,128)(2,1)S(1)}, bf16[64,256]{1,0:T(8,128)(2,1)S(1)}, u32[]{:S(2)}, u32[]{:S(2)}) %collective-permute-start.9) | collective-permute-done | bytes 32800 | tf_op jit(solution)/shard_map/ppermute | solution.py:199
  25.3 0.1 collective-permute-start.14
  25.4 0.4 %second_start.1.before = f32[4,64,256]{2,1,0:T(8,128)S(1)} custom-call(bf16[2,64,256]{2,1,0:T(8,128)(2,1)S(1)} %pad_maximum_fusion.5.vectors, bf16[16,1024,128]{2,1,0:T(8,128)(2,1)S(1)} %place.1.dense.a_1_), custom_call_target="tpu_custom_call" | custom-call | tf_op jit(solution)/shard_map/second_start/pallas_call | solution.py:249
  25.8 0.0 collective-permute-done.11
  25.8 0.9 %collective-permute-done.12 = bf16[64,256]{1,0:T(8,128)(2,1)S(1)} collective-permute-done((bf16[64,256]{1,0:T(8,128)(2,1)S(1)}, bf16[64,256]{1,0:T(8,128)(2,1)S(1)}, u32[]{:S(2)}, u32[]{:S(2)}) %collective-permute-start.12) | collective-permute-done | bytes 32800 | tf_op jit(solution)/shard_map/ppermute | solution.py:199
  26.7 0.1 collective-permute-start.13
  26.8 0.0 collective-permute-done.14
  26.8 0.0 copy-start.3
  26.8 0.0 copy-start.4
  26.8 0.0 copy-start.5
  26.8 0.7 %second_more.1.a_2_ = f32[4,64,256]{2,1,0:T(8,128)S(1)} custom-call(bf16[4,64,256]{2,1,0:T(8,128)(2,1)S(1)} %pad_maximum_fusion.1.vectors, bf16[16,1024,128]{2,1,0:T(8,128)(2,1)S(1)} %place.1.dense.a_1_, f32[4,64,256]{2,1,0:T(8,128)S(1)} %second_start.1.before), custom_call_target="tpu_custom_call" | custom-call | tf_op jit(solution)/shard_map/second_more/pallas_call | solution.py:252
  27.6 0.4 collective-permute-done.13.a_0_
  28.0 0.5 %second_end.1 = (f32[64,256]{1,0:T(8,128)S(1)}, bf16[144,128]{1,0:T(8,128)(2,1)S(1)}, bf16[144,128]{1,0:T(8,128)(2,1)S(1)}, bf16[144,128]{1,0:T(8,128)(2,1)S(1)}, f32[8,128]{1,0:T(8,128)S(1)}) custom-call(bf16[2,64,256]{2,1,0:T(8,128)(2,1)S(1)} %collective-permute-done.13.a_0_, bf16[16,1024,128]{2,1,0:T(8,128)(2,1)S(1)} %place.1.dense.a_1_, ...), custom_call_target="tpu_custom_call" | custom-call | tf_op jit(solution)/shard_map/second_end/pallas_call | solution.py:260
  28.6 1.1 %collective-permute-start.15 = (bf16[144,128]{1,0:T(8,128)(2,1)S(1)}, bf16[144,128]{1,0:T(8,128)(2,1)S(1)}, u32[]{:S(2)}, u32[]{:S(2)}) collective-permute-start(bf16[144,128]{1,0:T(8,128)(2,1)S(1)} %get-tuple-element.71), channel_id=1, source_target_pairs={{0,2},{1,3},{2,0},{3,1},{4,6},{5,7},{6,4},{7,5},{8,10},{9,11},{10,... | collective-permute-start | bytes 110600 | tf_op jit(solution)/shard_map/ppermute | solution.py:199
  29.7 1.3 %collective-permute-start.16 = (bf16[144,128]{1,0:T(8,128)(2,1)S(1)}, bf16[144,128]{1,0:T(8,128)(2,1)S(1)}, u32[]{:S(2)}, u32[]{:S(2)}) collective-permute-start(bf16[144,128]{1,0:T(8,128)(2,1)S(1)} %get-tuple-element.72), channel_id=1, source_target_pairs={{0,3},{1,2},{2,1},{3,0},{4,7},{5,6},{6,5},{7,4},{8,11},{9,10},{10,... | collective-permute-start | bytes 110600 | tf_op jit(solution)/shard_map/ppermute | solution.py:199
  31.0 1.1 %collective-permute-start.17 = (bf16[144,128]{1,0:T(8,128)(2,1)S(1)}, bf16[144,128]{1,0:T(8,128)(2,1)S(1)}, u32[]{:S(2)}, u32[]{:S(2)}) collective-permute-start(bf16[144,128]{1,0:T(8,128)(2,1)S(1)} %get-tuple-element.73), channel_id=1, source_target_pairs={{0,1},{1,0},{2,3},{3,2},{4,5},{5,4},{6,7},{7,6},{8,9},{9,8},{10,11... | collective-permute-start | bytes 110600 | tf_op jit(solution)/shard_map/ppermute | solution.py:199
  32.1 1.7 %collective-permute-done.15.refs_0_ = bf16[144,128]{1,0:T(8,128)(2,1)S(1)} collective-permute-done((bf16[144,128]{1,0:T(8,128)(2,1)S(1)}, bf16[144,128]{1,0:T(8,128)(2,1)S(1)}, u32[]{:S(2)}, u32[]{:S(2)}) %collective-permute-start.15) | collective-permute-done | bytes 36896 | tf_op jit(solution)/shard_map/ppermute | solution.py:199
  33.8 1.6 %collective-permute-done.16.refs_1_ = bf16[144,128]{1,0:T(8,128)(2,1)S(1)} collective-permute-done((bf16[144,128]{1,0:T(8,128)(2,1)S(1)}, bf16[144,128]{1,0:T(8,128)(2,1)S(1)}, u32[]{:S(2)}, u32[]{:S(2)}) %collective-permute-start.16) | collective-permute-done | bytes 36896 | tf_op jit(solution)/shard_map/ppermute | solution.py:199
  35.4 0.0 collective-permute-done.17.refs_2_
  35.5 0.1 collective-permute-start.18
  35.6 2.0 %collective-permute-start.19 = (f32[8,128]{1,0:T(8,128)S(1)}, f32[8,128]{1,0:T(8,128)S(1)}, u32[]{:S(2)}, u32[]{:S(2)}) collective-permute-start(f32[8,128]{1,0:T(8,128)S(1)} %get-tuple-element.75), channel_id=1, source_target_pairs={{0,20},{4,16},{8,28},{12,24},{16,4},{20,0},{24,12},{28,8},{1,21},{... | collective-permute-start | bytes 12296 | tf_op jit(solution)/shard_map/ppermute | solution.py:199
  37.6 0.5 %collective-permute-start.20 = (f32[8,128]{1,0:T(8,128)S(1)}, f32[8,128]{1,0:T(8,128)S(1)}, u32[]{:S(2)}, u32[]{:S(2)}) collective-permute-start(f32[8,128]{1,0:T(8,128)S(1)} %get-tuple-element.76), channel_id=1, source_target_pairs={{0,12},{4,8},{8,4},{12,0},{16,28},{20,24},{24,20},{28,16},{1,13},{... | collective-permute-start | bytes 12296 | tf_op jit(solution)/shard_map/ppermute | solution.py:199
  38.0 1.2 %last.1 = (f32[64,256]{1,0:T(8,128)}, f32[64,256]{1,0:T(8,128)}) custom-call(f32[2]{0:T(128)S(1)} %copy-done.5, f32[64,256]{1,0:T(8,128)S(1)} %get-tuple-element.77.own, bf16[144,128]{1,0:T(8,128)(2,1)S(1)} %collective-permute-done.15.refs_0_, bf16[144,128]{1,0:T(8,128)(2,1)S(1)} %collective-permute-done.16.refs_1_, ...), custom_call_target="tpu_custom_call" | custom-call | tf_op jit(solution)/shard_map/last/pallas_call | solution.py:333
  39.2 0.2 collective-permute-done.18
  39.5 0.0 collective-permute-done.19
  39.5 1.1 %collective-permute-done.20 = f32[8,128]{1,0:T(8,128)S(1)} collective-permute-done((f32[8,128]{1,0:T(8,128)S(1)}, f32[8,128]{1,0:T(8,128)S(1)}, u32[]{:S(2)}, u32[]{:S(2)}) %collective-permute-start.20) | collective-permute-done | bytes 4128 | tf_op jit(solution)/shard_map/ppermute | solution.py:199
  40.6 0.0 collective-permute-start.21
  40.6 1.2 %collective-permute-done.21 = f32[8,128]{1,0:T(8,128)S(1)} collective-permute-done((f32[8,128]{1,0:T(8,128)S(1)}, f32[8,128]{1,0:T(8,128)S(1)}, u32[]{:S(2)}, u32[]{:S(2)}) %collective-permute-start.21) | collective-permute-done | bytes 4128 | tf_op jit(solution)/shard_map/ppermute | solution.py:199
  41.8 0.6 %slice_multiply_fusion = f32[2,64]{1,0:T(2,128)} fusion(f32[8,128]{1,0:T(8,128)S(1)} %add.15), kind=kLoop, calls=%fused_computation.7 | loop fusion | flops 128 | bytes 1024 | tf_op jit(solution)/shard_map/mul | solution.py:345
  (13 shorter events, 0.1 us)
Async XLA Ops:
  1.5 8.2 %collective-permute-start.2 = (bf16[64,256]{1,0:T(8,128)(2,1)S(1)}, bf16[64,256]{1,0:T(8,128)(2,1)S(1)}, u32[]{:S(2)}, u32[]{:S(2)}) collective-permute-start(bf16[64,256]{1,0:T(8,128)(2,1)S(1)} %get-tuple-element.49), channel_id=1, source_target_pairs={{0,28},{4,24},{8,20},{12,16},{16,12},{20,8},{24,4},{28,0},{1,29},{... | collective-permute-start | bytes 98312 | tf_op jit(solution)/shard_map/ppermute | solution.py:199
  4.9 4.8 %collective-permute-start.3 = (bf16[64,256]{1,0:T(8,128)(2,1)S(1)}, bf16[64,256]{1,0:T(8,128)(2,1)S(1)}, u32[]{:S(2)}, u32[]{:S(2)}) collective-permute-start(bf16[64,256]{1,0:T(8,128)(2,1)S(1)} %get-tuple-element.50), channel_id=1, source_target_pairs={{0,20},{4,16},{8,28},{12,24},{16,4},{20,0},{24,12},{28,8},{1,21},{... | collective-permute-start | bytes 98312 | tf_op jit(solution)/shard_map/ppermute | solution.py:199
  5.7 4.4 %collective-permute-start = (bf16[64,256]{1,0:T(8,128)(2,1)S(1)}, bf16[64,256]{1,0:T(8,128)(2,1)S(1)}, u32[]{:S(2)}, u32[]{:S(2)}) collective-permute-start(bf16[64,256]{1,0:T(8,128)(2,1)S(1)} %get-tuple-element.45), channel_id=1, source_target_pairs={{0,12},{4,8},{8,4},{12,0},{16,28},{20,24},{24,20},{28,16},{1,13},{... | collective-permute-start | bytes 98312 | tf_op jit(solution)/shard_map/ppermute | solution.py:199
  5.9 6.2 %collective-permute-start.5 = (bf16[64,256]{1,0:T(8,128)(2,1)S(1)}, bf16[64,256]{1,0:T(8,128)(2,1)S(1)}, u32[]{:S(2)}, u32[]{:S(2)}) collective-permute-start(bf16[64,256]{1,0:T(8,128)(2,1)S(1)} %get-tuple-element.61), channel_id=1, source_target_pairs={{0,1},{1,0},{2,3},{3,2},{4,5},{5,4},{6,7},{7,6},{8,9},{9,8},{10,11... | collective-permute-start | bytes 98312 | tf_op jit(solution)/shard_map/ppermute | solution.py:199
  9.7 1.4 %collective-permute-start.4 = (bf16[3,64,256]{2,1,0:T(8,128)(2,1)S(1)}, bf16[3,64,256]{2,1,0:T(8,128)(2,1)S(1)}, u32[]{:S(2)}, u32[]{:S(2)}) collective-permute-start(bf16[3,64,256]{2,1,0:T(8,128)(2,1)S(1)} %pad_maximum_fusion.2), channel_id=1, source_target_pairs={{0,4},{4,0},{8,12},{12,8},{16,20},{20,16},{24,28},{28,24},{1,5},{5... | collective-permute-start | bytes 294920 | tf_op jit(solution)/shard_map/ppermute | solution.py:199
  10.1 1.6 %collective-permute-start.1 = (bf16[1,64,256]{2,1,0:T(8,128)(2,1)S(1)}, bf16[1,64,256]{2,1,0:T(8,128)(2,1)S(1)}, u32[]{:S(2)}, u32[]{:S(2)}) collective-permute-start(bf16[1,64,256]{2,1,0:T(8,128)(2,1)S(1)} %bitcast.24), channel_id=1, source_target_pairs={{0,4},{4,0},{8,12},{12,8},{16,20},{20,16},{24,28},{28,24},{1,5},{5... | collective-permute-start | bytes 98312 | tf_op jit(solution)/shard_map/ppermute | solution.py:199
  11.1 9.8 %copy-start.2 = (f32[64,256]{1,0:T(8,128)S(1)}, f32[64,256]{1,0:T(8,128)}, u32[]{:S(2)}) copy-start(f32[64,256]{1,0:T(8,128)} %refs_3_.4) | copy-start | bytes 196612
  11.1 12.2 %copy-start = (f32[64,256]{1,0:T(8,128)S(1)}, f32[64,256]{1,0:T(8,128)}, u32[]{:S(2)}) copy-start(f32[64,256]{1,0:T(8,128)} %a_5_.1) | copy-start | bytes 196612
  11.1 12.2 %copy-start.1 = (f32[64,256]{1,0:T(8,128)S(1)}, f32[64,256]{1,0:T(8,128)}, u32[]{:S(2)}) copy-start(f32[64,256]{1,0:T(8,128)} %refs_3_.5) | copy-start | bytes 196612
  12.0 6.2 %collective-permute-start.6 = (bf16[128,128]{1,0:T(8,128)(2,1)S(1)}, bf16[128,128]{1,0:T(8,128)(2,1)S(1)}, u32[]{:S(2)}, u32[]{:S(2)}) collective-permute-start(bf16[128,128]{1,0:T(8,128)(2,1)S(1)} %get-tuple-element.56), channel_id=1, source_target_pairs={{0,3},{1,2},{2,1},{3,0},{4,7},{5,6},{6,5},{7,4},{8,11},{9,10},{10,... | collective-permute-start | bytes 98312 | tf_op jit(solution)/shard_map/ppermute | solution.py:199
  14.9 6.0 %collective-permute-start.7 = (bf16[128,128]{1,0:T(8,128)(2,1)S(1)}, bf16[128,128]{1,0:T(8,128)(2,1)S(1)}, u32[]{:S(2)}, u32[]{:S(2)}) collective-permute-start(bf16[128,128]{1,0:T(8,128)(2,1)S(1)} %get-tuple-element.57), channel_id=1, source_target_pairs={{0,2},{1,3},{2,0},{3,1},{4,6},{5,7},{6,4},{7,5},{8,10},{9,11},{10,... | collective-permute-start | bytes 98312 | tf_op jit(solution)/shard_map/ppermute | solution.py:199
  14.9 6.0 %collective-permute-start.8 = (bf16[128,128]{1,0:T(8,128)(2,1)S(1)}, bf16[128,128]{1,0:T(8,128)(2,1)S(1)}, u32[]{:S(2)}, u32[]{:S(2)}) collective-permute-start(bf16[128,128]{1,0:T(8,128)(2,1)S(1)} %get-tuple-element.58), channel_id=1, source_target_pairs={{0,1},{1,0},{2,3},{3,2},{4,5},{5,4},{6,7},{7,6},{8,9},{9,8},{10,11... | collective-permute-start | bytes 98312 | tf_op jit(solution)/shard_map/ppermute | solution.py:199
  16.5 7.5 %collective-permute-start.10 = (bf16[2,64,256]{2,1,0:T(8,128)(2,1)S(1)}, bf16[2,64,256]{2,1,0:T(8,128)(2,1)S(1)}, u32[]{:S(2)}, u32[]{:S(2)}) collective-permute-start(bf16[2,64,256]{2,1,0:T(8,128)(2,1)S(1)} %pad_maximum_fusion.3), channel_id=1, source_target_pairs={{0,2},{1,3},{2,0},{3,1},{4,6},{5,7},{6,4},{7,5},{8,10},{9,11},{10,... | collective-permute-start | bytes 196616 | tf_op jit(solution)/shard_map/ppermute | solution.py:199
  20.9 4.4 %collective-permute-start.9 = (bf16[64,256]{1,0:T(8,128)(2,1)S(1)}, bf16[64,256]{1,0:T(8,128)(2,1)S(1)}, u32[]{:S(2)}, u32[]{:S(2)}) collective-permute-start(bf16[64,256]{1,0:T(8,128)(2,1)S(1)} %get-tuple-element.59), channel_id=1, source_target_pairs={{0,28},{4,24},{8,20},{12,16},{16,12},{20,8},{24,4},{28,0},{1,29},{... | collective-permute-start | bytes 98312 | tf_op jit(solution)/shard_map/ppermute | solution.py:199
  21.0 4.8 %collective-permute-start.11 = (bf16[64,256]{1,0:T(8,128)(2,1)S(1)}, bf16[64,256]{1,0:T(8,128)(2,1)S(1)}, u32[]{:S(2)}, u32[]{:S(2)}) collective-permute-start(bf16[64,256]{1,0:T(8,128)(2,1)S(1)} %get-tuple-element.64), channel_id=1, source_target_pairs={{0,20},{4,16},{8,28},{12,24},{16,4},{20,0},{24,12},{28,8},{1,21},{... | collective-permute-start | bytes 98312 | tf_op jit(solution)/shard_map/ppermute | solution.py:199
  23.3 3.3 %collective-permute-start.12 = (bf16[64,256]{1,0:T(8,128)(2,1)S(1)}, bf16[64,256]{1,0:T(8,128)(2,1)S(1)}, u32[]{:S(2)}, u32[]{:S(2)}) collective-permute-start(bf16[64,256]{1,0:T(8,128)(2,1)S(1)} %get-tuple-element.65), channel_id=1, source_target_pairs={{0,12},{4,8},{8,4},{12,0},{16,28},{20,24},{24,20},{28,16},{1,13},{... | collective-permute-start | bytes 98312 | tf_op jit(solution)/shard_map/ppermute | solution.py:199
  25.3 1.5 %collective-permute-start.14 = (bf16[2,64,256]{2,1,0:T(8,128)(2,1)S(1)}, bf16[2,64,256]{2,1,0:T(8,128)(2,1)S(1)}, u32[]{:S(2)}, u32[]{:S(2)}) collective-permute-start(bf16[2,64,256]{2,1,0:T(8,128)(2,1)S(1)} %pad_maximum_fusion.5.vectors), channel_id=1, source_target_pairs={{0,4},{4,0},{8,12},{12,8},{16,20},{20,16},{24,28},{28,24},{1,5},{5... | collective-permute-start | bytes 196616 | tf_op jit(solution)/shard_map/ppermute | solution.py:199
  26.7 1.3 %collective-permute-start.13 = (bf16[2,64,256]{2,1,0:T(8,128)(2,1)S(1)}, bf16[2,64,256]{2,1,0:T(8,128)(2,1)S(1)}, u32[]{:S(2)}, u32[]{:S(2)}) collective-permute-start(bf16[2,64,256]{2,1,0:T(8,128)(2,1)S(1)} %pad_maximum_fusion.4), channel_id=1, source_target_pairs={{0,4},{4,0},{8,12},{12,8},{16,20},{20,16},{24,28},{28,24},{1,5},{5... | collective-permute-start | bytes 196616 | tf_op jit(solution)/shard_map/ppermute | solution.py:199
  26.8 11.2 %copy-start.3 = (f32[64,256]{1,0:T(8,128)S(1)}, f32[64,256]{1,0:T(8,128)}, u32[]{:S(2)}) copy-start(f32[64,256]{1,0:T(8,128)} %refs_5_.3) | copy-start | bytes 196612
  26.8 11.2 %copy-start.4 = (f32[64,256]{1,0:T(8,128)S(1)}, f32[64,256]{1,0:T(8,128)}, u32[]{:S(2)}) copy-start(f32[64,256]{1,0:T(8,128)} %get-tuple-element.41.refs_4_) | copy-start | bytes 196612
  26.8 11.2 %copy-start.5 = (f32[2]{0:T(128)S(1)}, f32[2]{0:T(128)}, u32[]{:S(2)}) copy-start(f32[2]{0:T(128)} %coeffs.1) | copy-start | bytes 28
  28.6 5.3 %collective-permute-start.15 = (bf16[144,128]{1,0:T(8,128)(2,1)S(1)}, bf16[144,128]{1,0:T(8,128)(2,1)S(1)}, u32[]{:S(2)}, u32[]{:S(2)}) collective-permute-start(bf16[144,128]{1,0:T(8,128)(2,1)S(1)} %get-tuple-element.71), channel_id=1, source_target_pairs={{0,2},{1,3},{2,0},{3,1},{4,6},{5,7},{6,4},{7,5},{8,10},{9,11},{10,... | collective-permute-start | bytes 110600 | tf_op jit(solution)/shard_map/ppermute | solution.py:199
  29.7 5.8 %collective-permute-start.16 = (bf16[144,128]{1,0:T(8,128)(2,1)S(1)}, bf16[144,128]{1,0:T(8,128)(2,1)S(1)}, u32[]{:S(2)}, u32[]{:S(2)}) collective-permute-start(bf16[144,128]{1,0:T(8,128)(2,1)S(1)} %get-tuple-element.72), channel_id=1, source_target_pairs={{0,3},{1,2},{2,1},{3,0},{4,7},{5,6},{6,5},{7,4},{8,11},{9,10},{10,... | collective-permute-start | bytes 110600 | tf_op jit(solution)/shard_map/ppermute | solution.py:199
  31.0 4.4 %collective-permute-start.17 = (bf16[144,128]{1,0:T(8,128)(2,1)S(1)}, bf16[144,128]{1,0:T(8,128)(2,1)S(1)}, u32[]{:S(2)}, u32[]{:S(2)}) collective-permute-start(bf16[144,128]{1,0:T(8,128)(2,1)S(1)} %get-tuple-element.73), channel_id=1, source_target_pairs={{0,1},{1,0},{2,3},{3,2},{4,5},{5,4},{6,7},{7,6},{8,9},{9,8},{10,11... | collective-permute-start | bytes 110600 | tf_op jit(solution)/shard_map/ppermute | solution.py:199
  35.5 4.0 %collective-permute-start.18 = (f32[8,128]{1,0:T(8,128)S(1)}, f32[8,128]{1,0:T(8,128)S(1)}, u32[]{:S(2)}, u32[]{:S(2)}) collective-permute-start(f32[8,128]{1,0:T(8,128)S(1)} %get-tuple-element.74), channel_id=1, source_target_pairs={{0,28},{4,24},{8,20},{12,16},{16,12},{20,8},{24,4},{28,0},{1,29},{... | collective-permute-start | bytes 12296 | tf_op jit(solution)/shard_map/ppermute | solution.py:199
  35.6 3.9 %collective-permute-start.19 = (f32[8,128]{1,0:T(8,128)S(1)}, f32[8,128]{1,0:T(8,128)S(1)}, u32[]{:S(2)}, u32[]{:S(2)}) collective-permute-start(f32[8,128]{1,0:T(8,128)S(1)} %get-tuple-element.75), channel_id=1, source_target_pairs={{0,20},{4,16},{8,28},{12,24},{16,4},{20,0},{24,12},{28,8},{1,21},{... | collective-permute-start | bytes 12296 | tf_op jit(solution)/shard_map/ppermute | solution.py:199
  37.6 3.0 %collective-permute-start.20 = (f32[8,128]{1,0:T(8,128)S(1)}, f32[8,128]{1,0:T(8,128)S(1)}, u32[]{:S(2)}, u32[]{:S(2)}) collective-permute-start(f32[8,128]{1,0:T(8,128)S(1)} %get-tuple-element.76), channel_id=1, source_target_pairs={{0,12},{4,8},{8,4},{12,0},{16,28},{20,24},{24,20},{28,16},{1,13},{... | collective-permute-start | bytes 12296 | tf_op jit(solution)/shard_map/ppermute | solution.py:199
  40.6 1.2 %collective-permute-start.21 = (f32[8,128]{1,0:T(8,128)S(1)}, f32[8,128]{1,0:T(8,128)S(1)}, u32[]{:S(2)}, u32[]{:S(2)}) collective-permute-start(f32[8,128]{1,0:T(8,128)S(1)} %add_add_fusion), channel_id=1, source_target_pairs={{0,4},{4,0},{8,12},{12,8},{16,20},{20,16},{24,28},{28,24},{1,5},{5... | collective-permute-start | bytes 12296 | tf_op jit(solution)/shard_map/ppermute | solution.py:199
